TPU v7x, 32 devices: a whole 2x2x4 slice. The times are simulated.
32 devices in a mesh: dp: 8 (over z, y), tensor: 4 (over x, core).
Axes of the slice: x: 2, y: 2, z: 4, core: 2. Of those that a mesh axis runs over, the one named last changes fastest.
Arguments:
- inputs: bfloat16 [16384, 1024], P('dp'), may hold values from -6 to 6
- cotangent: bfloat16 [16384, 1024], P('dp', 'tensor'), may hold values from -12 to 12
- doc_lengths: int32 [8, 3], P('dp'), may hold values from 200 to 2000, as said below
- weight_qk: float32 [2, 1024, 512], P(None, 'dp', 'tensor'), may hold values from -0.1875 to 0.1875
- weight_vg: float32 [2, 1024, 1024], P(None, 'dp', 'tensor'), may hold values from -0.1875 to 0.1875
- weight_lowin: float32 [1024, 16], P('dp'), may hold values from -0.1875 to 0.1875
- weight_lowout: float32 [16, 4, 128], P(None, 'tensor', 'dp'), may hold values from -1.5 to 1.5
- weight_mixout: float32 [1024, 1024], P('tensor', 'dp'), may hold values from -0.1875 to 0.1875
- weight_gateup: float32 [2, 1024, 2816], P(None, 'dp', 'tensor'), may hold values from -0.1875 to 0.1875
- weight_down: float32 [2816, 1024], P('tensor', 'dp'), may hold values from -0.109375 to 0.109375
- weight_small: float32 [2816], replicated, may hold values from 0 to 6
- first_qk: float32 [2, 1024, 512], P(None, 'dp', 'tensor'), may hold values from -0.00048828125 to 0.00048828125
- first_vg: float32 [2, 1024, 1024], P(None, 'dp', 'tensor'), may hold values from -0.00048828125 to 0.00048828125
- first_lowin: float32 [1024, 16], P('dp'), may hold values from -0.00048828125 to 0.00048828125
- first_lowout: float32 [16, 4, 128], P(None, 'tensor', 'dp'), may hold values from -0.00048828125 to 0.00048828125
- first_mixout: float32 [1024, 1024], P('tensor', 'dp'), may hold values from -0.00048828125 to 0.00048828125
- first_gateup: float32 [2, 1024, 2816], P(None, 'dp', 'tensor'), may hold values from -0.00048828125 to 0.00048828125
- first_down: float32 [2816, 1024], P('tensor', 'dp'), may hold values from -0.00048828125 to 0.00048828125
- first_small: float32 [2816], replicated, may hold values from -0.00048828125 to 0.00048828125
- second_qk: float32 [2, 1024, 512], P(None, 'dp', 'tensor'), may hold values from 4.086247e-09 to 1.6313914e-08
- second_vg: float32 [2, 1024, 1024], P(None, 'dp', 'tensor'), may hold values from 4.086247e-09 to 1.6313914e-08
- second_lowin: float32 [1024, 16], P('dp'), may hold values from 4.086247e-09 to 1.6313914e-08
- second_lowout: float32 [16, 4, 128], P(None, 'tensor', 'dp'), may hold values from 4.086247e-09 to 1.6313914e-08
- second_mixout: float32 [1024, 1024], P('tensor', 'dp'), may hold values from 4.086247e-09 to 1.6313914e-08
- second_gateup: float32 [2, 1024, 2816], P(None, 'dp', 'tensor'), may hold values from 4.086247e-09 to 1.6313914e-08
- second_down: float32 [2816, 1024], P('tensor', 'dp'), may hold values from 4.086247e-09 to 1.6313914e-08
- second_small: float32 [2816], replicated, may hold values from 4.086247e-09 to 1.6313914e-08
Outputs:
- output: bfloat16 [16384, 1024], P('dp', 'tensor')
- input_grad: float32 [16384, 1024], P('dp', 'tensor')
- grad_norm: float32 [1], replicated
- momentum_qk: float32 [2, 1024, 512], P(None, 'dp', 'tensor')
- momentum_vg: float32 [2, 1024, 1024], P(None, 'dp', 'tensor')
- momentum_lowin: float32 [1024, 16], P('dp')
- momentum_lowout: float32 [16, 4, 128], P(None, 'tensor', 'dp')
- momentum_mixout: float32 [1024, 1024], P('tensor', 'dp')
- momentum_gateup: float32 [2, 1024, 2816], P(None, 'dp', 'tensor')
- momentum_down: float32 [2816, 1024], P('tensor', 'dp')
- momentum_small: float32 [2816], replicated
- variance_qk: float32 [2, 1024, 512], P(None, 'dp', 'tensor')
- variance_vg: float32 [2, 1024, 1024], P(None, 'dp', 'tensor')
- variance_lowin: float32 [1024, 16], P('dp')
- variance_lowout: float32 [16, 4, 128], P(None, 'tensor', 'dp')
- variance_mixout: float32 [1024, 1024], P('tensor', 'dp')
- variance_gateup: float32 [2, 1024, 2816], P(None, 'dp', 'tensor')
- variance_down: float32 [2816, 1024], P('tensor', 'dp')
- variance_small: float32 [2816], replicated
- updated_qk: float32 [2, 1024, 512], P(None, 'dp', 'tensor')
- updated_vg: float32 [2, 1024, 1024], P(None, 'dp', 'tensor')
- updated_lowin: float32 [1024, 16], P('dp')
- updated_lowout: float32 [16, 4, 128], P(None, 'tensor', 'dp')
- updated_mixout: float32 [1024, 1024], P('tensor', 'dp')
- updated_gateup: float32 [2, 1024, 2816], P(None, 'dp', 'tensor')
- updated_down: float32 [2816, 1024], P('tensor', 'dp')
- updated_small: float32 [2816], replicated
Inputs may be any that keep to these rules, and one draw needn't show every extreme that they name: `doc_lengths`: documents of a sequence are packed in order from its first token; tokens after them are padding, and a document that runs past 2048 tokens is cut there. Some sequence holds a document of 2000 tokens and one of 200.
All inputs are finite; a program needn't handle non-finite values.
Results may differ from a plain program's by a relative error of at most 0.029.
Values may be sent and summed in bfloat16 or wider, within the bound.
No kernel may reach another device: no remote copies, remote signals or barrier semaphores. Data moves between devices by JAX's collectives and lax.ppermute only.
A program may use at most 192 MiB of HBM per device.

v0:
```python
import functools

import jax
import jax.numpy as jnp
from jax import lax
from jax.experimental import pallas as pl
from jax.experimental.pallas import tpu as pltpu
from jax.sharding import PartitionSpec as P

D = 1024
HEADS = 4
DK = 128
DV = 256
RANK = 16
FF = 2816
SPAN = 64
SEQ_LEN = 2048
STEP = 10

NORM_EPS = 1e-06
GATE_NORM = 16.0
BETA_FIRST = 0.9
BETA_SECOND = 0.95
ADAM_EPS = 1e-08
WEIGHT_DECAY = 0.1
CLIP_NORM = 1.0
GAIN_RATE = 2.5
BIAS_RATE = 4.0

F32 = jnp.float32
BF16 = jnp.bfloat16
LANES = 128
SLAB = 256
SLABS = 4
CHUNK = 2 * SPAN
BLOCK = 256
PIECES = 2
ORDER = (0, 2, 1, 3)
MAIN = 768
ATTN = 896
FEED_COLS = 3 * 768
OUT_SCALE = DK**-0.5
VMEM_LIMIT = 60 * 1024 * 1024


def nn(a, b):
    return lax.dot_general(a, b, (((1,), (0,)), ((), ())), preferred_element_type=F32)


def nt(a, b):
    return lax.dot_general(a, b, (((1,), (1,)), ((), ())), preferred_element_type=F32)


def tn(a, b):
    return lax.dot_general(a, b, (((0,), (0,)), ((), ())), preferred_element_type=F32)


def doc_at(position, ends):
    number = jnp.zeros_like(position)
    for end in ends:
        number = number + jnp.where(position >= end, 1, 0)
    return number


def log_sigmoid(values):
    return jnp.minimum(values, 0.0) - jnp.log1p(jnp.exp(-jnp.abs(values)))


def prefix_sums(values, triangle):
    high = values.astype(BF16)
    low = (values - high.astype(F32)).astype(BF16)
    width = values.shape[1]
    both = nn(triangle, jnp.concatenate([high, low], axis=1))
    return both[:, :width] + both[:, width:]


def chunk_terms(queries, keys, forget, base, ends):
    row = lax.broadcasted_iota(jnp.int32, (CHUNK, CHUNK), 0)
    col = lax.broadcasted_iota(jnp.int32, (CHUNK, CHUNK), 1)
    decay = prefix_sums(forget, jnp.where(col <= row, 1.0, 0.0).astype(BF16))
    seg_row = doc_at(row + base, ends)
    same = seg_row == doc_at(col + base, ends)
    upper = row >= SPAN
    near = same & (col <= row) & (upper == (col >= SPAN))
    far = same & upper & (col < SPAN)
    before = jnp.where(base > 0, doc_at(base - 1, ends), -1)
    final = doc_at(base + CHUNK - 1, ends)
    alive = jnp.where(seg_row == before, 1.0, 0.0)
    keep = jnp.where(seg_row == final, 1.0, 0.0)
    carry = jnp.where(before == final, 1.0, 0.0)
    mid = jnp.where(upper, decay[SPAN + SPAN // 2 :][:1], decay[SPAN // 2 :][:1])
    grow = jnp.exp(decay - mid)
    shrink = jnp.exp(mid - decay)
    edge = jnp.exp(-jnp.abs(decay - decay[SPAN - 1 : SPAN]))
    from_start = jnp.exp(decay) * alive
    last = decay[CHUNK - 1 : CHUNK]
    to_end = jnp.exp(last - decay) * keep
    step = jnp.exp(last) * carry
    q_near = (queries * grow).astype(BF16)
    k_near = (keys * shrink).astype(BF16)
    q_far = (queries * edge).astype(BF16)
    k_far = (keys * edge).astype(BF16)
    q_state = (queries * from_start).astype(BF16)
    k_state = (keys * to_end).astype(BF16)
    scores = jnp.where(near, nt(q_near, k_near), jnp.where(far, nt(q_far, k_far), 0.0)).astype(BF16)
    return (
        (row, col, near, far),
        (grow, shrink, edge, from_start, to_end, step),
        (q_near, k_near, q_far, k_far, q_state, k_state),
        scores,
    )


def slab_at(meta, j):
    return pl.ds(pl.multiple_of(meta[j] * SLAB, SLAB), SLAB)


def lanes_at(start):
    return pl.ds(pl.multiple_of(start, LANES), LANES)


def one_hot(rows, shift):
    row = lax.broadcasted_iota(jnp.int32, (rows, LANES), 0)
    col = lax.broadcasted_iota(jnp.int32, (rows, LANES), 1)
    return jnp.where(col - row == shift, 1.0, 0.0).astype(BF16)


def pack_kernel(qk_ref, vg_ref, lowin_ref, lowout_ref, mixout_ref, gateup_ref, down_ref, attn_ref, feed_ref):
    units = gateup_ref.shape[1]
    width = feed_ref.shape[1] // 3
    attn_ref[:, :DK] = qk_ref[0].astype(BF16)
    attn_ref[:, DK : 2 * DK] = qk_ref[1].astype(BF16)
    attn_ref[:, 2 * DK : 2 * DK + DV] = vg_ref[0].astype(BF16)
    attn_ref[:, 2 * DK + DV : MAIN] = vg_ref[1].astype(BF16)
    attn_ref[:, MAIN:ATTN] = tn(lowin_ref[...].astype(BF16), one_hot(RANK, 0)).astype(BF16)
    lowout = lowout_ref[...].astype(BF16)
    attn_ref[:RANK, MAIN:ATTN] += nn(lowout, one_hot(lowout.shape[1], RANK)).astype(BF16)
    attn_ref[:, ATTN:] = mixout_ref[...].T.astype(BF16)
    rows = feed_ref.shape[0]
    pad = jnp.zeros((rows, width - units), BF16)
    feed_ref[:, :units] = gateup_ref[0].T.astype(BF16)
    feed_ref[:, units:width] = pad
    feed_ref[:, width : width + units] = gateup_ref[1].T.astype(BF16)
    feed_ref[:, width + units : 2 * width] = pad
    feed_ref[:, 2 * width : 2 * width + units] = down_ref[...].T.astype(BF16)
    feed_ref[:, 2 * width + units :] = pad


def assemble_kernel(place, *refs):
    pieces = refs[: 2 * SLABS]
    w_ref, wo_ref, wb_ref = refs[2 * SLABS :]
    rows = pieces[0].shape[0]
    keys = DK // (2 * SLABS)
    wb_ref[...] = jnp.zeros_like(wb_ref)
    for i, piece in enumerate(pieces):
        block = place[i]
        at = pl.ds(pl.multiple_of(block * rows, rows), rows)
        w_ref[at, :] = piece[:, :ATTN]
        wo_ref[at, :] = piece[:, ATTN:]
        row = lax.broadcasted_iota(jnp.int32, (LANES, DK), 0)
        col = lax.broadcasted_iota(jnp.int32, (LANES, DK), 1)
        inside = (row >= RANK) & (row < RANK + keys)
        move = jnp.where(inside & (col - row == block * keys - RANK), 1.0, 0.0).astype(BF16)
        wb_ref[:RANK, :] += nn(piece[:RANK, MAIN:ATTN], move).astype(BF16)


def attend_kernel(first_block, n_saved, meta, *refs):
    x_ref, w_ref, wo_ref, wb_ref, g1_ref, go_ref, c_ref, state_ref = refs[:8]
    refs = refs[8 + n_saved :]
    part_ref, state_out_ref = refs[:2]
    xn_ref, qkv_ref, gout_ref, lowr_ref, zeta_ref, mixed_ref, z_ref, states_ref = refs[2:]
    step = pl.program_id(0)

    @pl.when(step == 0)
    def _():
        state_out_ref[...] = state_ref[...]

    ends = [meta[SLABS + i] for i in range(meta.shape[0] - SLABS)]
    x = x_ref[...].astype(F32)
    scale = lax.rsqrt(jnp.mean(x * x, axis=-1, keepdims=True) + NORM_EPS)
    normed = (x * scale * g1_ref[...]).astype(BF16)
    xn_ref[...] = normed
    proj = nn(normed, w_ref[...])
    qkv = proj[:, : 2 * DK + DV].astype(BF16)
    qkv_ref[...] = qkv
    gout = proj[:, 2 * DK + DV : MAIN]
    gout_ref[...] = gout
    lowr = proj[:, MAIN:].astype(BF16)
    lowr_ref[...] = lowr
    zeta = nn(lowr, wb_ref[...]) + c_ref[...]
    zeta_ref[...] = zeta
    forget = log_sigmoid(zeta) * (1.0 / GATE_NORM)
    base = (first_block + step) * BLOCK
    state = state_out_ref[...]
    for i in range(BLOCK // CHUNK):
        rows = slice(i * CHUNK, (i + 1) * CHUNK)
        queries = qkv[rows, :DK].astype(F32)
        keys = qkv[rows, DK : 2 * DK].astype(F32)
        values = qkv[rows, 2 * DK :]
        start = base + i * CHUNK
        _, factors, terms, scores = chunk_terms(queries, keys, forget[rows], start, ends)
        q_state, k_state = terms[4:]
        state_low = state.astype(BF16)
        states_ref[i * DV : (i + 1) * DV, :] = state_low
        mixed = (nn(scores, values) + nt(q_state, state_low)) * OUT_SCALE
        mixed_ref[rows, :] = mixed
        state = state * factors[5] + tn(values, k_state)
        where = lax.broadcasted_iota(jnp.int32, (CHUNK, DV), 0) + start
        valid = jnp.where(where < ends[-1], 1.0, 0.0)
        head_scale = lax.rsqrt(jnp.mean(mixed * mixed, axis=-1, keepdims=True) + NORM_EPS)
        gate = gout[rows]
        z = mixed * head_scale * go_ref[...] * (gate * jax.nn.sigmoid(gate)) * valid
        z_ref[rows, :] = z.astype(BF16)
    state_out_ref[...] = state
    z = z_ref[...]
    for j in range(SLABS):
        part_ref[:, j * SLAB : (j + 1) * SLAB] = nt(z, wo_ref[slab_at(meta, j), :]).astype(BF16)


def summed(mine, core, far, far_core, j):
    other = (j + 2) % SLABS
    total = mine[:, j * SLAB : (j + 1) * SLAB].astype(F32)
    total = total + core[:, other * SLAB : (other + 1) * SLAB].astype(F32)
    beyond = far if j < 2 else far_core
    k = 1 - j % 2
    return total + beyond[:, k * SLAB : (k + 1) * SLAB].astype(F32)


def feed_kernel(n_saved, meta, *refs):
    x_ref, terms, dys = refs[0], refs[1:5], refs[5:9]
    wf_ref, g2_ref = refs[9:11]
    refs = refs[11 + n_saved :]
    part_ref = refs[0]
    feed_keep_ref, feed_send_ref, hn_ref, dy_ref, hidden_ref, dgu_ref, rhat_ref, rs_ref, resid_ref = refs[1:]
    width = hidden_ref.shape[1]
    resid = []
    total = 0.0
    for j in range(SLABS):
        part = x_ref[:, slab_at(meta, j)].astype(F32) + summed(*terms, j)
        resid.append(part)
        total = total + jnp.sum(part * part, axis=-1, keepdims=True)
    resid_ref[...] = resid[0]
    scale = lax.rsqrt(total / D + NORM_EPS)
    rs_ref[...] = jnp.broadcast_to(scale, rs_ref.shape)
    units = 0.0
    dhid = 0.0
    for j in range(SLABS):
        at = slab_at(meta, j)
        rhat = resid[j] * scale
        rhat_ref[:, j * SLAB : (j + 1) * SLAB] = rhat.astype(BF16)
        hn = (rhat * g2_ref[:, at]).astype(BF16)
        hn_ref[:, at] = hn
        dy = dys[j][...]
        dy_ref[:, at] = dy
        units = units + nn(hn, wf_ref[at, : 2 * width])
        dhid = dhid + nn(dy, wf_ref[at, 2 * width :])
    gate = units[:, :width]
    up = units[:, width:]
    sig = jax.nn.sigmoid(gate)
    act = gate * sig
    hidden = (act * up).astype(BF16)
    hidden_ref[...] = hidden
    dgate = (dhid * up * (sig * (1.0 + gate * (1.0 - sig)))).astype(BF16)
    dup = (dhid * act).astype(BF16)
    dgu_ref[:, :width] = dgate
    dgu_ref[:, width:] = dup
    for j in range(SLABS):
        at = slab_at(meta, j)
        part = nt(dgate, wf_ref[at, :width]) + nt(dup, wf_ref[at, width : 2 * width])
        part_ref[:, j * SLAB : (j + 1) * SLAB] = part.astype(BF16)
        fed = nt(hidden, wf_ref[at, 2 * width :]).astype(BF16)
        target = feed_keep_ref if j < 2 else feed_send_ref
        target[:, (j % 2) * SLAB : (j % 2 + 1) * SLAB] = fed


LOWIN_ROW = 0
IN_ROW = 16
MID_ROW = 17
HEAD_ROW = 18
LOWOUT_ROW = 24
SUM_ROWS = 32


def back_kernel(last_block, n_saved, meta, *refs):
    terms = refs[:4]
    dy_ref, rhat_ref, rs_ref, x_ref, xn_ref = refs[4:9]
    qkv_ref, gout_ref, lowr_ref, zeta_ref, mixed_ref, states_ref = refs[9:15]
    w_ref, wo_ref, wb_ref, g2_ref, go_ref = refs[15:20]
    dstate_ref, next_ref, sums_ref = refs[20:23]
    refs = refs[23 + n_saved :]
    keep_ref, send_ref, dstate_out_ref, next_out_ref, sums_out_ref = refs[:5]
    dres16_ref, dres_ref, dall_ref = refs[5:]
    step = pl.program_id(0)

    @pl.when(step == 0)
    def _():
        dstate_out_ref[...] = dstate_ref[...]
        next_out_ref[...] = next_ref[...]
        sums_out_ref[...] = sums_ref[...]

    ends = [meta[SLABS + i] for i in range(meta.shape[0] - SLABS)]
    base = (last_block - step) * BLOCK
    scaled = []
    dot = 0.0
    for j in range(SLABS):
        dhn = summed(*terms, j)
        rhat = rhat_ref[:, j * SLAB : (j + 1) * SLAB].astype(F32)
        if j == 0:
            sums_out_ref[MID_ROW : MID_ROW + 1, slab_at(meta, 0)] += jnp.sum(
                dhn * rhat, axis=0, keepdims=True
            )
        part = dhn * g2_ref[:, slab_at(meta, j)]
        scaled.append(part)
        dot = dot + jnp.sum(part * rhat, axis=-1, keepdims=True)
    scale = rs_ref[:, :1]
    mean = dot / D
    dz = 0.0
    for j in range(SLABS):
        at = slab_at(meta, j)
        rhat = rhat_ref[:, j * SLAB : (j + 1) * SLAB].astype(F32)
        dres = dy_ref[:, at].astype(F32) + scale * (scaled[j] - rhat * mean)
        if j == 0:
            dres_ref[...] = dres
        low = dres.astype(BF16)
        dres16_ref[:, at] = low
        dz = dz + nn(low, wo_ref[at, :])
    where = lax.broadcasted_iota(jnp.int32, (BLOCK, DV), 0) + base
    u = jnp.where(where < ends[-1], dz, 0.0)
    mixed = mixed_ref[...]
    head_scale = lax.rsqrt(jnp.mean(mixed * mixed, axis=-1, keepdims=True) + NORM_EPS)
    hat = mixed * head_scale
    gate = gout_ref[...]
    sig = jax.nn.sigmoid(gate)
    act = gate * sig
    uhat = u * hat
    go = go_ref[...]
    sums_out_ref[HEAD_ROW : HEAD_ROW + 1, :DV] += jnp.sum(uhat * act, axis=0, keepdims=True)
    dall_ref[:, 2 * DK + DV : MAIN] = (uhat * go * (sig * (1.0 + gate * (1.0 - sig)))).astype(BF16)
    dhat = u * go * act
    dmix = head_scale * (dhat - hat * jnp.mean(dhat * hat, axis=-1, keepdims=True))
    dmix = (dmix * OUT_SCALE).astype(BF16)
    zeta = zeta_ref[...]
    forget = log_sigmoid(zeta) * (1.0 / GATE_NORM)
    slope = jax.nn.sigmoid(-zeta) * (1.0 / GATE_NORM)
    dstate = dstate_out_ref[...]
    after = next_out_ref[...]
    head_at = meta[0] * DK
    for i in reversed(range(BLOCK // CHUNK)):
        rows = slice(i * CHUNK, (i + 1) * CHUNK)
        queries = qkv_ref[rows, :DK].astype(F32)
        keys = qkv_ref[rows, DK : 2 * DK].astype(F32)
        values = qkv_ref[rows, 2 * DK :]
        masks, factors, parts, scores = chunk_terms(
            queries, keys, forget[rows], base + i * CHUNK, ends
        )
        row, col, near, far = masks
        grow, shrink, edge, from_start, to_end, decay_step = factors
        q_near, k_near, q_far, k_far, q_state, k_state = parts
        state = states_ref[i * DV : (i + 1) * DV, :]
        do = dmix[rows]
        dstate_low = dstate.astype(BF16)
        dscores = nt(do, values)
        dnear = jnp.where(near, dscores, 0.0).astype(BF16)
        dfar = jnp.where(far, dscores, 0.0).astype(BF16)
        dv = tn(scores, do) + nt(k_state, dstate_low)
        dq = nn(do, state) * from_start + nn(dnear, k_near) * grow
        dq = dq + jnp.where(row >= SPAN, nn(dfar, k_far) * edge, 0.0)
        dk = nn(values, dstate_low) * to_end + tn(dnear, q_near) * shrink
        dk = dk + jnp.where(row < SPAN, tn(dfar, q_far) * edge, 0.0)
        dall_ref[rows, :DK] = dq.astype(BF16)
        dall_ref[rows, DK : 2 * DK] = dk.astype(BF16)
        dall_ref[rows, 2 * DK : 2 * DK + DV] = dv.astype(BF16)
        at_end = jnp.sum(dstate * after.astype(F32), axis=0, keepdims=True)
        ddecay = queries * dq - keys * dk
        dforget = prefix_sums(ddecay, jnp.where(col >= row, 1.0, 0.0).astype(BF16)) + at_end
        dzeta = (dforget * slope[rows]).astype(BF16)
        sums_out_ref[HEAD_ROW : HEAD_ROW + 1, lanes_at(DV + head_at)] += jnp.sum(
            dzeta.astype(F32), axis=0, keepdims=True
        )
        dlowout = tn(lowr_ref[rows, :], dzeta)
        for k in range(2):
            sums_out_ref[LOWOUT_ROW:, lanes_at(k * (D // 2) + head_at)] += dlowout[k * 8 : (k + 1) * 8]
        dall_ref[rows, MAIN:] = nt(dzeta, wb_ref[...]).astype(BF16)
        dstate = dstate * decay_step + tn(do, q_state)
        after = state
    dstate_out_ref[...] = dstate
    next_out_ref[...] = after
    dall = dall_ref[...]
    sums_out_ref[LOWIN_ROW : LOWIN_ROW + RANK, :] += tn(dall[:, MAIN:], xn_ref[...])[:RANK]
    x = x_ref[...].astype(F32)
    in_scale = lax.rsqrt(jnp.mean(x * x, axis=-1, keepdims=True) + NORM_EPS)
    for j in range(SLABS):
        at = slab_at(meta, j)
        part = nt(dall, w_ref[at, :])
        sums_out_ref[IN_ROW : IN_ROW + 1, at] += jnp.sum(
            part * (x_ref[:, at].astype(F32) * in_scale), axis=0, keepdims=True
        )
        target = keep_ref if j < 2 else send_ref
        target[:, (j % 2) * SLAB : (j % 2 + 1) * SLAB] = part.astype(BF16)


def feed_grad_kernel(first_ref, second_ref, *refs):
    refs[-1][...] = tn(first_ref[...], second_ref[...]).astype(BF16)


def attn_grad_kernel(row_ref, xn_ref, dres_ref, dall_ref, z_ref, here_ref, away_ref, both_ref):
    both_ref[:, :MAIN] = tn(xn_ref[...], dall_ref[:, :MAIN])
    both_ref[:, MAIN:] = tn(dres_ref[...], z_ref[...])
    rows = here_ref.shape[1]
    row = row_ref[0]
    here_ref[0] = both_ref[pl.ds(pl.multiple_of(row * rows, rows), rows), :].astype(BF16)
    away_ref[0] = both_ref[pl.ds(pl.multiple_of((1 - row) * rows, rows), rows), :].astype(BF16)


def update_kernel(clip_ref, attn_ref, feed_ref, *refs):
    masters, firsts, seconds = refs[:5], refs[5:10], refs[10:15]
    outs, turned, turned_attn = refs[15:30], refs[30], refs[31]
    step = pl.program_id(0)

    @pl.when(step == 0)
    def _():
        turned[...] = feed_ref[...].astype(F32).T
        turned_attn[...] = attn_ref[:, MAIN:].T

    clip = clip_ref[0]
    width = feed_ref.shape[1] // 3

    def rows(count):
        if count == attn_ref.shape[0]:
            return slice(None)
        return pl.ds(pl.multiple_of(step * count, 8), count)

    def units(k):
        count = masters[4].shape[0]
        return turned[pl.ds(pl.multiple_of(k * width + step * count, 8), count), :]

    attn = attn_ref[rows(masters[0].shape[1]), :]
    across = masters[2].shape[0]
    grads = (
        (attn[:, :DK], attn[:, DK : 2 * DK]),
        (attn[:, 2 * DK : 2 * DK + DV], attn[:, 2 * DK + DV : MAIN]),
        (turned_attn[pl.ds(pl.multiple_of(step * across, 8), across), :],),
        (units(0), units(1)),
        (units(2),),
    )
    rates = (D, D, HEADS * DV, D, FF)
    for i in range(5):
        for k, grad in enumerate(grads[i]):
            at = k if len(grads[i]) > 1 else Ellipsis
            results = adam_step(
                masters[i][at], grad, firsts[i][at], seconds[i][at], clip, 2.0 * rates[i] ** (-0.5), WEIGHT_DECAY
            )
            for n in range(3):
                outs[n * 5 + i][at] = results[n]


def whole(array):
    zeros = (0,) * array.ndim
    return pl.BlockSpec(array.shape, lambda i, meta: zeros, pipeline_mode=pl.Buffered(1))


def fixed(shape):
    return pl.BlockSpec(shape, lambda i, meta: (0,) * len(shape))


def rows_at(rows, width, place):
    return pl.BlockSpec((rows, width), lambda i, meta: (place(i), 0))


def like(shape, dtype):
    return jax.ShapeDtypeStruct(shape, dtype)


def params():
    return pltpu.CompilerParams(vmem_limit_bytes=VMEM_LIMIT)


def run_kernel(body, meta, steps, ins, in_specs, saved, outs, out_specs, saved_like, saved_specs, name, flops):
    given = [] if saved is None else list(saved)
    aliases = {1 + len(ins) + i: len(outs) + i for i in range(len(given))}
    result = pl.pallas_call(
        functools.partial(body, len(given)),
        grid_spec=pltpu.PrefetchScalarGridSpec(
            num_scalar_prefetch=1,
            grid=(steps,),
            in_specs=list(in_specs) + [pl.BlockSpec(memory_space=pl.ANY)] * len(given),
            out_specs=list(out_specs) + list(saved_specs),
        ),
        out_shape=list(outs) + list(saved_like),
        input_output_aliases=aliases,
        compiler_params=params(),
        cost_estimate=pl.CostEstimate(flops=flops, bytes_accessed=16 * 1024 * 1024, transcendentals=0),
        name=name,
    )(meta, *ins, *given)
    return list(result[: len(outs)]), list(result[len(outs) :])


def attend(piece, meta, x, w, wo, wb, g1, go, c, state, saved):
    tokens = x.shape[0]
    size = tokens // PIECES
    steps = size // BLOCK
    first = piece * steps
    here = lambda i: first + i
    ins = [x, w, wo, wb, g1, go, c, state]
    in_specs = [rows_at(BLOCK, D, here)] + [whole(a) for a in ins[1:]]
    outs = [like((size, D), BF16), like(state.shape, F32)]
    out_specs = [rows_at(BLOCK, D, lambda i: i), fixed(state.shape)]
    widths = [
        (D, BF16),
        (2 * DK + DV, BF16),
        (DV, F32),
        (LANES, BF16),
        (DK, F32),
        (DV, F32),
        (DV, BF16),
    ]
    saved_like = [like((tokens, n), d) for n, d in widths]
    saved_specs = [rows_at(BLOCK, n, here) for n, _ in widths]
    saved_like.append(like((tokens // CHUNK * DV, DK), BF16))
    saved_specs.append(rows_at(BLOCK // CHUNK * DV, DK, here))
    return run_kernel(
        functools.partial(attend_kernel, first),
        meta, steps, ins, in_specs, saved, outs, out_specs, saved_like, saved_specs,
        "attend", size * 8 * D * 1024,
    )


def feed(piece, meta, x, terms, dys, wf, g2, saved):
    tokens = x.shape[0]
    size = tokens // PIECES
    steps = size // BLOCK
    first = piece * steps
    here = lambda i: first + i
    width = wf.shape[1] // 3
    ins = [x, *terms, *dys, wf, g2]
    in_specs = (
        [rows_at(BLOCK, D, here)]
        + [rows_at(BLOCK, a.shape[1], lambda i: i) for a in terms]
        + [rows_at(BLOCK, SLAB, here)] * SLABS
        + [whole(wf), whole(g2)]
    )
    outs = [like((size, D), BF16)]
    out_specs = [rows_at(BLOCK, D, lambda i: i)]
    widths = [
        (2 * SLAB, BF16),
        (2 * SLAB, BF16),
        (D, BF16),
        (D, BF16),
        (width, BF16),
        (2 * width, BF16),
        (D, BF16),
        (LANES, F32),
        (SLAB, F32),
    ]
    saved_like = [like((tokens, n), d) for n, d in widths]
    saved_specs = [rows_at(BLOCK, n, here) for n, _ in widths]
    return run_kernel(
        feed_kernel,
        meta, steps, ins, in_specs, saved, outs, out_specs, saved_like, saved_specs,
        "feed", size * 2 * D * width * 6,
    )


def back(piece, meta, terms, dy, rhat, rs, x, xn, kept, w, wo, wb, g2, go, carried, saved):
    tokens = x.shape[0]
    size = tokens // PIECES
    steps = size // BLOCK
    last = (piece + 1) * steps - 1
    here = lambda i: last - i
    local = lambda i: steps - 1 - i
    ins = [*terms, dy, rhat, rs, x, xn, *kept, w, wo, wb, g2, go, *carried]
    in_specs = (
        [rows_at(BLOCK, a.shape[1], local) for a in terms]
        + [rows_at(BLOCK, a.shape[1], here) for a in (dy, rhat, rs, x, xn)]
        + [rows_at(BLOCK, a.shape[1], here) for a in kept[:-1]]
        + [rows_at(BLOCK // CHUNK * DV, DK, here)]
        + [whole(a) for a in (w, wo, wb, g2, go, *carried)]
    )
    outs = [like((size, 2 * SLAB), BF16)] * 2 + [like(a.shape, a.dtype) for a in carried]
    out_specs = [rows_at(BLOCK, 2 * SLAB, local)] * 2 + [fixed(a.shape) for a in carried]
    widths = [(D, BF16), (SLAB, F32), (ATTN, BF16)]
    saved_like = [like((tokens, n), d) for n, d in widths]
    saved_specs = [rows_at(BLOCK, n, here) for n, _ in widths]
    return run_kernel(
        functools.partial(back_kernel, last),
        meta, steps, ins, in_specs, saved, outs, out_specs, saved_like, saved_specs,
        "back", size * 12 * D * 1024,
    )


def feed_grad(first, second, column, full):
    tokens, width = second.shape
    ins = [first, second] + ([] if full is None else [full])
    return pl.pallas_call(
        feed_grad_kernel,
        grid=(D // SLAB,),
        in_specs=[
            pl.BlockSpec((tokens, SLAB), lambda i: (0, i)),
            pl.BlockSpec((tokens, width), lambda i: (0, 0), pipeline_mode=pl.Buffered(1)),
        ]
        + [pl.BlockSpec(memory_space=pl.ANY)] * (len(ins) - 2),
        out_specs=pl.BlockSpec((SLAB, width), lambda i: (i, column)),
        out_shape=like((D, FEED_COLS), BF16),
        input_output_aliases={2: 0} if len(ins) > 2 else {},
        compiler_params=params(),
        cost_estimate=pl.CostEstimate(
            flops=4 * D * tokens * width, bytes_accessed=8 * 1024 * 1024, transcendentals=0
        ),
        name="feed_grad",
    )(*ins)


def attn_grad(row, xn, dres16, dall, z):
    tokens = xn.shape[0]
    half = SLAB // 2
    column = lambda i, row: (0, i)
    return pl.pallas_call(
        attn_grad_kernel,
        grid_spec=pltpu.PrefetchScalarGridSpec(
            num_scalar_prefetch=1,
            grid=(SLABS,),
            in_specs=[pl.BlockSpec((tokens, SLAB), column)] * 2 + [whole(dall), whole(z)],
            out_specs=[pl.BlockSpec((1, half, D), lambda i, row: (i, 0, 0))] * 2,
            scratch_shapes=[pltpu.VMEM((SLAB, D), F32)],
        ),
        out_shape=[like((SLABS, half, D), BF16)] * 2,
        compiler_params=params(),
        cost_estimate=pl.CostEstimate(
            flops=4 * D * tokens * D, bytes_accessed=8 * 1024 * 1024, transcendentals=0
        ),
        name="attn_grad",
    )(row, xn, dres16, dall, z)


def update(clip, attn, feed, arrays):
    rows = attn.shape[0]
    steps = 4 if rows % 32 == 0 else 1
    masters = arrays[:5]

    def cut(array):
        shape = list(array.shape)
        shape[-2] //= steps
        zeros = (0,) * (len(shape) - 2)
        return pl.BlockSpec(tuple(shape), lambda i: (*zeros, i, 0))

    return pl.pallas_call(
        update_kernel,
        grid=(steps,),
        in_specs=[pl.BlockSpec(memory_space=pltpu.SMEM)]
        + [pl.BlockSpec(a.shape, lambda i: (0, 0), pipeline_mode=pl.Buffered(1)) for a in (attn, feed)]
        + [cut(a) for a in arrays],
        out_specs=[cut(a) for a in masters] * 3,
        out_shape=[like(a.shape, F32) for a in masters] * 3,
        scratch_shapes=[pltpu.VMEM((feed.shape[1], rows), F32), pltpu.VMEM((DV, rows), F32)],
        compiler_params=params(),
        name="update",
    )(clip, attn, feed, *arrays)


def after(array, *others):
    return lax.optimization_barrier((array, *others))[0]


def swap(array, axis, bit):
    return lax.ppermute(array, axis, [(i, i ^ bit) for i in range(lax.axis_size(axis))])


def swap_core(array):
    return swap(array, "tensor", 1)


def swap_far(array):
    return swap(array, "tensor", 2)


def swap_row(array):
    return swap(array, "dp", 1)


def shift_layer(array, by):
    count = lax.axis_size("dp")
    return lax.ppermute(array, "dp", [(i, (i + 2 * by) % count) for i in range(count)])


def gather_attn(own):
    dp_at = lax.axis_index("dp")
    found = {(0, 0): own, (1, 0): shift_layer(own, 1), (3, 0): shift_layer(own, 3), (0, 1): swap_row(own)}
    first = list(found.values())[1:]
    found[2, 0] = shift_layer(after(own, *first), 2)
    for k in (1, 3):
        found[k, 1] = swap_row(after(found[k, 0], *first))
    second = [found[2, 0], found[1, 1], found[3, 1]]
    found[2, 1] = swap_row(after(*second))
    places = [((dp_at - 2 * k) % (2 * SLABS)) ^ h for k, h in found]
    pieces = list(found.values())
    rows = D
    return second, pl.pallas_call(
        assemble_kernel,
        in_specs=[pl.BlockSpec(memory_space=pltpu.SMEM)]
        + [pl.BlockSpec(memory_space=pltpu.VMEM)] * (2 * SLABS),
        out_shape=(like((rows, ATTN), BF16), like((rows, DV), BF16), like((LANES, DK), BF16)),
        compiler_params=params(),
        name="assemble",
    )(jnp.stack(places).astype(jnp.int32), *pieces)


def gather_plain(own):
    count, rows = lax.axis_size("dp"), own.shape[0]
    full = lax.all_gather(own, "dp", axis=0, tiled=True)
    keys = DK // count
    blocks = full.reshape(count, rows, -1)[:, :RANK, MAIN + RANK : MAIN + RANK + keys]
    wb = jnp.pad(blocks.transpose(1, 0, 2).reshape(RANK, DK), ((0, LANES - RANK), (0, 0)))
    return [own], (full[:, :ATTN], full[:, ATTN:], wb)


def scatter_attn(here, away):
    dp_at = lax.axis_index("dp")
    high, low = dp_at // 4, (dp_at // 2) % 2
    rows, width = here.shape[1:]

    def pick(array, axis, index):
        return lax.dynamic_index_in_dim(array, index, axis, keepdims=False)

    first = here.astype(F32) + swap_row(away).astype(F32)
    here = first.reshape(2, 2, rows, width)
    away = pick(here, 1, 1 - low).astype(BF16)
    here = pick(here, 1, low) + swap(away, "dp", 2).astype(F32)
    away = pick(here, 0, 1 - high).astype(BF16)
    return first, pick(here, 0, high) + swap(away, "dp", 4).astype(F32)


def sum_terms(part, earlier):
    core = swap_core(after(part, *earlier))
    own = (part[:, : 2 * SLAB].astype(F32) + core[:, 2 * SLAB :].astype(F32)).astype(BF16)
    return own, part, core, swap_far(own)


def slab_sum(keep, send, earlier):
    own = keep.astype(F32) + swap_core(send).astype(F32)
    far = swap_far(after(own[:, SLAB:].astype(BF16), earlier))
    return own[:, :SLAB] + far.astype(F32), far


def sum_everywhere(array, axes=("tensor", "dp")):
    for axis in axes:
        size = lax.axis_size(axis)
        bit = 1
        while bit < size:
            array = array + swap(array, axis, bit)
            bit *= 2
    return array


def adam_step(weight, gradient, first_moment, second_moment, clip_factor, learn_rate, weight_decay):
    clipped = gradient * clip_factor
    momentum = BETA_FIRST * first_moment + (1.0 - BETA_FIRST) * clipped
    variance = BETA_SECOND * second_moment + (1.0 - BETA_SECOND) * clipped * clipped
    step_size = (
        momentum
        / (1.0 - BETA_FIRST**STEP)
        / (jnp.sqrt(variance / (1.0 - BETA_SECOND**STEP)) + ADAM_EPS)
    )
    updated = weight * (1.0 - learn_rate * weight_decay) - learn_rate * step_size
    return (momentum, variance, updated)


LARGE = (0, 1, 4, 5, 6)


def body(*args):
    inputs, cotangent, doc_lengths = args[:3]
    masters, firsts, seconds = args[3:11], args[11:19], args[19:27]
    weight_qk, weight_vg, weight_lowin, weight_lowout, weight_mixout, weight_gateup, weight_down = masters[:7]
    weight_small = masters[7]
    tensor_at = lax.axis_index("tensor")
    dp_at = lax.axis_index("dp")
    layered = lax.axis_size("dp") == 2 * SLABS
    rows_here = weight_qk.shape[1]
    ranks, _, keys_here = weight_lowout.shape
    turn = lambda i, a: jnp.swapaxes(a, 1, 2) if i == 5 else a
    far_cot = swap_far(cotangent)

    attn_pack, feed_pack = pl.pallas_call(
        pack_kernel,
        out_shape=(like((rows_here, ATTN + DV), BF16), like((rows_here, FEED_COLS), BF16)),
        compiler_params=params(),
        name="pack",
    )(
        weight_qk, weight_vg, weight_lowin.T, weight_lowout[:, 0, :], weight_mixout,
        turn(5, weight_gateup), weight_down,
    )
    arrived, (w, wo, wb) = (gather_attn if layered else gather_plain)(attn_pack)
    wf = lax.all_gather(after(feed_pack, *arrived), "dp", axis=0, tiled=True)
    doc_ends = jnp.cumsum(doc_lengths[0])
    slots = jnp.stack([tensor_at ^ o for o in ORDER])
    meta = jnp.concatenate([slots.astype(jnp.int32), doc_ends.astype(jnp.int32)])

    g1, g2 = weight_small[:D].reshape(1, D), weight_small[D : 2 * D].reshape(1, D)
    go = weight_small[2 * D : 2 * D + DV].reshape(1, DV)
    gate_bias = lax.dynamic_slice_in_dim(weight_small, 2 * D + DV + tensor_at * DK, DK).reshape(1, DK)
    x = inputs
    meta = after(meta, far_cot)
    dys = [cotangent, far_cot, swap_core(after(cotangent, w)), swap_core(after(far_cot, w))]

    state = jnp.zeros((DV, DK), F32)
    saved = None
    terms = []
    earlier = []
    for piece in range(PIECES):
        (part, state), saved = attend(piece, meta, x, w, wo, wb, g1, go, gate_bias, state, saved)
        own, part, core, far = sum_terms(part, earlier)
        terms.append((part, core, far, swap_core(far)))
        earlier = [far]
        state = after(state, own)
    xn, *kept = saved
    z = kept.pop(5)

    fed = None
    back_terms = []
    order = after(meta, own)
    for piece in range(PIECES):
        (part,), fed = feed(piece, order, x, terms[piece], dys, wf, g2, fed)
        own, part, core, far = sum_terms(part, earlier)
        earlier = [far]
        order = after(meta, own)
        if piece < PIECES - 1:
            back_terms.append((part, core, far, swap_core(far)))
    feed_keep, feed_send, hn, dy, hidden, dgu, rhat, rs, resid = fed
    fed_own = (feed_keep.astype(F32) + swap_core(feed_send).astype(F32)).astype(BF16)
    grad_feed = feed_grad(dy, hidden, 2, None)
    grad_feed = feed_grad(after(hn, own, fed_own), dgu, 0, grad_feed)
    back_terms.append((part, core, far, swap_core(after(far, grad_feed))))
    shard_feed = lax.psum_scatter(grad_feed, "dp", scatter_dimension=0, tiled=True)
    fed_far = swap_far(after(fed_own[:, SLAB:], far))
    output = (resid + (fed_own[:, :SLAB].astype(F32) + fed_far.astype(F32))).astype(BF16)

    carried = [jnp.zeros((DV, DK), F32), jnp.zeros((DV, DK), BF16), jnp.zeros((SUM_ROWS, D), F32)]
    backed = None
    dxn = []
    order = after(meta, grad_feed)
    for piece in reversed(range(PIECES)):
        (keep, send, *carried), backed = back(
            piece, order, back_terms[piece], dy, rhat, rs, x, xn, kept, w, wo, wb, g2, go, carried, backed
        )
        if piece == PIECES - 1:
            order = meta
        dxn.insert(0, (keep, send))
    dres16, dres, dall = backed
    row_at = (dp_at % 2 if layered else jnp.zeros_like(dp_at)).astype(jnp.int32).reshape(1)
    here, away = attn_grad(row_at, xn, dres16, dall, z)
    earlier = fed_far
    for piece in reversed(range(PIECES)):
        keep, send = dxn[piece]
        dxn[piece], earlier = slab_sum(keep, after(send, here), earlier)
    if layered:
        half_summed, shard_attn = scatter_attn(here, away)
    else:
        half_summed = here
        shard_attn = lax.psum_scatter(
            jnp.stack([here, away], axis=1).reshape(D, D), "dp", scatter_dimension=0, tiled=True
        ).astype(F32)

    dxn = jnp.concatenate(dxn, axis=0)
    x_wide = x.astype(F32)
    in_scale = lax.rsqrt(jnp.mean(x_wide * x_wide, axis=-1, keepdims=True) + NORM_EPS)
    hat_here = lax.dynamic_slice_in_dim(x, tensor_at * SLAB, SLAB, 1).astype(F32) * in_scale
    scaled = dxn * lax.dynamic_slice_in_dim(g1, tensor_at * SLAB, SLAB, 1)
    row_sums = jnp.sum(scaled * hat_here, axis=-1).reshape(-1, LANES)
    row_mean = sum_everywhere(row_sums, ("tensor",)).reshape(-1, 1) / D
    input_grad = dres + in_scale * (scaled - hat_here * row_mean)

    wide = sum_everywhere(after(carried[2], half_summed))
    small_grad = jnp.concatenate([wide[IN_ROW], wide[MID_ROW], wide[HEAD_ROW, : DV + HEADS * DK]])
    grad_lowin = lax.dynamic_slice(wide, (LOWIN_ROW, dp_at * rows_here), (RANK, rows_here)).T
    lowout = jnp.concatenate([wide[LOWOUT_ROW:, : D // 2], wide[LOWOUT_ROW:, D // 2 :]], axis=0)
    grad_lowout = lax.dynamic_slice(
        lowout, (0, tensor_at * DK + dp_at * keys_here), (RANK, keys_here)
    ).reshape(weight_lowout.shape)

    squares = sum(jnp.sum(jnp.square(s.astype(F32))) for s in (shard_feed, shard_attn))
    square_total = sum_everywhere(jnp.broadcast_to(squares, (8, LANES)))[0, 0]
    grad_norm = jnp.sqrt(square_total + jnp.sum(wide * wide))
    clip_factor = jnp.minimum(1.0, CLIP_NORM / (grad_norm + 1e-06))
    arrays = [turn(i, group[i]) for group in (masters, firsts, seconds) for i in LARGE]
    large = update(clip_factor.reshape(1), shard_attn, shard_feed, arrays)
    small_rate = jnp.where(
        lax.broadcasted_iota(jnp.int32, weight_small.shape, 0) < 2 * D + DV, GAIN_RATE, BIAS_RATE
    )
    steps = {}
    for k, i in enumerate(LARGE):
        steps[i] = [turn(i, a) for a in large[k::5]]
    for i, grad, rate, decay in (
        (2, grad_lowin, 2.0 * D ** (-0.5), WEIGHT_DECAY),
        (3, grad_lowout, 2.0 * RANK ** (-0.5), WEIGHT_DECAY),
        (7, small_grad, small_rate, 0.0),
    ):
        steps[i] = adam_step(masters[i], grad, firsts[i], seconds[i], clip_factor, rate, decay)
    return (output, input_grad, grad_norm.reshape(1), *(steps[i][k] for k in range(3) for i in range(8)))


def solution(mesh):
    weights = (
        P(None, "dp", "tensor"),
        P(None, "dp", "tensor"),
        P("dp", None),
        P(None, "tensor", "dp"),
        P("tensor", "dp"),
        P(None, "dp", "tensor"),
        P("tensor", "dp"),
        P(),
    )
    return jax.shard_map(
        body,
        mesh=mesh,
        in_specs=(P("dp", None), P("dp", "tensor"), P("dp", None), *weights, *weights, *weights),
        out_specs=(P("dp", "tensor"), P("dp", "tensor"), P(), *weights, *weights, *weights),
        check_vma=False,
    )
```

profile of v0, /device:TPU:0, one launch (start us, length us, event | category | flops | bytes accessed | tf_op | source)
XLA Modules:
  0.0 393.2 jit_solution(13863973250375619940)
XLA Ops:
  9.9 3.0 collective-permute-start.1
  16.7 6.3 %collective-permute-done.1.refs_1_ = bf16[128,1152]{1,0:T(8,128)(2,1)S(1)} collective-permute-done((bf16[128,1152]{1,0:T(8,128)(2,1)}, bf16[128,1152]{1,0:T(8,128)(2,1)S(1)}, u32[]{:S(2)}, u32[]{:S(2)}) %collective-permute-start.1) | collective-permute-done | bytes 294944 | tf_op jit(solution)/shard_map/ppermute | solution.py:682
  23.0 4.9 %collective-permute-done.2.refs_2_ = bf16[128,1152]{1,0:T(8,128)(2,1)S(1)} collective-permute-done((bf16[128,1152]{1,0:T(8,128)(2,1)}, bf16[128,1152]{1,0:T(8,128)(2,1)S(1)}, u32[]{:S(2)}, u32[]{:S(2)}) %collective-permute-start.2) | collective-permute-done | bytes 294944 | tf_op jit(solution)/shard_map/ppermute | solution.py:682
  31.3 12.4 %collective-permute-done.4.refs_4_ = bf16[128,1152]{1,0:T(8,128)(2,1)S(1)} collective-permute-done((bf16[128,1152]{1,0:T(8,128)(2,1)}, bf16[128,1152]{1,0:T(8,128)(2,1)S(1)}, u32[]{:S(2)}, u32[]{:S(2)}) %collective-permute-start.4) | collective-permute-done | bytes 294944 | tf_op jit(solution)/shard_map/ppermute | solution.py:682
  51.5 6.8 %collective-permute-done.7.refs_7_ = bf16[128,1152]{1,0:T(8,128)(2,1)S(1)} collective-permute-done((bf16[128,1152]{1,0:T(8,128)(2,1)S(1)}, bf16[128,1152]{1,0:T(8,128)(2,1)S(1)}, u32[]{:S(2)}, u32[]{:S(2)}) %collective-permute-start.7) | collective-permute-done | bytes 294944 | tf_op jit(solution)/shard_map/ppermute | solution.py:665
  59.1 3.1 assemble.1
  62.2 7.0 %collective-permute-done.refs_6_ = bf16[2048,256]{1,0:T(8,128)(2,1)S(1)} collective-permute-done((bf16[2048,256]{1,0:T(8,128)(2,1)S(1)}, bf16[2048,256]{1,0:T(8,128)(2,1)S(1)}, u32[]{:S(2)}, u32[]{:S(2)}) %collective-permute-start) | collective-permute-done | bytes 1048608 | tf_op jit(solution)/shard_map/ppermute | solution.py:665
  69.9 12.1 %attend.2 = (bf16[1024,1024]{1,0:T(8,128)(2,1)}, f32[256,128]{1,0:T(8,128)}, bf16[2048,1024]{1,0:T(8,128)(2,1)}, bf16[2048,512]{1,0:T(8,128)(2,1)}, f32[2048,256...) custom-call(s32[7]{0:T(128)} %concatenate.12.meta, ...), custom_call_target="tpu_custom_call" | custom-call | flops 8589934592 | bytes 16777216 | tf_op jit(solution)/shard_map/attend/pallas_call | solution.py:481
  82.1 4.4 %collective-permute-done.8.refs_2_ = bf16[1024,1024]{1,0:T(8,128)(2,1)S(1)} collective-permute-done((bf16[1024,1024]{1,0:T(8,128)(2,1)}, bf16[1024,1024]{1,0:T(8,128)(2,1)S(1)}, u32[]{:S(2)}, u32[]{:S(2)}) %collective-permute-start.8) | collective-permute-done | bytes 2097184 | tf_op jit(solution)/shard_map/ppermute | solution.py:665
  90.4 12.2 %attend.3 = (bf16[1024,1024]{1,0:T(8,128)(2,1)}, f32[256,128]{1,0:T(8,128)}, bf16[2048,1024]{1,0:T(8,128)(2,1)}, bf16[2048,512]{1,0:T(8,128)(2,1)}, f32[2048,256...) custom-call(s32[7]{0:T(128)} %concatenate.12.meta, ...), custom_call_target="tpu_custom_call", output_to_operand_aliasing={{2}: (9, {}), {3}: (10, {}), {4}: (11, {}), {5}: (12, {}), ... | custom-call | flops 8589934592 | bytes 16777216 | tf_op jit(solution)/shard_map/attend/pallas_call | solution.py:481
  102.6 11.5 %collective-permute-done.9.refs_3_ = bf16[1024,512]{1,0:T(8,128)(2,1)S(1)} collective-permute-done((bf16[1024,512]{1,0:T(8,128)(2,1)S(1)}, bf16[1024,512]{1,0:T(8,128)(2,1)S(1)}, u32[]{:S(2)}, u32[]{:S(2)}) %collective-permute-start.9) | collective-permute-done | bytes 1048608 | tf_op jit(solution)/shard_map/ppermute | solution.py:665
  116.1 6.3 %collective-permute-done.10.refs_2_ = bf16[1024,1024]{1,0:T(8,128)(2,1)S(1)} collective-permute-done((bf16[1024,1024]{1,0:T(8,128)(2,1)}, bf16[1024,1024]{1,0:T(8,128)(2,1)S(1)}, u32[]{:S(2)}, u32[]{:S(2)}) %collective-permute-start.10) | collective-permute-done | bytes 2097184 | tf_op jit(solution)/shard_map/ppermute | solution.py:665
  122.4 3.3 add_convert_fusion.4
  129.3 20.3 %feed.2 = (bf16[1024,1024]{1,0:T(8,128)(2,1)}, bf16[2048,512]{1,0:T(8,128)(2,1)}, bf16[2048,512]{1,0:T(8,128)(2,1)}, bf16[2048,1024]{1,0:T(8,128)(2,1)}, bf16[20...) custom-call(s32[7]{0:T(128)} %concatenate.12.meta, ...), custom_call_target="tpu_custom_call" | custom-call | flops 9663676416 | bytes 16777216 | tf_op jit(solution)/shard_map/feed/pallas_call | solution.py:481
  151.8 3.9 collective-permute-done.15.refs_1_
  160.6 20.3 %feed.3 = (bf16[1024,1024]{1,0:T(8,128)(2,1)}, bf16[2048,512]{1,0:T(8,128)(2,1)}, bf16[2048,512]{1,0:T(8,128)(2,1)}, bf16[2048,1024]{1,0:T(8,128)(2,1)}, bf16[20...) custom-call(s32[7]{0:T(128)} %concatenate.12.meta, ...), custom_call_target="tpu_custom_call", output_to_operand_aliasing={{1}: (12, {}), {2}: (13, {}), {3}: (14, {}), {4}: (15, {}),... | custom-call | flops 9663676416 | bytes 16777216 | tf_op jit(solution)/shard_map/feed/pallas_call | solution.py:481
  183.4 7.6 %feed_grad.2.refs_0_ = bf16[1024,2304]{1,0:T(8,128)(2,1)} custom-call(bf16[2048,1024]{1,0:T(8,128)(2,1)} %get-tuple-element.170.first_ref.refs_4_, bf16[2048,768]{1,0:T(8,128)(2,1)} %get-tuple-element.183.second_ref), custom_call_target="tpu_custom_call" | custom-call | flops 6442450944 | bytes 8388608 | tf_op jit(solution)/shard_map/feed_grad/pallas_call | solution.py:594
  198.5 11.4 %feed_grad.3 = bf16[1024,2304]{1,0:T(8,128)(2,1)} custom-call(bf16[2048,1024]{1,0:T(8,128)(2,1)} %get-tuple-element.181.first_ref, bf16[2048,1536]{1,0:T(8,128)(2,1)} %get-tuple-element.182.second_ref, bf16[1024,2304]{1,0:T(8,128)(2,1)} %feed_grad.2.refs_0_), custom_call_target="tpu_custom_call", output_to_operand_aliasing={{}: (2, {})} | custom-call | flops 12884901888 | bytes 8388608 | tf_op jit(solution)/shard_map/feed_grad/pallas_call | solution.py:594
  209.8 12.8 %collective-permute-done.20.refs_2_ = bf16[1024,512]{1,0:T(8,128)(2,1)} collective-permute-done((bf16[1024,512]{1,0:T(8,128)(2,1)S(1)}, bf16[1024,512]{1,0:T(8,128)(2,1)}, u32[]{:S(2)}, u32[]{:S(2)}) %collective-permute-start.20) | collective-permute-done | bytes 1048608 | tf_op jit(solution)/shard_map/ppermute | solution.py:665
  223.1 4.0 %collective-permute-done.23.refs_3_ = bf16[1024,512]{1,0:T(8,128)(2,1)} collective-permute-done((bf16[1024,512]{1,0:T(8,128)(2,1)}, bf16[1024,512]{1,0:T(8,128)(2,1)}, u32[]{:S(2)}, u32[]{:S(2)}) %collective-permute-start.23) | collective-permute-done | bytes 1048608 | tf_op jit(solution)/shard_map/ppermute | solution.py:665
  228.4 18.7 %back.2 = (bf16[1024,512]{1,0:T(8,128)(2,1)}, bf16[1024,512]{1,0:T(8,128)(2,1)}, f32[256,128]{1,0:T(8,128)}, bf16[256,128]{1,0:T(8,128)(2,1)}, f32[32,1024]{1,0:...) custom-call(s32[7]{0:T(128)} %concatenate.12.meta, ...), custom_call_target="tpu_custom_call" | custom-call | flops 12884901888 | bytes 16777216 | tf_op jit(solution)/shard_map/back/pallas_call | solution.py:481
  248.1 18.6 %back.3 = (bf16[1024,512]{1,0:T(8,128)(2,1)}, bf16[1024,512]{1,0:T(8,128)(2,1)}, f32[256,128]{1,0:T(8,128)}, bf16[256,128]{1,0:T(8,128)(2,1)}, f32[32,1024]{1,0:...) custom-call(s32[7]{0:T(128)} %concatenate.12.meta, ...), custom_call_target="tpu_custom_call", output_to_operand_aliasing={{5}: (24, {}), {6}: (25, {}), {7}: (26, {})} | custom-call | flops 12884901888 | bytes 16777216 | tf_op jit(solution)/shard_map/back/pallas_call | solution.py:481
  266.7 9.7 %attn_grad.1 = (bf16[4,128,1024]{2,1,0:T(8,128)(2,1)}, bf16[4,128,1024]{2,1,0:T(8,128)(2,1)}) custom-call(s32[1]{0:T(128)} %bitcast.21.row_ref, bf16[2048,1024]{1,0:T(8,128)(2,1)} %get-tuple-element.173.refs_8_.xn_ref, bf16[2048,1024]{1,0:T(8,128)(2,1)} %get-tuple-element.195.dres_ref, bf16[2048,896]{1,0:T(8,128)(2,1)} %get-tuple-element.196.dall_ref, ...), custom_call_target="tpu_custom_call" | custom-call | flops 8589934592 | bytes 8388608 | tf_op jit(solution)/shard_map/attn_grad/pallas_call | solution.py:617
  280.4 3.1 multiply_reduce_fusion
  284.0 24.0 %collective-permute-done.30 = bf16[4,128,1024]{2,1,0:T(8,128)(2,1)S(1)} collective-permute-done((bf16[4,128,1024]{2,1,0:T(8,128)(2,1)}, bf16[4,128,1024]{2,1,0:T(8,128)(2,1)S(1)}, u32[]{:S(2)}, u32[]{:S(2)}) %collective-permute-start.30) | collective-permute-done | bytes 1048608 | tf_op jit(solution)/shard_map/ppermute | solution.py:665
  312.7 3.1 add_convert_fusion.1
  324.8 7.7 %collective-permute-done.41 = f32[32,1024]{1,0:T(8,128)S(1)} collective-permute-done((f32[32,1024]{1,0:T(8,128)S(1)}, f32[32,1024]{1,0:T(8,128)S(1)}, u32[]{:S(2)}, u32[]{:S(2)}) %collective-permute-start.41) | collective-permute-done | bytes 131104 | tf_op jit(solution)/shard_map/ppermute | solution.py:665
  336.4 10.5 %collective-permute-done.42 = f32[32,1024]{1,0:T(8,128)S(1)} collective-permute-done((f32[32,1024]{1,0:T(8,128)S(1)}, f32[32,1024]{1,0:T(8,128)S(1)}, u32[]{:S(2)}, u32[]{:S(2)}) %collective-permute-start.42) | collective-permute-done | bytes 131104 | tf_op jit(solution)/shard_map/ppermute | solution.py:665
  347.5 4.4 %collective-permute-done.32 = bf16[128,1024]{1,0:T(8,128)(2,1)S(1)} collective-permute-done((bf16[128,1024]{1,0:T(8,128)(2,1)S(1)}, bf16[128,1024]{1,0:T(8,128)(2,1)S(1)}, u32[]{:S(2)}, u32[]{:S(2)}) %collective-permute-start.32) | collective-permute-done | bytes 262176 | tf_op jit(solution)/shard_map/ppermute | solution.py:665
  366.7 3.5 collective-permute-done.36
  371.8 3.0 multiply_add_fusion
  378.7 6.5 %update.1 = (f32[2,128,128]{2,1,0:T(8,128)}, f32[2,128,256]{2,1,0:T(8,128)}, f32[256,128]{1,0:T(8,128)}, f32[2,704,128]{2,1,0:T(8,128)}, f32[704,128]{1,0:T(8,12...) custom-call(f32[1]{0:T(128)} %bitcast.31.clip_ref, ...), custom_call_target="tpu_custom_call" | custom-call | tf_op jit(solution)/shard_map/update/pallas_call | solution.py:646
  (195 shorter events, 88.6 us)
Async XLA Ops:
  7.2 122.1 %all-gather.2.cloned.1.call-start = ((), (), s32[]{:S(2)}) async-start(), calls=%async_computation.1 | async-start | bytes 5308416 | tf_op jit(solution)/shard_map/all_gather | solution.py:793
  9.9 13.1 %collective-permute-start.1 = (bf16[128,1152]{1,0:T(8,128)(2,1)}, bf16[128,1152]{1,0:T(8,128)(2,1)S(1)}, u32[]{:S(2)}, u32[]{:S(2)}) collective-permute-start(bf16[128,1152]{1,0:T(8,128)(2,1)} %get-tuple-element.127.refs_0_), channel_id=1, source_target_pairs={{0,8},{4,12},{8,16},{12,20},{16,24},{20,28},{24,0},{28,4},{1,9},{5... | collective-permute-start | bytes 884744 | tf_op jit(solution)/shard_map/ppermute | solution.py:682
  12.9 15.0 %collective-permute-start.2 = (bf16[128,1152]{1,0:T(8,128)(2,1)}, bf16[128,1152]{1,0:T(8,128)(2,1)S(1)}, u32[]{:S(2)}, u32[]{:S(2)}) collective-permute-start(bf16[128,1152]{1,0:T(8,128)(2,1)} %get-tuple-element.127.refs_0_), channel_id=1, source_target_pairs={{0,24},{4,28},{8,0},{12,4},{16,8},{20,12},{24,16},{28,20},{1,25},{... | collective-permute-start | bytes 884744 | tf_op jit(solution)/shard_map/ppermute | solution.py:682
  14.9 13.0 %collective-permute-start.3 = (bf16[128,1152]{1,0:T(8,128)(2,1)}, bf16[128,1152]{1,0:T(8,128)(2,1)S(1)}, u32[]{:S(2)}, u32[]{:S(2)}) collective-permute-start(bf16[128,1152]{1,0:T(8,128)(2,1)} %get-tuple-element.127.refs_0_), channel_id=1, source_target_pairs={{0,4},{4,0},{8,12},{12,8},{16,20},{20,16},{24,28},{28,24},{1,5},{5... | collective-permute-start | bytes 884744 | tf_op jit(solution)/shard_map/ppermute | solution.py:665
  27.9 15.8 %collective-permute-start.4 = (bf16[128,1152]{1,0:T(8,128)(2,1)}, bf16[128,1152]{1,0:T(8,128)(2,1)S(1)}, u32[]{:S(2)}, u32[]{:S(2)}) collective-permute-start(bf16[128,1152]{1,0:T(8,128)(2,1)} %get-tuple-element.127.refs_0_), channel_id=1, source_target_pairs={{0,16},{4,20},{8,24},{12,28},{16,0},{20,4},{24,8},{28,12},{1,17},{... | collective-permute-start | bytes 884744 | tf_op jit(solution)/shard_map/ppermute | solution.py:682
  29.3 14.4 %collective-permute-start.6 = (bf16[128,1152]{1,0:T(8,128)(2,1)S(1)}, bf16[128,1152]{1,0:T(8,128)(2,1)S(1)}, u32[]{:S(2)}, u32[]{:S(2)}) collective-permute-start(bf16[128,1152]{1,0:T(8,128)(2,1)S(1)} %collective-permute-done.2.refs_2_), channel_id=1, source_target_pairs={{0,4},{4,0},{8,12},{12,8},{16,20},{20,16},{24,28},{28,24},{1,5},{5... | collective-permute-start | bytes 884744 | tf_op jit(solution)/shard_map/ppermute | solution.py:665
  30.8 12.9 %collective-permute-start.5 = (bf16[128,1152]{1,0:T(8,128)(2,1)S(1)}, bf16[128,1152]{1,0:T(8,128)(2,1)S(1)}, u32[]{:S(2)}, u32[]{:S(2)}) collective-permute-start(bf16[128,1152]{1,0:T(8,128)(2,1)S(1)} %collective-permute-done.1.refs_1_), channel_id=1, source_target_pairs={{0,4},{4,0},{8,12},{12,8},{16,20},{20,16},{24,28},{28,24},{1,5},{5... | collective-permute-start | bytes 884744 | tf_op jit(solution)/shard_map/ppermute | solution.py:665
  45.2 308.3 %reduce-scatter.2.cloned.1.call-start = ((), (), s32[]{:S(2)}) async-start(), calls=%async_computation.2 | async-start | bytes 5308416 | tf_op jit(solution)/shard_map/reduce_scatter | solution.py:833
  45.3 23.9 %collective-permute-start = (bf16[2048,256]{1,0:T(8,128)(2,1)S(1)}, bf16[2048,256]{1,0:T(8,128)(2,1)S(1)}, u32[]{:S(2)}, u32[]{:S(2)}) collective-permute-start(bf16[2048,256]{1,0:T(8,128)(2,1)S(1)} %copy-done.4), channel_id=1, source_target_pairs={{0,2},{1,3},{2,0},{3,1},{4,6},{5,7},{6,4},{7,5},{8,10},{9,11},{10,... | collective-permute-start | bytes 3145736 | tf_op jit(solution)/shard_map/ppermute | solution.py:665
  48.8 9.5 %collective-permute-start.7 = (bf16[128,1152]{1,0:T(8,128)(2,1)S(1)}, bf16[128,1152]{1,0:T(8,128)(2,1)S(1)}, u32[]{:S(2)}, u32[]{:S(2)}) collective-permute-start(bf16[128,1152]{1,0:T(8,128)(2,1)S(1)} %collective-permute-done.4.refs_4_), channel_id=1, source_target_pairs={{0,4},{4,0},{8,12},{12,8},{16,20},{20,16},{24,28},{28,24},{1,5},{5... | collective-permute-start | bytes 884744 | tf_op jit(solution)/shard_map/ppermute | solution.py:665
  88.8 25.3 %collective-permute-start.9 = (bf16[1024,512]{1,0:T(8,128)(2,1)S(1)}, bf16[1024,512]{1,0:T(8,128)(2,1)S(1)}, u32[]{:S(2)}, u32[]{:S(2)}) collective-permute-start(bf16[1024,512]{1,0:T(8,128)(2,1)S(1)} %add_convert_fusion.5), channel_id=1, source_target_pairs={{0,2},{1,3},{2,0},{3,1},{4,6},{5,7},{6,4},{7,5},{8,10},{9,11},{10,... | collective-permute-start | bytes 3145736 | tf_op jit(solution)/shard_map/ppermute | solution.py:665
  115.1 7.3 %collective-permute-start.10 = (bf16[1024,1024]{1,0:T(8,128)(2,1)}, bf16[1024,1024]{1,0:T(8,128)(2,1)S(1)}, u32[]{:S(2)}, u32[]{:S(2)}) collective-permute-start(bf16[1024,1024]{1,0:T(8,128)(2,1)} %get-tuple-element.146.refs_1_), channel_id=1, source_target_pairs={{0,1},{1,0},{2,3},{3,2},{4,5},{5,4},{6,7},{7,6},{8,9},{9,8},{10,11... | collective-permute-start | bytes 6291464 | tf_op jit(solution)/shard_map/ppermute | solution.py:665
  115.1 12.2 %collective-permute-start.12 = (bf16[2048,256]{1,0:T(8,128)(2,1)S(1)}, bf16[2048,256]{1,0:T(8,128)(2,1)S(1)}, u32[]{:S(2)}, u32[]{:S(2)}) collective-permute-start(bf16[2048,256]{1,0:T(8,128)(2,1)S(1)} %copy-done.4), channel_id=1, source_target_pairs={{0,1},{1,0},{2,3},{3,2},{4,5},{5,4},{6,7},{7,6},{8,9},{9,8},{10,11... | collective-permute-start | bytes 3145736 | tf_op jit(solution)/shard_map/ppermute | solution.py:665
  115.6 12.7 %collective-permute-start.13 = (bf16[2048,256]{1,0:T(8,128)(2,1)}, bf16[2048,256]{1,0:T(8,128)(2,1)S(1)}, u32[]{:S(2)}, u32[]{:S(2)}) collective-permute-start(bf16[2048,256]{1,0:T(8,128)(2,1)} %copy-done.5), channel_id=1, source_target_pairs={{0,1},{1,0},{2,3},{3,2},{4,5},{5,4},{6,7},{7,6},{8,9},{9,8},{10,11... | collective-permute-start | bytes 3145736 | tf_op jit(solution)/shard_map/ppermute | solution.py:665
  115.6 13.7 %collective-permute-start.11 = (bf16[1024,512]{1,0:T(8,128)(2,1)}, bf16[1024,512]{1,0:T(8,128)(2,1)}, u32[]{:S(2)}, u32[]{:S(2)}) collective-permute-start(bf16[1024,512]{1,0:T(8,128)(2,1)} %copy-done.32), channel_id=1, source_target_pairs={{0,1},{1,0},{2,3},{3,2},{4,5},{5,4},{6,7},{7,6},{8,9},{9,8},{10,11... | collective-permute-start | bytes 3145736 | tf_op jit(solution)/shard_map/ppermute | solution.py:665
  125.8 25.5 %collective-permute-start.14 = (bf16[1024,512]{1,0:T(8,128)(2,1)}, bf16[1024,512]{1,0:T(8,128)(2,1)}, u32[]{:S(2)}, u32[]{:S(2)}) collective-permute-start(bf16[1024,512]{1,0:T(8,128)(2,1)} %add_convert_fusion.4), channel_id=1, source_target_pairs={{0,2},{1,3},{2,0},{3,1},{4,6},{5,7},{6,4},{7,5},{8,10},{9,11},{10,... | collective-permute-start | bytes 3145736 | tf_op jit(solution)/shard_map/ppermute | solution.py:665
  151.3 8.3 %collective-permute-start.16 = (bf16[1024,512]{1,0:T(8,128)(2,1)}, bf16[1024,512]{1,0:T(8,128)(2,1)S(1)}, u32[]{:S(2)}, u32[]{:S(2)}) collective-permute-start(bf16[1024,512]{1,0:T(8,128)(2,1)} %collective-permute-done.14.refs_3_), channel_id=1, source_target_pairs={{0,1},{1,0},{2,3},{3,2},{4,5},{5,4},{6,7},{7,6},{8,9},{9,8},{10,11... | collective-permute-start | bytes 3145736 | tf_op jit(solution)/shard_map/ppermute | solution.py:665
  158.0 25.4 %collective-permute-start.18 = (bf16[1024,512]{1,0:T(8,128)(2,1)S(1)}, bf16[1024,512]{1,0:T(8,128)(2,1)}, u32[]{:S(2)}, u32[]{:S(2)}) collective-permute-start(bf16[1024,512]{1,0:T(8,128)(2,1)S(1)} %add_convert_fusion.3), channel_id=1, source_target_pairs={{0,2},{1,3},{2,0},{3,1},{4,6},{5,7},{6,4},{7,5},{8,10},{9,11},{10,... | collective-permute-start | bytes 3145736 | tf_op jit(solution)/shard_map/ppermute | solution.py:665
  180.9 10.1 %collective-permute-start.17 = (bf16[2048,512]{1,0:T(8,128)(2,1)}, bf16[2048,512]{1,0:T(8,128)(2,1)S(1)}, u32[]{:S(2)}, u32[]{:S(2)}) collective-permute-start(bf16[2048,512]{1,0:T(8,128)(2,1)} %get-tuple-element.166), channel_id=1, source_target_pairs={{0,1},{1,0},{2,3},{3,2},{4,5},{5,4},{6,7},{7,6},{8,9},{9,8},{10,11... | collective-permute-start | bytes 6291464 | tf_op jit(solution)/shard_map/ppermute | solution.py:665
  183.4 11.9 %collective-permute-start.19 = (bf16[1024,1024]{1,0:T(8,128)(2,1)}, bf16[1024,1024]{1,0:T(8,128)(2,1)}, u32[]{:S(2)}, u32[]{:S(2)}) collective-permute-start(bf16[1024,1024]{1,0:T(8,128)(2,1)} %get-tuple-element.168.refs_0_), channel_id=1, source_target_pairs={{0,1},{1,0},{2,3},{3,2},{4,5},{5,4},{6,7},{7,6},{8,9},{9,8},{10,11... | collective-permute-start | bytes 6291464 | tf_op jit(solution)/shard_map/ppermute | solution.py:665
  196.9 25.7 %collective-permute-start.20 = (bf16[1024,512]{1,0:T(8,128)(2,1)S(1)}, bf16[1024,512]{1,0:T(8,128)(2,1)}, u32[]{:S(2)}, u32[]{:S(2)}) collective-permute-start(bf16[1024,512]{1,0:T(8,128)(2,1)S(1)} %add_convert_fusion.2), channel_id=1, source_target_pairs={{0,2},{1,3},{2,0},{3,1},{4,6},{5,7},{6,4},{7,5},{8,10},{9,11},{10,... | collective-permute-start | bytes 3145736 | tf_op jit(solution)/shard_map/ppermute | solution.py:665
  222.6 24.5 %collective-permute-start.22 = (bf16[1024,512]{1,0:T(8,128)(2,1)}, bf16[1024,512]{1,0:T(8,128)(2,1)S(1)}, u32[]{:S(2)}, u32[]{:S(2)}) collective-permute-start(bf16[1024,512]{1,0:T(8,128)(2,1)} %collective-permute-done.18.refs_2_), channel_id=1, source_target_pairs={{0,1},{1,0},{2,3},{3,2},{4,5},{5,4},{6,7},{7,6},{8,9},{9,8},{10,11... | collective-permute-start | bytes 3145736 | tf_op jit(solution)/shard_map/ppermute | solution.py:665
  276.4 31.6 %collective-permute-start.30 = (bf16[4,128,1024]{2,1,0:T(8,128)(2,1)}, bf16[4,128,1024]{2,1,0:T(8,128)(2,1)S(1)}, u32[]{:S(2)}, u32[]{:S(2)}) collective-permute-start(bf16[4,128,1024]{2,1,0:T(8,128)(2,1)} %get-tuple-element.205), channel_id=1, source_target_pairs={{0,4},{4,0},{8,12},{12,8},{16,20},{20,16},{24,28},{28,24},{1,5},{5... | collective-permute-start | bytes 3145736 | tf_op jit(solution)/shard_map/ppermute | solution.py:665
  278.9 33.8 %collective-permute-start.21 = (bf16[2048,256]{1,0:T(8,128)(2,1)}, bf16[2048,256]{1,0:T(8,128)(2,1)S(1)}, u32[]{:S(2)}, u32[]{:S(2)}) collective-permute-start(bf16[2048,256]{1,0:T(8,128)(2,1)} %slice.98), channel_id=1, source_target_pairs={{0,2},{1,3},{2,0},{3,1},{4,6},{5,7},{6,4},{7,5},{8,10},{9,11},{10,... | collective-permute-start | bytes 3145736 | tf_op jit(solution)/shard_map/ppermute | solution.py:665
  283.5 39.7 %collective-permute-start.24 = (bf16[1024,512]{1,0:T(8,128)(2,1)}, bf16[1024,512]{1,0:T(8,128)(2,1)}, u32[]{:S(2)}, u32[]{:S(2)}) collective-permute-start(bf16[1024,512]{1,0:T(8,128)(2,1)} %get-tuple-element.199), channel_id=1, source_target_pairs={{0,1},{1,0},{2,3},{3,2},{4,5},{5,4},{6,7},{7,6},{8,9},{9,8},{10,11... | collective-permute-start | bytes 3145736 | tf_op jit(solution)/shard_map/ppermute | solution.py:665
  283.6 34.8 %collective-permute-start.25 = (bf16[1024,512]{1,0:T(8,128)(2,1)}, bf16[1024,512]{1,0:T(8,128)(2,1)}, u32[]{:S(2)}, u32[]{:S(2)}) collective-permute-start(bf16[1024,512]{1,0:T(8,128)(2,1)} %get-tuple-element.202), channel_id=1, source_target_pairs={{0,1},{1,0},{2,3},{3,2},{4,5},{5,4},{6,7},{7,6},{8,9},{9,8},{10,11... | collective-permute-start | bytes 3145736 | tf_op jit(solution)/shard_map/ppermute | solution.py:665
  315.9 18.4 %collective-permute-start.31 = (bf16[2,128,1024]{2,1,0:T(8,128)(2,1)S(1)}, bf16[2,128,1024]{2,1,0:T(8,128)(2,1)S(1)}, u32[]{:S(2)}, u32[]{:S(2)}) collective-permute-start(bf16[2,128,1024]{2,1,0:T(8,128)(2,1)S(1)} %fusion), channel_id=1, source_target_pairs={{0,8},{4,12},{8,0},{12,4},{16,24},{20,28},{24,16},{28,20},{1,9},{5... | collective-permute-start | bytes 1572872 | tf_op jit(solution)/shard_map/ppermute | solution.py:665
  320.0 15.7 %collective-permute-start.26 = (bf16[1024,256]{1,0:T(8,128)(2,1)S(1)}, bf16[1024,256]{1,0:T(8,128)(2,1)S(1)}, u32[]{:S(2)}, u32[]{:S(2)}) collective-permute-start(bf16[1024,256]{1,0:T(8,128)(2,1)S(1)} %slice.123), channel_id=1, source_target_pairs={{0,2},{1,3},{2,0},{3,1},{4,6},{5,7},{6,4},{7,5},{8,10},{9,11},{10,... | collective-permute-start | bytes 1572872 | tf_op jit(solution)/shard_map/ppermute | solution.py:665
  321.8 10.6 %collective-permute-start.41 = (f32[32,1024]{1,0:T(8,128)S(1)}, f32[32,1024]{1,0:T(8,128)S(1)}, u32[]{:S(2)}, u32[]{:S(2)}) collective-permute-start(f32[32,1024]{1,0:T(8,128)S(1)} %add.244), channel_id=1, source_target_pairs={{0,8},{4,12},{8,0},{12,4},{16,24},{20,28},{24,16},{28,20},{1,9},{5... | collective-permute-start | bytes 393224 | tf_op jit(solution)/shard_map/ppermute | solution.py:665
  332.5 14.4 %collective-permute-start.42 = (f32[32,1024]{1,0:T(8,128)S(1)}, f32[32,1024]{1,0:T(8,128)S(1)}, u32[]{:S(2)}, u32[]{:S(2)}) collective-permute-start(f32[32,1024]{1,0:T(8,128)S(1)} %add.245), channel_id=1, source_target_pairs={{0,16},{4,20},{8,24},{12,28},{16,0},{20,4},{24,8},{28,12},{1,17},{... | collective-permute-start | bytes 393224 | tf_op jit(solution)/shard_map/ppermute | solution.py:665
  334.5 17.4 %collective-permute-start.32 = (bf16[128,1024]{1,0:T(8,128)(2,1)S(1)}, bf16[128,1024]{1,0:T(8,128)(2,1)S(1)}, u32[]{:S(2)}, u32[]{:S(2)}) collective-permute-start(bf16[128,1024]{1,0:T(8,128)(2,1)S(1)} %fusion.1), channel_id=1, source_target_pairs={{0,16},{4,20},{8,24},{12,28},{16,0},{20,4},{24,8},{28,12},{1,17},{... | collective-permute-start | bytes 786440 | tf_op jit(solution)/shard_map/ppermute | solution.py:665
  335.7 17.6 %collective-permute-start.27 = (bf16[1024,256]{1,0:T(8,128)(2,1)S(1)}, bf16[1024,256]{1,0:T(8,128)(2,1)S(1)}, u32[]{:S(2)}, u32[]{:S(2)}) collective-permute-start(bf16[1024,256]{1,0:T(8,128)(2,1)S(1)} %slice.124), channel_id=1, source_target_pairs={{0,2},{1,3},{2,0},{3,1},{4,6},{5,7},{6,4},{7,5},{8,10},{9,11},{10,... | collective-permute-start | bytes 1572872 | tf_op jit(solution)/shard_map/ppermute | solution.py:665
  (48 other events, 467.3 us)
Sparse Core Ops, SparseCore 0:
  45.4 79.5 all-gather.1
  210.0 99.8 reduce-scatter.1
where the time goes:
time: 394 us; the launch traced here: 393 us
  Pallas kernels  143 us (36%)
  waiting for transfers between devices  140 us (36%)
  starting transfers between devices  40.5 us (10%)
  other arithmetic  35.5 us (9%)
  between operations  18.4 us (5%)
  local copies, waits for them, and re-layouts  16.1 us (4%)
    ppermute x40, waiting for transfers between devices, swap(): lax.ppermute(array, axis, [(i, i ^ bit) for i in range(lax.axis_size(axis...  116 us
    pallas_call x6, Pallas kernels, run_kernel(): pl.pallas_call(functools.partial(body, len(given)), grid_spec=pltpu.Prefe...  102 us
    ppermute x40, starting transfers between devices, swap(): lax.ppermute(array, axis, [(i, i ^ bit) for i in range(lax.axis_size(axis...  33.9 us
    ppermute x3, waiting for transfers between devices, shift_layer(): lax.ppermute(array, 'dp', [(i, (i + 2 * by) % count) for i in range(count)])  23.6 us
    pallas_call x2, Pallas kernels, feed_grad(): pl.pallas_call(feed_grad_kernel, grid=(D // SLAB,), in_specs=[pl.BlockSpe...  18.9 us
    pallas_call x1, Pallas kernels, attn_grad(): pl.pallas_call(attn_grad_kernel, grid_spec=pltpu.PrefetchScalarGridSpec(n...  9.69 us
    convert_element_type x4, other arithmetic, sum_terms(): (part[:, :2 * SLAB].astype(F32) + core[:, 2 * SLAB:].astype(F32)).astype(...  9.68 us
    unnamed x70, local copies, waits for them, and re-layouts  8.55 us
  transfers between devices with their start and end apart: 45, of which 24 were waited for; matrix products, arithmetic and copies ran while one was open for 9% of the time, Pallas kernels for 34%

commit v1 on v0

--- a/solution.py
+++ b/solution.py
@@ -36,8 +36,10 @@
 BLOCK = 256
 PIECES = 2
 ORDER = (0, 2, 1, 3)
+QKV = 512
+QKVL = 640
+ATTN = 896
 MAIN = 768
-ATTN = 896
 FEED_COLS = 3 * 768
 OUT_SCALE = DK**-0.5
 VMEM_LIMIT = 60 * 1024 * 1024
@@ -131,10 +133,10 @@
     attn_ref[:, :DK] = qk_ref[0].astype(BF16)
     attn_ref[:, DK : 2 * DK] = qk_ref[1].astype(BF16)
     attn_ref[:, 2 * DK : 2 * DK + DV] = vg_ref[0].astype(BF16)
-    attn_ref[:, 2 * DK + DV : MAIN] = vg_ref[1].astype(BF16)
-    attn_ref[:, MAIN:ATTN] = tn(lowin_ref[...].astype(BF16), one_hot(RANK, 0)).astype(BF16)
+    attn_ref[:, QKV:QKVL] = tn(lowin_ref[...].astype(BF16), one_hot(RANK, 0)).astype(BF16)
     lowout = lowout_ref[...].astype(BF16)
-    attn_ref[:RANK, MAIN:ATTN] += nn(lowout, one_hot(lowout.shape[1], RANK)).astype(BF16)
+    attn_ref[:RANK, QKV:QKVL] += nn(lowout, one_hot(lowout.shape[1], RANK)).astype(BF16)
+    attn_ref[:, QKVL:ATTN] = vg_ref[1].astype(BF16)
     attn_ref[:, ATTN:] = mixout_ref[...].T.astype(BF16)
     rows = feed_ref.shape[0]
     pad = jnp.zeros((rows, width - units), BF16)
@@ -161,7 +163,7 @@
         col = lax.broadcasted_iota(jnp.int32, (LANES, DK), 1)
         inside = (row >= RANK) & (row < RANK + keys)
         move = jnp.where(inside & (col - row == block * keys - RANK), 1.0, 0.0).astype(BF16)
-        wb_ref[:RANK, :] += nn(piece[:RANK, MAIN:ATTN], move).astype(BF16)
+        wb_ref[:RANK, :] += nn(piece[:RANK, QKV:QKVL], move).astype(BF16)
 
 
 def attend_kernel(first_block, n_saved, meta, *refs):
@@ -175,17 +177,17 @@
     def _():
         state_out_ref[...] = state_ref[...]
 
-    ends = [meta[SLABS + i] for i in range(meta.shape[0] - SLABS)]
+    ends = [meta[META_ENDS + i] for i in range(meta.shape[0] - META_ENDS)]
     x = x_ref[...].astype(F32)
     scale = lax.rsqrt(jnp.mean(x * x, axis=-1, keepdims=True) + NORM_EPS)
     normed = (x * scale * g1_ref[...]).astype(BF16)
     xn_ref[...] = normed
     proj = nn(normed, w_ref[...])
-    qkv = proj[:, : 2 * DK + DV].astype(BF16)
+    qkv = proj[:, :QKV].astype(BF16)
     qkv_ref[...] = qkv
-    gout = proj[:, 2 * DK + DV : MAIN]
+    gout = proj[:, QKVL:]
     gout_ref[...] = gout
-    lowr = proj[:, MAIN:].astype(BF16)
+    lowr = proj[:, QKV:QKVL].astype(BF16)
     lowr_ref[...] = lowr
     zeta = nn(lowr, wb_ref[...]) + c_ref[...]
     zeta_ref[...] = zeta
@@ -217,26 +219,29 @@
         part_ref[:, j * SLAB : (j + 1) * SLAB] = nt(z, wo_ref[slab_at(meta, j), :]).astype(BF16)
 
 
-def summed(mine, core, far, far_core, j):
+def summed(j, mine, core, *beyond):
     other = (j + 2) % SLABS
     total = mine[:, j * SLAB : (j + 1) * SLAB].astype(F32)
     total = total + core[:, other * SLAB : (other + 1) * SLAB].astype(F32)
-    beyond = far if j < 2 else far_core
     k = 1 - j % 2
-    return total + beyond[:, k * SLAB : (k + 1) * SLAB].astype(F32)
-
-
-def feed_kernel(n_saved, meta, *refs):
-    x_ref, terms, dys = refs[0], refs[1:5], refs[5:9]
-    wf_ref, g2_ref = refs[9:11]
-    refs = refs[11 + n_saved :]
+    if len(beyond) == 2:
+        far = beyond[j // 2][:, k * SLAB : (k + 1) * SLAB]
+    else:
+        far = beyond[2 * (j // 2) + k][...]
+    return total + far.astype(F32)
+
+
+def feed_kernel(n_terms, n_saved, meta, *refs):
+    x_ref, terms, refs = refs[0], refs[1 : 1 + n_terms], refs[1 + n_terms :]
+    dys, wf_ref, g2_ref = refs[:SLABS], refs[SLABS], refs[SLABS + 1]
+    refs = refs[SLABS + 2 + n_saved :]
     part_ref = refs[0]
     feed_keep_ref, feed_send_ref, hn_ref, dy_ref, hidden_ref, dgu_ref, rhat_ref, rs_ref, resid_ref = refs[1:]
     width = hidden_ref.shape[1]
     resid = []
     total = 0.0
     for j in range(SLABS):
-        part = x_ref[:, slab_at(meta, j)].astype(F32) + summed(*terms, j)
+        part = x_ref[:, slab_at(meta, j)].astype(F32) + summed(j, *terms)
         resid.append(part)
         total = total + jnp.sum(part * part, axis=-1, keepdims=True)
     resid_ref[...] = resid[0]
@@ -273,6 +278,9 @@
         target[:, (j % 2) * SLAB : (j % 2 + 1) * SLAB] = fed
 
 
+META_TOKENS = SLABS
+META_ENDS = SLABS + 1
+
 LOWIN_ROW = 0
 IN_ROW = 16
 MID_ROW = 17
@@ -281,29 +289,23 @@
 SUM_ROWS = 32
 
 
-def back_kernel(last_block, n_saved, meta, *refs):
+def turn_kernel(first_block, n_saved, meta, *refs):
     terms = refs[:4]
-    dy_ref, rhat_ref, rs_ref, x_ref, xn_ref = refs[4:9]
-    qkv_ref, gout_ref, lowr_ref, zeta_ref, mixed_ref, states_ref = refs[9:15]
-    w_ref, wo_ref, wb_ref, g2_ref, go_ref = refs[15:20]
-    dstate_ref, next_ref, sums_ref = refs[20:23]
-    refs = refs[23 + n_saved :]
-    keep_ref, send_ref, dstate_out_ref, next_out_ref, sums_out_ref = refs[:5]
-    dres16_ref, dres_ref, dall_ref = refs[5:]
+    dy_ref, rhat_ref, rs_ref, gout_ref, mixed_ref = refs[4:9]
+    wo_ref, g2_ref, go_ref, sums_ref = refs[9:13]
+    refs = refs[13 + n_saved :]
+    sums_out_ref, dres16_ref, dres_ref, dgout_ref, dmix_ref = refs
     step = pl.program_id(0)
 
     @pl.when(step == 0)
     def _():
-        dstate_out_ref[...] = dstate_ref[...]
-        next_out_ref[...] = next_ref[...]
         sums_out_ref[...] = sums_ref[...]
 
-    ends = [meta[SLABS + i] for i in range(meta.shape[0] - SLABS)]
-    base = (last_block - step) * BLOCK
+    base = (first_block + step) * BLOCK
     scaled = []
     dot = 0.0
     for j in range(SLABS):
-        dhn = summed(*terms, j)
+        dhn = summed(j, *terms)
         rhat = rhat_ref[:, j * SLAB : (j + 1) * SLAB].astype(F32)
         if j == 0:
             sums_out_ref[MID_ROW : MID_ROW + 1, slab_at(meta, 0)] += jnp.sum(
@@ -325,7 +327,7 @@
         dres16_ref[:, at] = low
         dz = dz + nn(low, wo_ref[at, :])
     where = lax.broadcasted_iota(jnp.int32, (BLOCK, DV), 0) + base
-    u = jnp.where(where < ends[-1], dz, 0.0)
+    u = jnp.where(where < meta[META_TOKENS], dz, 0.0)
     mixed = mixed_ref[...]
     head_scale = lax.rsqrt(jnp.mean(mixed * mixed, axis=-1, keepdims=True) + NORM_EPS)
     hat = mixed * head_scale
@@ -335,15 +337,34 @@
     uhat = u * hat
     go = go_ref[...]
     sums_out_ref[HEAD_ROW : HEAD_ROW + 1, :DV] += jnp.sum(uhat * act, axis=0, keepdims=True)
-    dall_ref[:, 2 * DK + DV : MAIN] = (uhat * go * (sig * (1.0 + gate * (1.0 - sig)))).astype(BF16)
+    dgout_ref[...] = (uhat * go * (sig * (1.0 + gate * (1.0 - sig)))).astype(BF16)
     dhat = u * go * act
     dmix = head_scale * (dhat - hat * jnp.mean(dhat * hat, axis=-1, keepdims=True))
-    dmix = (dmix * OUT_SCALE).astype(BF16)
+    dmix_ref[...] = (dmix * OUT_SCALE).astype(BF16)
+
+
+def back_kernel(last_block, n_saved, meta, *refs):
+    dmix_ref, dgout_ref, x_ref, xn_ref = refs[:4]
+    qkv_ref, lowr_ref, zeta_ref, states_ref = refs[4:8]
+    w_ref, wb_ref = refs[8:10]
+    dstate_ref, next_ref, sums_ref = refs[10:13]
+    refs = refs[13 + n_saved :]
+    keep_ref, send_ref, dstate_out_ref, next_out_ref, sums_out_ref, dall_ref = refs
+    step = pl.program_id(0)
+
+    @pl.when(step == 0)
+    def _():
+        dstate_out_ref[...] = dstate_ref[...]
+        next_out_ref[...] = next_ref[...]
+        sums_out_ref[...] = sums_ref[...]
+
+    ends = [meta[META_ENDS + i] for i in range(meta.shape[0] - META_ENDS)]
+    base = (last_block - step) * BLOCK
     zeta = zeta_ref[...]
     forget = log_sigmoid(zeta) * (1.0 / GATE_NORM)
     slope = jax.nn.sigmoid(-zeta) * (1.0 / GATE_NORM)
     dstate = dstate_out_ref[...]
-    after = next_out_ref[...]
+    after_state = next_out_ref[...]
     head_at = meta[0] * DK
     for i in reversed(range(BLOCK // CHUNK)):
         rows = slice(i * CHUNK, (i + 1) * CHUNK)
@@ -357,7 +378,7 @@
         grow, shrink, edge, from_start, to_end, decay_step = factors
         q_near, k_near, q_far, k_far, q_state, k_state = parts
         state = states_ref[i * DV : (i + 1) * DV, :]
-        do = dmix[rows]
+        do = dmix_ref[rows, :]
         dstate_low = dstate.astype(BF16)
         dscores = nt(do, values)
         dnear = jnp.where(near, dscores, 0.0).astype(BF16)
@@ -369,8 +390,8 @@
         dk = dk + jnp.where(row < SPAN, tn(dfar, q_far) * edge, 0.0)
         dall_ref[rows, :DK] = dq.astype(BF16)
         dall_ref[rows, DK : 2 * DK] = dk.astype(BF16)
-        dall_ref[rows, 2 * DK : 2 * DK + DV] = dv.astype(BF16)
-        at_end = jnp.sum(dstate * after.astype(F32), axis=0, keepdims=True)
+        dall_ref[rows, 2 * DK : QKV] = dv.astype(BF16)
+        at_end = jnp.sum(dstate * after_state.astype(F32), axis=0, keepdims=True)
         ddecay = queries * dq - keys * dk
         dforget = prefix_sums(ddecay, jnp.where(col >= row, 1.0, 0.0).astype(BF16)) + at_end
         dzeta = (dforget * slope[rows]).astype(BF16)
@@ -380,13 +401,13 @@
         dlowout = tn(lowr_ref[rows, :], dzeta)
         for k in range(2):
             sums_out_ref[LOWOUT_ROW:, lanes_at(k * (D // 2) + head_at)] += dlowout[k * 8 : (k + 1) * 8]
-        dall_ref[rows, MAIN:] = nt(dzeta, wb_ref[...]).astype(BF16)
+        dall_ref[rows, QKV:] = nt(dzeta, wb_ref[...]).astype(BF16)
         dstate = dstate * decay_step + tn(do, q_state)
-        after = state
+        after_state = state
     dstate_out_ref[...] = dstate
-    next_out_ref[...] = after
-    dall = dall_ref[...]
-    sums_out_ref[LOWIN_ROW : LOWIN_ROW + RANK, :] += tn(dall[:, MAIN:], xn_ref[...])[:RANK]
+    next_out_ref[...] = after_state
+    dall = jnp.concatenate([dall_ref[...], dgout_ref[...]], axis=1)
+    sums_out_ref[LOWIN_ROW : LOWIN_ROW + RANK, :] += tn(dall[:, QKV:QKVL], xn_ref[...])[:RANK]
     x = x_ref[...].astype(F32)
     in_scale = lax.rsqrt(jnp.mean(x * x, axis=-1, keepdims=True) + NORM_EPS)
     for j in range(SLABS):
@@ -403,19 +424,37 @@
     refs[-1][...] = tn(first_ref[...], second_ref[...]).astype(BF16)
 
 
-def attn_grad_kernel(row_ref, xn_ref, dres_ref, dall_ref, z_ref, here_ref, away_ref, both_ref):
-    both_ref[:, :MAIN] = tn(xn_ref[...], dall_ref[:, :MAIN])
-    both_ref[:, MAIN:] = tn(dres_ref[...], z_ref[...])
+def attn_grad_kernel(row_ref, *refs):
+    here_ref, away_ref, both_ref = refs[-3:]
+    start = 0
+    for first_ref, second_ref in zip(refs[:-3:2], refs[1:-3:2]):
+        stop = start + min(second_ref.shape[1], QKV)
+        both_ref[:, start:stop] = tn(first_ref[...], second_ref[:, : stop - start])
+        start = stop
     rows = here_ref.shape[1]
     row = row_ref[0]
     here_ref[0] = both_ref[pl.ds(pl.multiple_of(row * rows, rows), rows), :].astype(BF16)
     away_ref[0] = both_ref[pl.ds(pl.multiple_of((1 - row) * rows, rows), rows), :].astype(BF16)
 
 
+def squares_kernel(*refs):
+    feed_ref, attn_ref, squares_ref = refs[-3:]
+    feed = feed_ref[...].astype(F32)
+    total = jnp.sum(jnp.sum(feed * feed, axis=1, keepdims=True), axis=0, keepdims=True)
+    start = 0
+    for kept_ref, came_ref in zip(refs[:-3:2], refs[1:-3:2]):
+        attn = kept_ref[...] + came_ref[...].astype(F32)
+        attn_ref[:, start : start + attn.shape[1]] = attn
+        start += attn.shape[1]
+        total = total + jnp.sum(jnp.sum(attn * attn, axis=1, keepdims=True), axis=0, keepdims=True)
+    squares_ref[...] = jnp.broadcast_to(total, squares_ref.shape)
+
+
 def update_kernel(clip_ref, attn_ref, feed_ref, *refs):
     masters, firsts, seconds = refs[:5], refs[5:10], refs[10:15]
     outs, turned, turned_attn = refs[15:30], refs[30], refs[31]
     step = pl.program_id(0)
+    width = feed_ref.shape[1] // 3
 
     @pl.when(step == 0)
     def _():
@@ -423,7 +462,6 @@
         turned_attn[...] = attn_ref[:, MAIN:].T
 
     clip = clip_ref[0]
-    width = feed_ref.shape[1] // 3
 
     def rows(count):
         if count == attn_ref.shape[0]:
@@ -438,7 +476,7 @@
     across = masters[2].shape[0]
     grads = (
         (attn[:, :DK], attn[:, DK : 2 * DK]),
-        (attn[:, 2 * DK : 2 * DK + DV], attn[:, 2 * DK + DV : MAIN]),
+        (attn[:, 2 * DK : QKV], attn[:, QKV:MAIN]),
         (turned_attn[pl.ds(pl.multiple_of(step * across, 8), across), :],),
         (units(0), units(1)),
         (units(2),),
@@ -489,7 +527,7 @@
         out_shape=list(outs) + list(saved_like),
         input_output_aliases=aliases,
         compiler_params=params(),
-        cost_estimate=pl.CostEstimate(flops=flops, bytes_accessed=16 * 1024 * 1024, transcendentals=0),
+        cost_estimate=pl.CostEstimate(flops=flops, bytes_accessed=1024, transcendentals=0),
         name=name,
     )(meta, *ins, *given)
     return list(result[: len(outs)]), list(result[len(outs) :])
@@ -536,7 +574,7 @@
     in_specs = (
         [rows_at(BLOCK, D, here)]
         + [rows_at(BLOCK, a.shape[1], lambda i: i) for a in terms]
-        + [rows_at(BLOCK, SLAB, here)] * SLABS
+        + [rows_at(BLOCK, SLAB, here), rows_at(BLOCK, SLAB, lambda i: i)] * 2
         + [whole(wf), whole(g2)]
     )
     outs = [like((size, D), BF16)]
@@ -555,36 +593,53 @@
     saved_like = [like((tokens, n), d) for n, d in widths]
     saved_specs = [rows_at(BLOCK, n, here) for n, _ in widths]
     return run_kernel(
-        feed_kernel,
+        functools.partial(feed_kernel, len(terms)),
         meta, steps, ins, in_specs, saved, outs, out_specs, saved_like, saved_specs,
         "feed", size * 2 * D * width * 6,
     )
 
 
-def back(piece, meta, terms, dy, rhat, rs, x, xn, kept, w, wo, wb, g2, go, carried, saved):
-    tokens = x.shape[0]
+def turn_back(piece, meta, terms, rows_in, wo, g2, go, sums, saved):
+    tokens = rows_in[0].shape[0]
+    size = tokens // PIECES
+    steps = size // BLOCK
+    first = piece * steps
+    here = lambda i: first + i
+    ins = [*terms, *rows_in, wo, g2, go, sums]
+    in_specs = (
+        [rows_at(BLOCK, a.shape[1], lambda i: i) for a in terms]
+        + [rows_at(BLOCK, a.shape[1], here) for a in rows_in]
+        + [whole(a) for a in (wo, g2, go, sums)]
+    )
+    widths = [(D, BF16), (SLAB, F32), (DV, BF16), (DV, BF16)]
+    return run_kernel(
+        functools.partial(turn_kernel, first),
+        meta, steps, ins, in_specs, saved, [like(sums.shape, F32)], [fixed(sums.shape)],
+        [like((tokens, n), d) for n, d in widths], [rows_at(BLOCK, n, here) for n, _ in widths],
+        "turn", int(0.01 * size * 4 * D * 1024),
+    )
+
+
+def back(piece, meta, rows_in, states, w, wb, carried, saved):
+    tokens = rows_in[0].shape[0]
     size = tokens // PIECES
     steps = size // BLOCK
     last = (piece + 1) * steps - 1
     here = lambda i: last - i
     local = lambda i: steps - 1 - i
-    ins = [*terms, dy, rhat, rs, x, xn, *kept, w, wo, wb, g2, go, *carried]
+    ins = [*rows_in, states, w, wb, *carried]
     in_specs = (
-        [rows_at(BLOCK, a.shape[1], local) for a in terms]
-        + [rows_at(BLOCK, a.shape[1], here) for a in (dy, rhat, rs, x, xn)]
-        + [rows_at(BLOCK, a.shape[1], here) for a in kept[:-1]]
+        [rows_at(BLOCK, a.shape[1], here) for a in rows_in]
         + [rows_at(BLOCK // CHUNK * DV, DK, here)]
-        + [whole(a) for a in (w, wo, wb, g2, go, *carried)]
+        + [whole(a) for a in (w, wb, *carried)]
     )
     outs = [like((size, 2 * SLAB), BF16)] * 2 + [like(a.shape, a.dtype) for a in carried]
     out_specs = [rows_at(BLOCK, 2 * SLAB, local)] * 2 + [fixed(a.shape) for a in carried]
-    widths = [(D, BF16), (SLAB, F32), (ATTN, BF16)]
-    saved_like = [like((tokens, n), d) for n, d in widths]
-    saved_specs = [rows_at(BLOCK, n, here) for n, _ in widths]
     return run_kernel(
         functools.partial(back_kernel, last),
-        meta, steps, ins, in_specs, saved, outs, out_specs, saved_like, saved_specs,
-        "back", size * 12 * D * 1024,
+        meta, steps, ins, in_specs, saved, outs, out_specs,
+        [like((tokens, QKVL), BF16)], [rows_at(BLOCK, QKVL, here)],
+        "back", int(0.7 * size * 12 * D * 1024),
     )
 
 
@@ -604,32 +659,45 @@
         input_output_aliases={2: 0} if len(ins) > 2 else {},
         compiler_params=params(),
         cost_estimate=pl.CostEstimate(
-            flops=4 * D * tokens * width, bytes_accessed=8 * 1024 * 1024, transcendentals=0
+            flops=int(1 * 4 * D * tokens * width), bytes_accessed=1024, transcendentals=0
         ),
         name="feed_grad",
     )(*ins)
 
 
-def attn_grad(row, xn, dres16, dall, z):
-    tokens = xn.shape[0]
+def attn_grad(row, *pairs):
+    tokens = pairs[0].shape[0]
     half = SLAB // 2
-    column = lambda i, row: (0, i)
+    width = sum(min(a.shape[1], QKV) for a in pairs[1::2])
+    specs = [
+        whole(a) if i % 2 else pl.BlockSpec((tokens, SLAB), lambda i, row: (0, i)) for i, a in enumerate(pairs)
+    ]
     return pl.pallas_call(
         attn_grad_kernel,
         grid_spec=pltpu.PrefetchScalarGridSpec(
             num_scalar_prefetch=1,
             grid=(SLABS,),
-            in_specs=[pl.BlockSpec((tokens, SLAB), column)] * 2 + [whole(dall), whole(z)],
-            out_specs=[pl.BlockSpec((1, half, D), lambda i, row: (i, 0, 0))] * 2,
-            scratch_shapes=[pltpu.VMEM((SLAB, D), F32)],
+            in_specs=specs,
+            out_specs=[pl.BlockSpec((1, half, width), lambda i, row: (i, 0, 0))] * 2,
+            scratch_shapes=[pltpu.VMEM((SLAB, width), F32)],
         ),
-        out_shape=[like((SLABS, half, D), BF16)] * 2,
+        out_shape=[like((SLABS, half, width), BF16)] * 2,
         compiler_params=params(),
         cost_estimate=pl.CostEstimate(
-            flops=4 * D * tokens * D, bytes_accessed=8 * 1024 * 1024, transcendentals=0
+            flops=int(0.5 * 4 * D * tokens * width), bytes_accessed=1024, transcendentals=0
         ),
         name="attn_grad",
-    )(row, xn, dres16, dall, z)
+    )(row, *pairs)
+
+
+def shard_squares(*parts):
+    rows = parts[0].shape[0]
+    return pl.pallas_call(
+        squares_kernel,
+        out_shape=(like((rows, D), F32), like((8, LANES), F32)),
+        compiler_params=params(),
+        name="squares",
+    )(*parts)
 
 
 def update(clip, attn, feed, arrays):
@@ -651,7 +719,7 @@
         + [cut(a) for a in arrays],
         out_specs=[cut(a) for a in masters] * 3,
         out_shape=[like(a.shape, F32) for a in masters] * 3,
-        scratch_shapes=[pltpu.VMEM((feed.shape[1], rows), F32), pltpu.VMEM((DV, rows), F32)],
+        scratch_shapes=[pltpu.VMEM((FEED_COLS, rows), F32), pltpu.VMEM((DV, rows), F32)],
         compiler_params=params(),
         name="update",
     )(clip, attn, feed, *arrays)
@@ -682,7 +750,7 @@
     return lax.ppermute(array, "dp", [(i, (i + 2 * by) % count) for i in range(count)])
 
 
-def gather_attn(own):
+def gather_attn(own, earlier):
     dp_at = lax.axis_index("dp")
     found = {(0, 0): own, (1, 0): shift_layer(own, 1), (3, 0): shift_layer(own, 3), (0, 1): swap_row(own)}
     first = list(found.values())[1:]
@@ -690,11 +758,11 @@
     for k in (1, 3):
         found[k, 1] = swap_row(after(found[k, 0], *first))
     second = [found[2, 0], found[1, 1], found[3, 1]]
-    found[2, 1] = swap_row(after(*second))
+    found[2, 1] = swap_row(after(*second, earlier))
     places = [((dp_at - 2 * k) % (2 * SLABS)) ^ h for k, h in found]
     pieces = list(found.values())
     rows = D
-    return second, pl.pallas_call(
+    return first, pl.pallas_call(
         assemble_kernel,
         in_specs=[pl.BlockSpec(memory_space=pltpu.SMEM)]
         + [pl.BlockSpec(memory_space=pltpu.VMEM)] * (2 * SLABS),
@@ -704,35 +772,44 @@
     )(jnp.stack(places).astype(jnp.int32), *pieces)
 
 
-def gather_plain(own):
+def gather_plain(own, earlier):
     count, rows = lax.axis_size("dp"), own.shape[0]
     full = lax.all_gather(own, "dp", axis=0, tiled=True)
     keys = DK // count
-    blocks = full.reshape(count, rows, -1)[:, :RANK, MAIN + RANK : MAIN + RANK + keys]
+    blocks = full.reshape(count, rows, -1)[:, :RANK, QKV + RANK : QKV + RANK + keys]
     wb = jnp.pad(blocks.transpose(1, 0, 2).reshape(RANK, DK), ((0, LANES - RANK), (0, 0)))
     return [own], (full[:, :ATTN], full[:, ATTN:], wb)
 
 
-def scatter_attn(here, away):
-    dp_at = lax.axis_index("dp")
-    high, low = dp_at // 4, (dp_at // 2) % 2
-    rows, width = here.shape[1:]
-
-    def pick(array, axis, index):
-        return lax.dynamic_index_in_dim(array, index, axis, keepdims=False)
-
-    first = here.astype(F32) + swap_row(away).astype(F32)
-    here = first.reshape(2, 2, rows, width)
-    away = pick(here, 1, 1 - low).astype(BF16)
-    here = pick(here, 1, low) + swap(away, "dp", 2).astype(F32)
-    away = pick(here, 0, 1 - high).astype(BF16)
-    return first, pick(here, 0, high) + swap(away, "dp", 4).astype(F32)
-
-
-def sum_terms(part, earlier):
-    core = swap_core(after(part, *earlier))
-    own = (part[:, : 2 * SLAB].astype(F32) + core[:, 2 * SLAB :].astype(F32)).astype(BF16)
-    return own, part, core, swap_far(own)
+def pick(array, axis, index):
+    return lax.dynamic_index_in_dim(array, index, axis, keepdims=False)
+
+
+def scatter_rows(here, away, *earlier):
+    came = after(swap_row(away), *earlier)
+    return (here.astype(F32) + came.astype(F32)).reshape(2, 2, *here.shape[1:])
+
+
+def scatter_near(total, low, *earlier):
+    away = pick(total, 1, 1 - low).astype(BF16)
+    return pick(total, 1, low) + after(swap(away, "dp", 2), *earlier).astype(F32)
+
+
+def scatter_far(total, high, *earlier):
+    away = pick(total, 0, 1 - high).astype(BF16)
+    return pick(total, 0, high), after(swap(away, "dp", 4), *earlier)
+
+
+def sum_terms(part, earlier, beside=(), before=(), halves=False):
+    core = after(swap_core(after(part, *earlier)), *beside)
+    own = []
+    for start, stop in ((0, SLAB), (SLAB, 2 * SLAB)) if halves else ((0, 2 * SLAB),):
+        beside = core[:, 2 * SLAB + start : 2 * SLAB + stop].astype(F32)
+        own.append((part[:, start:stop].astype(F32) + beside).astype(BF16))
+    far = [swap_far(after(own[0], *before))]
+    if halves:
+        far.append(swap_far(after(own[1], far[0])))
+    return own, part, core, far
 
 
 def slab_sum(keep, send, earlier):
@@ -749,6 +826,11 @@
             array = array + swap(array, axis, bit)
             bit *= 2
     return array
+
+
+def add_rounded(array, axis, bit, *earlier):
+    low = after(array.astype(BF16), *earlier)
+    return low.astype(F32) + swap(low, axis, bit).astype(F32)
 
 
 def adam_step(weight, gradient, first_moment, second_moment, clip_factor, learn_rate, weight_decay):
@@ -778,7 +860,8 @@
     rows_here = weight_qk.shape[1]
     ranks, _, keys_here = weight_lowout.shape
     turn = lambda i, a: jnp.swapaxes(a, 1, 2) if i == 5 else a
-    far_cot = swap_far(cotangent)
+    size = cotangent.shape[0] // PIECES
+    far_cots = [swap_far(cotangent[i * size : (i + 1) * size]) for i in range(PIECES)]
 
     attn_pack, feed_pack = pl.pallas_call(
         pack_kernel,
@@ -789,87 +872,123 @@
         weight_qk, weight_vg, weight_lowin.T, weight_lowout[:, 0, :], weight_mixout,
         turn(5, weight_gateup), weight_down,
     )
-    arrived, (w, wo, wb) = (gather_attn if layered else gather_plain)(attn_pack)
+    arrived, (w, wo, wb) = (gather_attn if layered else gather_plain)(attn_pack, far_cots[0])
     wf = lax.all_gather(after(feed_pack, *arrived), "dp", axis=0, tiled=True)
     doc_ends = jnp.cumsum(doc_lengths[0])
     slots = jnp.stack([tensor_at ^ o for o in ORDER])
-    meta = jnp.concatenate([slots.astype(jnp.int32), doc_ends.astype(jnp.int32)])
+    meta = jnp.concatenate([slots.astype(jnp.int32), doc_ends[-1:].astype(jnp.int32), doc_ends.astype(jnp.int32)])
 
     g1, g2 = weight_small[:D].reshape(1, D), weight_small[D : 2 * D].reshape(1, D)
     go = weight_small[2 * D : 2 * D + DV].reshape(1, DV)
     gate_bias = lax.dynamic_slice_in_dim(weight_small, 2 * D + DV + tensor_at * DK, DK).reshape(1, DK)
     x = inputs
-    meta = after(meta, far_cot)
-    dys = [cotangent, far_cot, swap_core(after(cotangent, w)), swap_core(after(far_cot, w))]
+    x_wide = x.astype(F32)
+    in_scale = lax.rsqrt(jnp.mean(x_wide * x_wide, axis=-1, keepdims=True) + NORM_EPS)
+    meta, _, in_scale = lax.optimization_barrier((meta, far_cots[-1], in_scale))
+    core_cot = swap_core(after(cotangent, w))
+    dys = [(cotangent, far, core_cot, swap_core(after(far, w))) for far in far_cots]
 
     state = jnp.zeros((DV, DK), F32)
     saved = None
     terms = []
-    earlier = []
+    earlier = before = []
     for piece in range(PIECES):
         (part, state), saved = attend(piece, meta, x, w, wo, wb, g1, go, gate_bias, state, saved)
-        own, part, core, far = sum_terms(part, earlier)
-        terms.append((part, core, far, swap_core(far)))
-        earlier = [far]
-        state = after(state, own)
+        own, part, core, far = sum_terms(part, earlier, before=before, halves=piece < PIECES - 1)
+        terms.append((part, core, far))
+        earlier = far[:1]
+        before = far[-1:]
+        state = after(state, *own)
     xn, *kept = saved
     z = kept.pop(5)
+    terms = [(part, core, *far, *(swap_core(after(f, *own)) for f in far)) for part, core, far in terms]
 
     fed = None
     back_terms = []
-    order = after(meta, own)
+    order = after(meta, *own)
     for piece in range(PIECES):
-        (part,), fed = feed(piece, order, x, terms[piece], dys, wf, g2, fed)
-        own, part, core, far = sum_terms(part, earlier)
+        (part,), fed = feed(piece, order, x, terms[piece], dys[piece], wf, g2, fed)
+        beside = []
+        if piece == PIECES - 1:
+            feed_keep, feed_send, hn, dy, hidden, dgu, rhat, rs, resid = fed
+            grad_feed = feed_grad(dy, hidden, 2, None)
+            beside = [grad_feed]
+        own, part, core, far = sum_terms(part, earlier, beside)
+        (own,), (far,) = own, far
         earlier = [far]
         order = after(meta, own)
         if piece < PIECES - 1:
             back_terms.append((part, core, far, swap_core(far)))
-    feed_keep, feed_send, hn, dy, hidden, dgu, rhat, rs, resid = fed
-    fed_own = (feed_keep.astype(F32) + swap_core(feed_send).astype(F32)).astype(BF16)
-    grad_feed = feed_grad(dy, hidden, 2, None)
-    grad_feed = feed_grad(after(hn, own, fed_own), dgu, 0, grad_feed)
-    back_terms.append((part, core, far, swap_core(after(far, grad_feed))))
+    grad_feed = feed_grad(after(hn, own), dgu, 0, grad_feed)
+    fed_own = (feed_keep.astype(F32) + swap_core(after(feed_send, own)).astype(F32)).astype(BF16)
     shard_feed = lax.psum_scatter(grad_feed, "dp", scatter_dimension=0, tiled=True)
+
+    qkv, gout, lowr, zeta, mixed, states = kept
+    turned = None
+    sums = jnp.zeros((SUM_ROWS, D), F32)
+    order = after(meta, grad_feed, fed_own)
+    for piece in range(PIECES):
+        if piece == PIECES - 1:
+            back_terms.append((part, core, far, swap_core(after(far, sums))))
+        (sums,), turned = turn_back(
+            piece, order, back_terms[piece], (dy, rhat, rs, gout, mixed), wo, g2, go, sums, turned
+        )
+    dres16, dres, dgout, dmix = turned
     fed_far = swap_far(after(fed_own[:, SLAB:], far))
-    output = (resid + (fed_own[:, :SLAB].astype(F32) + fed_far.astype(F32))).astype(BF16)
-
-    carried = [jnp.zeros((DV, DK), F32), jnp.zeros((DV, DK), BF16), jnp.zeros((SUM_ROWS, D), F32)]
+    row_at = (dp_at % 2 if layered else jnp.zeros_like(dp_at)).astype(jnp.int32).reshape(1)
+    high, low = dp_at // 4, (dp_at // 2) % 2
+    here, away = attn_grad(row_at, xn, dgout, dres16, z)
+    if layered:
+        early = scatter_rows(here, away)
+        early_layer = scatter_near(early, low)
+        early_parts = scatter_far(early_layer, high)
+
+    carried = [jnp.zeros((DV, DK), F32), jnp.zeros((DV, DK), BF16), sums]
     backed = None
     dxn = []
-    order = after(meta, grad_feed)
+    order = after(meta, away)
     for piece in reversed(range(PIECES)):
         (keep, send, *carried), backed = back(
-            piece, order, back_terms[piece], dy, rhat, rs, x, xn, kept, w, wo, wb, g2, go, carried, backed
+            piece, order, (dmix, dgout, x, xn, qkv, lowr, zeta), states, w, wb, carried, backed
         )
-        if piece == PIECES - 1:
-            order = meta
+        if layered:
+            order = after(meta, early)
         dxn.insert(0, (keep, send))
-    dres16, dres, dall = backed
-    row_at = (dp_at % 2 if layered else jnp.zeros_like(dp_at)).astype(jnp.int32).reshape(1)
-    here, away = attn_grad(row_at, xn, dres16, dall, z)
-    earlier = fed_far
+    (dall,) = backed
+    late_here, late_away = attn_grad(after(row_at, early_layer, fed_far) if layered else row_at, xn, dall)
+    dxn_far = [fed_far]
     for piece in reversed(range(PIECES)):
         keep, send = dxn[piece]
-        dxn[piece], earlier = slab_sum(keep, after(send, here), earlier)
+        dxn[piece], far = slab_sum(keep, after(send, late_here), dxn_far[-1])
+        dxn_far.append(far)
     if layered:
-        half_summed, shard_attn = scatter_attn(here, away)
+        late = scatter_rows(late_here, late_away, early_parts[1], *dxn_far[1:-1])
     else:
-        half_summed = here
-        shard_attn = lax.psum_scatter(
-            jnp.stack([here, away], axis=1).reshape(D, D), "dp", scatter_dimension=0, tiled=True
+        late = late_here
+    fed_sum = fed_own[:, :SLAB].astype(F32) + after(fed_far, late).astype(F32)
+    output = (resid + fed_sum).astype(BF16)
+    if layered:
+        late_layer = scatter_near(late, low, output)
+        parts = *scatter_far(late_layer, high, dxn_far[-1]), *early_parts
+    else:
+        late_layer = late_here
+        grads = [jnp.stack(g, axis=1).reshape(D, -1) for g in ((late_here, late_away), (here, away))]
+        kept = lax.psum_scatter(
+            jnp.concatenate(grads, axis=1), "dp", scatter_dimension=0, tiled=True
         ).astype(F32)
+        parts = kept, jnp.zeros(kept.shape, BF16)
 
     dxn = jnp.concatenate(dxn, axis=0)
-    x_wide = x.astype(F32)
-    in_scale = lax.rsqrt(jnp.mean(x_wide * x_wide, axis=-1, keepdims=True) + NORM_EPS)
     hat_here = lax.dynamic_slice_in_dim(x, tensor_at * SLAB, SLAB, 1).astype(F32) * in_scale
     scaled = dxn * lax.dynamic_slice_in_dim(g1, tensor_at * SLAB, SLAB, 1)
     row_sums = jnp.sum(scaled * hat_here, axis=-1).reshape(-1, LANES)
     row_mean = sum_everywhere(row_sums, ("tensor",)).reshape(-1, 1) / D
     input_grad = dres + in_scale * (scaled - hat_here * row_mean)
 
-    wide = sum_everywhere(after(carried[2], half_summed))
+    wide = add_rounded(carried[2], "tensor", 1, late_here)
+    wide = add_rounded(wide, "tensor", 2)
+    for bit in (1 << i for i in range(lax.axis_size("dp").bit_length() - 1)):
+        wide = add_rounded(wide, "dp", bit, late if bit == 1 else late_layer)
     small_grad = jnp.concatenate([wide[IN_ROW], wide[MID_ROW], wide[HEAD_ROW, : DV + HEADS * DK]])
     grad_lowin = lax.dynamic_slice(wide, (LOWIN_ROW, dp_at * rows_here), (RANK, rows_here)).T
     lowout = jnp.concatenate([wide[LOWOUT_ROW:, : D // 2], wide[LOWOUT_ROW:, D // 2 :]], axis=0)
@@ -877,8 +996,8 @@
         lowout, (0, tensor_at * DK + dp_at * keys_here), (RANK, keys_here)
     ).reshape(weight_lowout.shape)
 
-    squares = sum(jnp.sum(jnp.square(s.astype(F32))) for s in (shard_feed, shard_attn))
-    square_total = sum_everywhere(jnp.broadcast_to(squares, (8, LANES)))[0, 0]
+    shard_attn, squares = shard_squares(*parts, shard_feed)
+    square_total = sum_everywhere(squares)[0, 0]
     grad_norm = jnp.sqrt(square_total + jnp.sum(wide * wide))
     clip_factor = jnp.minimum(1.0, CLIP_NORM / (grad_norm + 1e-06))
     arrays = [turn(i, group[i]) for group in (masters, firsts, seconds) for i in LARGE]

time: 394 us -> 366 us (0.929)
  waiting for transfers between devices: 140 us -> 90.8 us
  Pallas kernels: 143 us -> 161 us
    ppermute x40 -> x47, waiting for transfers between devices: 116 us -> 63.5 us  [swap(): lax.ppermute(array, axis, [(i, i ^ bit) for i in range(lax.axis_size(axis...]
    pallas_call x6 -> x8, Pallas kernels: 102 us -> 113 us  [run_kernel(): pl.pallas_call(functools.partial(body, len(given)), grid_spec=pltpu.Prefe...]
    pallas_call x1 -> x2, Pallas kernels: 9.69 us -> 14 us  [attn_grad(): pl.pallas_call(attn_grad_kernel, grid_spec=pltpu.PrefetchScalarGridSpec(n...]
    reduce_sum x3 -> x0, other arithmetic: 4.08 us -> none  [the longest x2 3.45 us: body(): jnp.sum(jnp.square(s.astype(F32)))]
    ppermute x40 -> x47, starting transfers between devices: 33.9 us -> 36.3 us  [swap(): lax.ppermute(array, axis, [(i, i ^ bit) for i in range(lax.axis_size(axis...]
    convert_element_type x6 -> x11, other arithmetic: 15.7 us -> 14.6 us  [the longest x4 9.08 us: sum_terms(): own.append((part[:, start:stop].astype(F32) + beside).astype(BF16))]
    unnamed x70 -> x78, local copies, waits for them, and re-layouts: 8.55 us -> 9.57 us
  transfers between devices with their start and end apart: 45 -> 52, of which waited for: 24 -> 24; matrix products, arithmetic and copies ran while one was open for 9% -> 10% of each run, Pallas kernels for 34% -> 42%
where the time goes in v1:
time: 366 us; the launch traced here: 365 us
  Pallas kernels  161 us (44%)
  waiting for transfers between devices  90.8 us (25%)
  starting transfers between devices  42.8 us (12%)
  other arithmetic  32.7 us (9%)
  local copies, waits for them, and re-layouts  19.9 us (5%)
  between operations  17.3 us (5%)
    pallas_call x8, Pallas kernels, run_kernel(): pl.pallas_call(functools.partial(body, len(given)), grid_spec=pltpu.Prefe...  113 us
    ppermute x47, waiting for transfers between devices, swap(): lax.ppermute(array, axis, [(i, i ^ bit) for i in range(lax.axis_size(axis...  63.5 us
    ppermute x47, starting transfers between devices, swap(): lax.ppermute(array, axis, [(i, i ^ bit) for i in range(lax.axis_size(axis...  36.3 us
    ppermute x3, waiting for transfers between devices, shift_layer(): lax.ppermute(array, 'dp', [(i, (i + 2 * by) % count) for i in range(count)])  27.3 us
    pallas_call x2, Pallas kernels, feed_grad(): pl.pallas_call(feed_grad_kernel, grid=(D // SLAB,), in_specs=[pl.BlockSpe...  19.3 us
    pallas_call x2, Pallas kernels, attn_grad(): pl.pallas_call(attn_grad_kernel, grid_spec=pltpu.PrefetchScalarGridSpec(n...  14 us
    unnamed x78, local copies, waits for them, and re-layouts  9.57 us
    convert_element_type x4, other arithmetic, sum_terms(): own.append((part[:, start:stop].astype(F32) + beside).astype(BF16))  9.08 us
  transfers between devices with their start and end apart: 52, of which 24 were waited for; matrix products, arithmetic and copies ran while one was open for 10% of the time, Pallas kernels for 42%

profile of v1, /device:TPU:0, one launch (start us, length us, event | category | flops | bytes accessed | tf_op | source)
XLA Modules:
  0.0 364.8 jit_solution(14999204382462792256)
XLA Ops:
  9.9 3.0 collective-permute-start.1
  16.7 6.4 %collective-permute-done.1.refs_1_ = bf16[128,1152]{1,0:T(8,128)(2,1)S(1)} collective-permute-done((bf16[128,1152]{1,0:T(8,128)(2,1)}, bf16[128,1152]{1,0:T(8,128)(2,1)S(1)}, u32[]{:S(2)}, u32[]{:S(2)}) %collective-permute-start.1) | collective-permute-done | bytes 294944 | tf_op jit(solution)/shard_map/ppermute | solution.py:750
  23.1 4.8 %collective-permute-done.2.refs_2_ = bf16[128,1152]{1,0:T(8,128)(2,1)S(1)} collective-permute-done((bf16[128,1152]{1,0:T(8,128)(2,1)}, bf16[128,1152]{1,0:T(8,128)(2,1)S(1)}, u32[]{:S(2)}, u32[]{:S(2)}) %collective-permute-start.2) | collective-permute-done | bytes 294944 | tf_op jit(solution)/shard_map/ppermute | solution.py:750
  33.5 3.2 multiply_reduce_fusion
  43.1 16.0 %collective-permute-done.4.refs_4_ = bf16[128,1152]{1,0:T(8,128)(2,1)} collective-permute-done((bf16[128,1152]{1,0:T(8,128)(2,1)S(1)}, bf16[128,1152]{1,0:T(8,128)(2,1)}, u32[]{:S(2)}, u32[]{:S(2)}) %collective-permute-start.4) | collective-permute-done | bytes 294944 | tf_op jit(solution)/shard_map/ppermute | solution.py:750
  61.5 4.5 %collective-permute-done.8.refs_7_ = bf16[128,1152]{1,0:T(8,128)(2,1)S(1)} collective-permute-done((bf16[128,1152]{1,0:T(8,128)(2,1)}, bf16[128,1152]{1,0:T(8,128)(2,1)S(1)}, u32[]{:S(2)}, u32[]{:S(2)}) %collective-permute-start.8) | collective-permute-done | bytes 294944 | tf_op jit(solution)/shard_map/ppermute | solution.py:733
  66.8 3.1 assemble.1
  70.6 12.0 %attend.2 = (bf16[1024,1024]{1,0:T(8,128)(2,1)}, f32[256,128]{1,0:T(8,128)}, bf16[2048,1024]{1,0:T(8,128)(2,1)}, bf16[2048,512]{1,0:T(8,128)(2,1)}, f32[2048,256...) custom-call(s32[8]{0:T(128)} %concatenate.12.meta, ...), custom_call_target="tpu_custom_call" | custom-call | flops 8589934592 | bytes 1024 | tf_op jit(solution)/shard_map/attend/pallas_call | solution.py:519
  82.7 4.4 %collective-permute-done.9.refs_2_ = bf16[1024,1024]{1,0:T(8,128)(2,1)S(1)} collective-permute-done((bf16[1024,1024]{1,0:T(8,128)(2,1)}, bf16[1024,1024]{1,0:T(8,128)(2,1)S(1)}, u32[]{:S(2)}, u32[]{:S(2)}) %collective-permute-start.9) | collective-permute-done | bytes 2097184 | tf_op jit(solution)/shard_map/ppermute | solution.py:733
  91.7 11.8 %attend.3 = (bf16[1024,1024]{1,0:T(8,128)(2,1)}, f32[256,128]{1,0:T(8,128)}, bf16[2048,1024]{1,0:T(8,128)(2,1)}, bf16[2048,512]{1,0:T(8,128)(2,1)}, f32[2048,256...) custom-call(s32[8]{0:T(128)} %concatenate.12.meta, ...), custom_call_target="tpu_custom_call", output_to_operand_aliasing={{2}: (9, {}), {3}: (10, {}), {4}: (11, {}), {5}: (12, {}), ... | custom-call | flops 8589934592 | bytes 1024 | tf_op jit(solution)/shard_map/attend/pallas_call | solution.py:519
  109.2 3.3 add_convert_fusion.4
  112.5 6.6 %collective-permute-done.12.refs_4_ = bf16[1024,256]{1,0:T(8,128)(2,1)S(1)} collective-permute-done((bf16[1024,256]{1,0:T(8,128)(2,1)S(1)}, bf16[1024,256]{1,0:T(8,128)(2,1)S(1)}, u32[]{:S(2)}, u32[]{:S(2)}) %collective-permute-start.12) | collective-permute-done | bytes 524320 | tf_op jit(solution)/shard_map/ppermute | solution.py:733
  123.3 20.2 %feed.2 = (bf16[1024,1024]{1,0:T(8,128)(2,1)}, bf16[2048,512]{1,0:T(8,128)(2,1)}, bf16[2048,512]{1,0:T(8,128)(2,1)}, bf16[2048,1024]{1,0:T(8,128)(2,1)}, bf16[20...) custom-call(s32[8]{0:T(128)} %concatenate.12.meta, ...), custom_call_target="tpu_custom_call" | custom-call | flops 9663676416 | bytes 1024 | tf_op jit(solution)/shard_map/feed/pallas_call | solution.py:519
  145.6 3.9 %collective-permute-done.18.refs_1_ = bf16[1024,1024]{1,0:T(8,128)(2,1)S(1)} collective-permute-done((bf16[1024,1024]{1,0:T(8,128)(2,1)}, bf16[1024,1024]{1,0:T(8,128)(2,1)S(1)}, u32[]{:S(2)}, u32[]{:S(2)}) %collective-permute-start.18) | collective-permute-done | bytes 2097184 | tf_op jit(solution)/shard_map/ppermute | solution.py:733
  155.4 20.3 %feed.3 = (bf16[1024,1024]{1,0:T(8,128)(2,1)}, bf16[2048,512]{1,0:T(8,128)(2,1)}, bf16[2048,512]{1,0:T(8,128)(2,1)}, bf16[2048,1024]{1,0:T(8,128)(2,1)}, bf16[20...) custom-call(s32[8]{0:T(128)} %concatenate.12.meta, ...), custom_call_target="tpu_custom_call", output_to_operand_aliasing={{1}: (12, {}), {2}: (13, {}), {3}: (14, {}), {4}: (15, {}),... | custom-call | flops 9663676416 | bytes 1024 | tf_op jit(solution)/shard_map/feed/pallas_call | solution.py:519
  177.8 7.9 %feed_grad.2.refs_0_ = bf16[1024,2304]{1,0:T(8,128)(2,1)} custom-call(bf16[2048,1024]{1,0:T(8,128)(2,1)} %get-tuple-element.204.first_ref.refs_4_, bf16[2048,768]{1,0:T(8,128)(2,1)} %get-tuple-element.205.second_ref), custom_call_target="tpu_custom_call" | custom-call | flops 6442450944 | bytes 1024 | tf_op jit(solution)/shard_map/feed_grad/pallas_call | solution.py:649
  190.6 11.4 %feed_grad.3 = bf16[1024,2304]{1,0:T(8,128)(2,1)} custom-call(bf16[2048,1024]{1,0:T(8,128)(2,1)} %get-tuple-element.211.first_ref, bf16[2048,1536]{1,0:T(8,128)(2,1)} %get-tuple-element.212.second_ref, bf16[1024,2304]{1,0:T(8,128)(2,1)} %feed_grad.2.refs_0_), custom_call_target="tpu_custom_call", output_to_operand_aliasing={{}: (2, {})} | custom-call | flops 12884901888 | bytes 1024 | tf_op jit(solution)/shard_map/feed_grad/pallas_call | solution.py:649
  203.3 2.8 add_convert_fusion
  206.8 9.6 %turn.2 = (f32[32,1024]{1,0:T(8,128)}, bf16[2048,1024]{1,0:T(8,128)(2,1)}, f32[2048,256]{1,0:T(8,128)}, bf16[2048,256]{1,0:T(8,128)(2,1)}, bf16[2048,256]{1,0:T(8,128)(2,1)}) custom-call(s32[8]{0:T(128)} %concatenate.12.meta, bf16[1024,1024]{1,0:T(8,128)(2,1)} %get-tuple-element.186.refs_0_, bf16[1024,1024]{1,0:T(8,128)(2,1)} %copy-done.3, ...), custom_call_target="tpu_custom_call" | custom-call | flops 42949672 | bytes 1024 | tf_op jit(solution)/shard_map/turn/pallas_call | solution.py:519
  219.2 10.1 %turn.3 = (f32[32,1024]{1,0:T(8,128)}, bf16[2048,1024]{1,0:T(8,128)(2,1)}, f32[2048,256]{1,0:T(8,128)}, bf16[2048,256]{1,0:T(8,128)(2,1)}, bf16[2048,256]{1,0:T(8,128)(2,1)}) custom-call(s32[8]{0:T(128)} %concatenate.12.meta, ...), custom_call_target="tpu_custom_call", output_to_operand_aliasing={{1}: (14, {}), {2}: (15, {}), {3}: (16, {}), {4}: (17, {})} | custom-call | flops 42949672 | bytes 1024 | tf_op jit(solution)/shard_map/turn/pallas_call | solution.py:519
  229.4 7.3 %attn_grad.2 = (bf16[4,128,512]{2,1,0:T(8,128)(2,1)}, bf16[4,128,512]{2,1,0:T(8,128)(2,1)}) custom-call(s32[1]{0:T(128)} %bitcast.23.row_ref, bf16[2048,1024]{1,0:T(8,128)(2,1)} %get-tuple-element.209.refs_0_.refs_3_, bf16[2048,256]{1,0:T(8,128)(2,1)} %get-tuple-element.224.refs_1_, bf16[2048,1024]{1,0:T(8,128)(2,1)} %get-tuple-element.225.refs_2_, ...), custom_call_target="tpu_custom_call" | custom-call | flops 2147483648 | bytes 1024 | tf_op jit(solution)/shard_map/attn_grad/pallas_call | solution.py:675
  238.9 14.7 %back.2 = (bf16[1024,512]{1,0:T(8,128)(2,1)}, bf16[1024,512]{1,0:T(8,128)(2,1)}, f32[256,128]{1,0:T(8,128)}, bf16[256,128]{1,0:T(8,128)(2,1)}, f32[32,1024]{1,0:T(8,128)}, /*index=5*/bf16[2048,640]{1,0:T(8,128)(2,1)}) custom-call(s32[8]{0:T(128)} %concatenate.12.meta, bf16[2048,256]{1,0:T(8,128)(2,1)} %get-tuple-element.231.refs_0_, ...), custom_call_target="tpu_custom_call" | custom-call | flops 9019430912 | bytes 1024 | tf_op jit(solution)/shard_map/back/pallas_call | solution.py:519
  258.2 14.7 %back.3 = (bf16[1024,512]{1,0:T(8,128)(2,1)}, bf16[1024,512]{1,0:T(8,128)(2,1)}, f32[256,128]{1,0:T(8,128)}, bf16[256,128]{1,0:T(8,128)(2,1)}, f32[32,1024]{1,0:T(8,128)}, /*index=5*/bf16[2048,640]{1,0:T(8,128)(2,1)}) custom-call(s32[8]{0:T(128)} %concatenate.12.meta, ...), custom_call_target="tpu_custom_call", output_to_operand_aliasing={{5}: (14, {})} | custom-call | flops 9019430912 | bytes 1024 | tf_op jit(solution)/shard_map/back/pallas_call | solution.py:519
  273.8 6.7 %attn_grad.3 = (bf16[4,128,512]{2,1,0:T(8,128)(2,1)}, bf16[4,128,512]{2,1,0:T(8,128)(2,1)}) custom-call(s32[1]{0:T(128)} %bitcast.23.row_ref, bf16[2048,1024]{1,0:T(8,128)(2,1)} %get-tuple-element.209.refs_0_.refs_3_, bf16[2048,640]{1,0:T(8,128)(2,1)} %get-tuple-element.242.refs_1_), custom_call_target="tpu_custom_call" | custom-call | flops 2147483648 | bytes 1024 | tf_op jit(solution)/shard_map/attn_grad/pallas_call | solution.py:675
  291.8 10.1 %collective-permute-done.31.refs_3_ = bf16[128,512]{1,0:T(8,128)(2,1)S(1)} collective-permute-done((bf16[128,512]{1,0:T(8,128)(2,1)S(1)}, bf16[128,512]{1,0:T(8,128)(2,1)S(1)}, u32[]{:S(2)}, u32[]{:S(2)}) %collective-permute-start.31) | collective-permute-done | bytes 131104 | tf_op jit(solution)/shard_map/ppermute | solution.py:733
  306.0 2.6 add_convert_fusion.1
  308.8 3.4 collective-permute-done.38
  313.7 3.5 collective-permute-done.48
  318.1 5.6 %collective-permute-done.49 = bf16[32,1024]{1,0:T(8,128)(2,1)S(1)} collective-permute-done((bf16[32,1024]{1,0:T(8,128)(2,1)S(1)}, bf16[32,1024]{1,0:T(8,128)(2,1)S(1)}, u32[]{:S(2)}, u32[]{:S(2)}) %collective-permute-start.49) | collective-permute-done | bytes 65568 | tf_op jit(solution)/shard_map/ppermute | solution.py:733
  338.3 3.6 collective-permute-done.43
  342.0 3.3 multiply_add_fusion
  350.4 6.5 %update.1 = (f32[2,128,128]{2,1,0:T(8,128)}, f32[2,128,256]{2,1,0:T(8,128)}, f32[256,128]{1,0:T(8,128)}, f32[2,704,128]{2,1,0:T(8,128)}, f32[704,128]{1,0:T(8,12...) custom-call(f32[1]{0:T(128)} %bitcast.39.clip_ref, ...), custom_call_target="tpu_custom_call" | custom-call | tf_op jit(solution)/shard_map/update/pallas_call | solution.py:714
  (227 shorter events, 100.0 us)
Async XLA Ops:
  7.2 116.1 %all-gather.2.cloned.1.call-start = ((), (), s32[]{:S(2)}) async-start(), calls=%async_computation.1 | async-start | bytes 5308416 | tf_op jit(solution)/shard_map/all_gather | solution.py:876
  9.9 13.2 %collective-permute-start.1 = (bf16[128,1152]{1,0:T(8,128)(2,1)}, bf16[128,1152]{1,0:T(8,128)(2,1)S(1)}, u32[]{:S(2)}, u32[]{:S(2)}) collective-permute-start(bf16[128,1152]{1,0:T(8,128)(2,1)} %get-tuple-element.156.refs_0_), channel_id=1, source_target_pairs={{0,8},{4,12},{8,16},{12,20},{16,24},{20,28},{24,0},{28,4},{1,9},{5... | collective-permute-start | bytes 884744 | tf_op jit(solution)/shard_map/ppermute | solution.py:750
  12.9 15.0 %collective-permute-start.2 = (bf16[128,1152]{1,0:T(8,128)(2,1)}, bf16[128,1152]{1,0:T(8,128)(2,1)S(1)}, u32[]{:S(2)}, u32[]{:S(2)}) collective-permute-start(bf16[128,1152]{1,0:T(8,128)(2,1)} %get-tuple-element.156.refs_0_), channel_id=1, source_target_pairs={{0,24},{4,28},{8,0},{12,4},{16,8},{20,12},{24,16},{28,20},{1,25},{... | collective-permute-start | bytes 884744 | tf_op jit(solution)/shard_map/ppermute | solution.py:750
  15.0 12.9 %collective-permute-start.3 = (bf16[128,1152]{1,0:T(8,128)(2,1)}, bf16[128,1152]{1,0:T(8,128)(2,1)S(1)}, u32[]{:S(2)}, u32[]{:S(2)}) collective-permute-start(bf16[128,1152]{1,0:T(8,128)(2,1)} %get-tuple-element.156.refs_0_), channel_id=1, source_target_pairs={{0,4},{4,0},{8,12},{12,8},{16,20},{20,16},{24,28},{28,24},{1,5},{5... | collective-permute-start | bytes 884744 | tf_op jit(solution)/shard_map/ppermute | solution.py:733
  27.9 298.7 %reduce-scatter.2.cloned.1.call-start = ((), (), s32[]{:S(2)}) async-start(), calls=%async_computation.2 | async-start | bytes 5308416 | tf_op jit(solution)/shard_map/reduce_scatter | solution.py:924
  28.1 15.0 %collective-permute-start.7 = (bf16[1024,256]{1,0:T(8,128)(2,1)S(1)}, bf16[1024,256]{1,0:T(8,128)(2,1)}, u32[]{:S(2)}, u32[]{:S(2)}) collective-permute-start(bf16[1024,256]{1,0:T(8,128)(2,1)S(1)} %get-tuple-element.346), channel_id=1, source_target_pairs={{0,2},{1,3},{2,0},{3,1},{4,6},{5,7},{6,4},{7,5},{8,10},{9,11},{10,... | collective-permute-start | bytes 1572872 | tf_op jit(solution)/shard_map/ppermute | solution.py:733
  29.6 31.9 %collective-permute-start = (bf16[1024,256]{1,0:T(8,128)(2,1)S(1)}, bf16[1024,256]{1,0:T(8,128)(2,1)}, u32[]{:S(2)}, u32[]{:S(2)}) collective-permute-start(bf16[1024,256]{1,0:T(8,128)(2,1)S(1)} %get-tuple-element.347), channel_id=1, source_target_pairs={{0,2},{1,3},{2,0},{3,1},{4,6},{5,7},{6,4},{7,5},{8,10},{9,11},{10,... | collective-permute-start | bytes 1572872 | tf_op jit(solution)/shard_map/ppermute | solution.py:733
  30.2 29.0 %collective-permute-start.4 = (bf16[128,1152]{1,0:T(8,128)(2,1)S(1)}, bf16[128,1152]{1,0:T(8,128)(2,1)}, u32[]{:S(2)}, u32[]{:S(2)}) collective-permute-start(bf16[128,1152]{1,0:T(8,128)(2,1)S(1)} %copy-done.16), channel_id=1, source_target_pairs={{0,16},{4,20},{8,24},{12,28},{16,0},{20,4},{24,8},{28,12},{1,17},{... | collective-permute-start | bytes 884744 | tf_op jit(solution)/shard_map/ppermute | solution.py:750
  31.5 27.7 %collective-permute-start.5 = (bf16[128,1152]{1,0:T(8,128)(2,1)S(1)}, bf16[128,1152]{1,0:T(8,128)(2,1)}, u32[]{:S(2)}, u32[]{:S(2)}) collective-permute-start(bf16[128,1152]{1,0:T(8,128)(2,1)S(1)} %collective-permute-done.1.refs_1_), channel_id=1, source_target_pairs={{0,4},{4,0},{8,12},{12,8},{16,20},{20,16},{24,28},{28,24},{1,5},{5... | collective-permute-start | bytes 884744 | tf_op jit(solution)/shard_map/ppermute | solution.py:733
  33.0 26.1 %collective-permute-start.6 = (bf16[128,1152]{1,0:T(8,128)(2,1)S(1)}, bf16[128,1152]{1,0:T(8,128)(2,1)}, u32[]{:S(2)}, u32[]{:S(2)}) collective-permute-start(bf16[128,1152]{1,0:T(8,128)(2,1)S(1)} %collective-permute-done.2.refs_2_), channel_id=1, source_target_pairs={{0,4},{4,0},{8,12},{12,8},{16,20},{20,16},{24,28},{28,24},{1,5},{5... | collective-permute-start | bytes 884744 | tf_op jit(solution)/shard_map/ppermute | solution.py:733
  89.9 14.0 %collective-permute-start.10 = (bf16[1024,256]{1,0:T(8,128)(2,1)S(1)}, bf16[1024,256]{1,0:T(8,128)(2,1)S(1)}, u32[]{:S(2)}, u32[]{:S(2)}) collective-permute-start(bf16[1024,256]{1,0:T(8,128)(2,1)S(1)} %get-tuple-element.345), channel_id=1, source_target_pairs={{0,2},{1,3},{2,0},{3,1},{4,6},{5,7},{6,4},{7,5},{8,10},{9,11},{10,... | collective-permute-start | bytes 1572872 | tf_op jit(solution)/shard_map/ppermute | solution.py:733
  104.8 14.3 %collective-permute-start.12 = (bf16[1024,256]{1,0:T(8,128)(2,1)S(1)}, bf16[1024,256]{1,0:T(8,128)(2,1)S(1)}, u32[]{:S(2)}, u32[]{:S(2)}) collective-permute-start(bf16[1024,256]{1,0:T(8,128)(2,1)S(1)} %get-tuple-element.177), channel_id=1, source_target_pairs={{0,2},{1,3},{2,0},{3,1},{4,6},{5,7},{6,4},{7,5},{8,10},{9,11},{10,... | collective-permute-start | bytes 1572872 | tf_op jit(solution)/shard_map/ppermute | solution.py:733
  106.5 14.9 %collective-permute-start.15 = (bf16[2048,256]{1,0:T(8,128)(2,1)S(1)}, bf16[2048,256]{1,0:T(8,128)(2,1)S(1)}, u32[]{:S(2)}, u32[]{:S(2)}) collective-permute-start(bf16[2048,256]{1,0:T(8,128)(2,1)S(1)} %copy-done.4), channel_id=1, source_target_pairs={{0,1},{1,0},{2,3},{3,2},{4,5},{5,4},{6,7},{7,6},{8,9},{9,8},{10,11... | collective-permute-start | bytes 3145736 | tf_op jit(solution)/shard_map/ppermute | solution.py:733
  106.7 14.6 %collective-permute-start.16 = (bf16[1024,256]{1,0:T(8,128)(2,1)}, bf16[1024,256]{1,0:T(8,128)(2,1)S(1)}, u32[]{:S(2)}, u32[]{:S(2)}) collective-permute-start(bf16[1024,256]{1,0:T(8,128)(2,1)} %collective-permute-done.7.refs_8_), channel_id=1, source_target_pairs={{0,1},{1,0},{2,3},{3,2},{4,5},{5,4},{6,7},{7,6},{8,9},{9,8},{10,11... | collective-permute-start | bytes 1572872 | tf_op jit(solution)/shard_map/ppermute | solution.py:733
  119.6 25.5 %collective-permute-start.17 = (bf16[1024,512]{1,0:T(8,128)(2,1)}, bf16[1024,512]{1,0:T(8,128)(2,1)}, u32[]{:S(2)}, u32[]{:S(2)}) collective-permute-start(bf16[1024,512]{1,0:T(8,128)(2,1)} %add_convert_fusion.4), channel_id=1, source_target_pairs={{0,2},{1,3},{2,0},{3,1},{4,6},{5,7},{6,4},{7,5},{8,10},{9,11},{10,... | collective-permute-start | bytes 3145736 | tf_op jit(solution)/shard_map/ppermute | solution.py:733
  145.1 9.2 %collective-permute-start.19 = (bf16[1024,512]{1,0:T(8,128)(2,1)}, bf16[1024,512]{1,0:T(8,128)(2,1)S(1)}, u32[]{:S(2)}, u32[]{:S(2)}) collective-permute-start(bf16[1024,512]{1,0:T(8,128)(2,1)} %collective-permute-done.17.refs_3_), channel_id=1, source_target_pairs={{0,1},{1,0},{2,3},{3,2},{4,5},{5,4},{6,7},{7,6},{8,9},{9,8},{10,11... | collective-permute-start | bytes 3145736 | tf_op jit(solution)/shard_map/ppermute | solution.py:733
  145.6 8.6 %collective-permute-start.20 = (bf16[1024,256]{1,0:T(8,128)(2,1)}, bf16[1024,256]{1,0:T(8,128)(2,1)S(1)}, u32[]{:S(2)}, u32[]{:S(2)}) collective-permute-start(bf16[1024,256]{1,0:T(8,128)(2,1)} %collective-permute-done.refs_6_), channel_id=1, source_target_pairs={{0,1},{1,0},{2,3},{3,2},{4,5},{5,4},{6,7},{7,6},{8,9},{9,8},{10,11... | collective-permute-start | bytes 1572872 | tf_op jit(solution)/shard_map/ppermute | solution.py:733
  152.4 25.4 %collective-permute-start.21 = (bf16[1024,512]{1,0:T(8,128)(2,1)S(1)}, bf16[1024,512]{1,0:T(8,128)(2,1)}, u32[]{:S(2)}, u32[]{:S(2)}) collective-permute-start(bf16[1024,512]{1,0:T(8,128)(2,1)S(1)} %add_convert_fusion.3), channel_id=1, source_target_pairs={{0,2},{1,3},{2,0},{3,1},{4,6},{5,7},{6,4},{7,5},{8,10},{9,11},{10,... | collective-permute-start | bytes 3145736 | tf_op jit(solution)/shard_map/ppermute | solution.py:733
  177.8 7.9 %collective-permute-start.22 = (bf16[1024,1024]{1,0:T(8,128)(2,1)}, bf16[1024,1024]{1,0:T(8,128)(2,1)}, u32[]{:S(2)}, u32[]{:S(2)}) collective-permute-start(bf16[1024,1024]{1,0:T(8,128)(2,1)} %get-tuple-element.203.refs_0_), channel_id=1, source_target_pairs={{0,1},{1,0},{2,3},{3,2},{4,5},{5,4},{6,7},{7,6},{8,9},{9,8},{10,11... | collective-permute-start | bytes 6291464 | tf_op jit(solution)/shard_map/ppermute | solution.py:733
  188.3 13.6 %collective-permute-start.23 = (bf16[2048,512]{1,0:T(8,128)(2,1)}, bf16[2048,512]{1,0:T(8,128)(2,1)S(1)}, u32[]{:S(2)}, u32[]{:S(2)}) collective-permute-start(bf16[2048,512]{1,0:T(8,128)(2,1)} %get-tuple-element.207), channel_id=1, source_target_pairs={{0,1},{1,0},{2,3},{3,2},{4,5},{5,4},{6,7},{7,6},{8,9},{9,8},{10,11... | collective-permute-start | bytes 6291464 | tf_op jit(solution)/shard_map/ppermute | solution.py:733
  188.6 17.5 %collective-permute-start.26 = (bf16[1024,512]{1,0:T(8,128)(2,1)}, bf16[1024,512]{1,0:T(8,128)(2,1)}, u32[]{:S(2)}, u32[]{:S(2)}) collective-permute-start(bf16[1024,512]{1,0:T(8,128)(2,1)} %collective-permute-done.21.refs_2_), channel_id=1, source_target_pairs={{0,1},{1,0},{2,3},{3,2},{4,5},{5,4},{6,7},{7,6},{8,9},{9,8},{10,11... | collective-permute-start | bytes 3145736 | tf_op jit(solution)/shard_map/ppermute | solution.py:733
  188.8 27.5 %collective-permute-start.24 = (bf16[1024,512]{1,0:T(8,128)(2,1)}, bf16[1024,512]{1,0:T(8,128)(2,1)S(1)}, u32[]{:S(2)}, u32[]{:S(2)}) collective-permute-start(bf16[1024,512]{1,0:T(8,128)(2,1)} %add_convert_fusion.2), channel_id=1, source_target_pairs={{0,2},{1,3},{2,0},{3,1},{4,6},{5,7},{6,4},{7,5},{8,10},{9,11},{10,... | collective-permute-start | bytes 3145736 | tf_op jit(solution)/shard_map/ppermute | solution.py:733
  217.7 56.1 %collective-permute-start.25 = (bf16[2048,256]{1,0:T(8,128)(2,1)}, bf16[2048,256]{1,0:T(8,128)(2,1)}, u32[]{:S(2)}, u32[]{:S(2)}) collective-permute-start(bf16[2048,256]{1,0:T(8,128)(2,1)} %slice.123), channel_id=1, source_target_pairs={{0,2},{1,3},{2,0},{3,1},{4,6},{5,7},{6,4},{7,5},{8,10},{9,11},{10,... | collective-permute-start | bytes 3145736 | tf_op jit(solution)/shard_map/ppermute | solution.py:733
  236.6 19.5 %collective-permute-start.28 = (bf16[4,128,512]{2,1,0:T(8,128)(2,1)}, bf16[4,128,512]{2,1,0:T(8,128)(2,1)S(1)}, u32[]{:S(2)}, u32[]{:S(2)}) collective-permute-start(bf16[4,128,512]{2,1,0:T(8,128)(2,1)} %get-tuple-element.228), channel_id=1, source_target_pairs={{0,4},{4,0},{8,12},{12,8},{16,20},{20,16},{24,28},{28,24},{1,5},{5... | collective-permute-start | bytes 1572872 | tf_op jit(solution)/shard_map/ppermute | solution.py:733
  258.1 14.8 %collective-permute-start.29 = (bf16[2,128,512]{2,1,0:T(8,128)(2,1)S(1)}, bf16[2,128,512]{2,1,0:T(8,128)(2,1)S(1)}, u32[]{:S(2)}, u32[]{:S(2)}) collective-permute-start(bf16[2,128,512]{2,1,0:T(8,128)(2,1)S(1)} %fusion), channel_id=1, source_target_pairs={{0,8},{4,12},{8,0},{12,4},{16,24},{20,28},{24,16},{28,20},{1,9},{5... | collective-permute-start | bytes 786440 | tf_op jit(solution)/shard_map/ppermute | solution.py:733
  280.5 21.3 %collective-permute-start.34 = (bf16[1024,512]{1,0:T(8,128)(2,1)}, bf16[1024,512]{1,0:T(8,128)(2,1)}, u32[]{:S(2)}, u32[]{:S(2)}) collective-permute-start(bf16[1024,512]{1,0:T(8,128)(2,1)} %get-tuple-element.255), channel_id=1, source_target_pairs={{0,1},{1,0},{2,3},{3,2},{4,5},{5,4},{6,7},{7,6},{8,9},{9,8},{10,11... | collective-permute-start | bytes 3145736 | tf_op jit(solution)/shard_map/ppermute | solution.py:733
  281.9 21.7 %collective-permute-start.30 = (bf16[4,128,512]{2,1,0:T(8,128)(2,1)}, bf16[4,128,512]{2,1,0:T(8,128)(2,1)S(1)}, u32[]{:S(2)}, u32[]{:S(2)}) collective-permute-start(bf16[4,128,512]{2,1,0:T(8,128)(2,1)} %get-tuple-element.244), channel_id=1, source_target_pairs={{0,4},{4,0},{8,12},{12,8},{16,20},{20,16},{24,28},{28,24},{1,5},{5... | collective-permute-start | bytes 1572872 | tf_op jit(solution)/shard_map/ppermute | solution.py:733
  284.2 17.7 %collective-permute-start.31 = (bf16[128,512]{1,0:T(8,128)(2,1)S(1)}, bf16[128,512]{1,0:T(8,128)(2,1)S(1)}, u32[]{:S(2)}, u32[]{:S(2)}) collective-permute-start(bf16[128,512]{1,0:T(8,128)(2,1)S(1)} %fusion.2), channel_id=1, source_target_pairs={{0,16},{4,20},{8,24},{12,28},{16,0},{20,4},{24,8},{28,12},{1,17},{... | collective-permute-start | bytes 393224 | tf_op jit(solution)/shard_map/ppermute | solution.py:733
  289.5 14.1 %collective-permute-start.33 = (bf16[1024,256]{1,0:T(8,128)(2,1)S(1)}, bf16[1024,256]{1,0:T(8,128)(2,1)S(1)}, u32[]{:S(2)}, u32[]{:S(2)}) collective-permute-start(bf16[1024,256]{1,0:T(8,128)(2,1)S(1)} %slice.150), channel_id=1, source_target_pairs={{0,2},{1,3},{2,0},{3,1},{4,6},{5,7},{6,4},{7,5},{8,10},{9,11},{10,... | collective-permute-start | bytes 1572872 | tf_op jit(solution)/shard_map/ppermute | solution.py:733
  303.9 8.4 %collective-permute-start.38 = (bf16[2,128,512]{2,1,0:T(8,128)(2,1)S(1)}, bf16[2,128,512]{2,1,0:T(8,128)(2,1)S(1)}, u32[]{:S(2)}, u32[]{:S(2)}) collective-permute-start(bf16[2,128,512]{2,1,0:T(8,128)(2,1)S(1)} %fusion.1), channel_id=1, source_target_pairs={{0,8},{4,12},{8,0},{12,4},{16,24},{20,28},{24,16},{28,20},{1,9},{5... | collective-permute-start | bytes 786440 | tf_op jit(solution)/shard_map/ppermute | solution.py:733
  304.3 20.1 %collective-permute-start.35 = (bf16[1024,256]{1,0:T(8,128)(2,1)S(1)}, bf16[1024,256]{1,0:T(8,128)(2,1)S(1)}, u32[]{:S(2)}, u32[]{:S(2)}) collective-permute-start(bf16[1024,256]{1,0:T(8,128)(2,1)S(1)} %slice.149), channel_id=1, source_target_pairs={{0,2},{1,3},{2,0},{3,1},{4,6},{5,7},{6,4},{7,5},{8,10},{9,11},{10,... | collective-permute-start | bytes 1572872 | tf_op jit(solution)/shard_map/ppermute | solution.py:733
  312.7 11.6 %collective-permute-start.39 = (bf16[128,512]{1,0:T(8,128)(2,1)S(1)}, bf16[128,512]{1,0:T(8,128)(2,1)S(1)}, u32[]{:S(2)}, u32[]{:S(2)}) collective-permute-start(bf16[128,512]{1,0:T(8,128)(2,1)S(1)} %fusion.3), channel_id=1, source_target_pairs={{0,16},{4,20},{8,24},{12,28},{16,0},{20,4},{24,8},{28,12},{1,17},{... | collective-permute-start | bytes 393224 | tf_op jit(solution)/shard_map/ppermute | solution.py:733
  (59 other events, 369.1 us)
Sparse Core Ops, SparseCore 0:
  28.1 85.1 all-gather.1
  202.1 103.9 reduce-scatter.1

commit v2 on v1

--- a/solution.py
+++ b/solution.py
@@ -167,10 +167,10 @@
 
 
 def attend_kernel(first_block, n_saved, meta, *refs):
-    x_ref, w_ref, wo_ref, wb_ref, g1_ref, go_ref, c_ref, state_ref = refs[:8]
-    refs = refs[8 + n_saved :]
+    xn_ref, w_ref, wo_ref, wb_ref, go_ref, c_ref, state_ref = refs[:7]
+    refs = refs[7 + n_saved :]
     part_ref, state_out_ref = refs[:2]
-    xn_ref, qkv_ref, gout_ref, lowr_ref, zeta_ref, mixed_ref, z_ref, states_ref = refs[2:]
+    qkv_ref, gout_ref, lowr_ref, zeta_ref, mixed_ref, z_ref, states_ref = refs[2:]
     step = pl.program_id(0)
 
     @pl.when(step == 0)
@@ -178,11 +178,7 @@
         state_out_ref[...] = state_ref[...]
 
     ends = [meta[META_ENDS + i] for i in range(meta.shape[0] - META_ENDS)]
-    x = x_ref[...].astype(F32)
-    scale = lax.rsqrt(jnp.mean(x * x, axis=-1, keepdims=True) + NORM_EPS)
-    normed = (x * scale * g1_ref[...]).astype(BF16)
-    xn_ref[...] = normed
-    proj = nn(normed, w_ref[...])
+    proj = nn(xn_ref[...], w_ref[...])
     qkv = proj[:, :QKV].astype(BF16)
     qkv_ref[...] = qkv
     gout = proj[:, QKVL:]
@@ -247,8 +243,6 @@
     resid_ref[...] = resid[0]
     scale = lax.rsqrt(total / D + NORM_EPS)
     rs_ref[...] = jnp.broadcast_to(scale, rs_ref.shape)
-    units = 0.0
-    dhid = 0.0
     for j in range(SLABS):
         at = slab_at(meta, j)
         rhat = resid[j] * scale
@@ -257,8 +251,8 @@
         hn_ref[:, at] = hn
         dy = dys[j][...]
         dy_ref[:, at] = dy
-        units = units + nn(hn, wf_ref[at, : 2 * width])
-        dhid = dhid + nn(dy, wf_ref[at, 2 * width :])
+    units = nn(hn_ref[...], wf_ref[:, : 2 * width])
+    dhid = nn(dy_ref[...], wf_ref[:, 2 * width :])
     gate = units[:, :width]
     up = units[:, width:]
     sig = jax.nn.sigmoid(gate)
@@ -271,7 +265,7 @@
     dgu_ref[:, width:] = dup
     for j in range(SLABS):
         at = slab_at(meta, j)
-        part = nt(dgate, wf_ref[at, :width]) + nt(dup, wf_ref[at, width : 2 * width])
+        part = nt(dgu_ref[...], wf_ref[at, : 2 * width])
         part_ref[:, j * SLAB : (j + 1) * SLAB] = part.astype(BF16)
         fed = nt(hidden, wf_ref[at, 2 * width :]).astype(BF16)
         target = feed_keep_ref if j < 2 else feed_send_ref
@@ -533,18 +527,17 @@
     return list(result[: len(outs)]), list(result[len(outs) :])
 
 
-def attend(piece, meta, x, w, wo, wb, g1, go, c, state, saved):
-    tokens = x.shape[0]
+def attend(piece, meta, xn, w, wo, wb, go, c, state, saved):
+    tokens = xn.shape[0]
     size = tokens // PIECES
     steps = size // BLOCK
     first = piece * steps
     here = lambda i: first + i
-    ins = [x, w, wo, wb, g1, go, c, state]
+    ins = [xn, w, wo, wb, go, c, state]
     in_specs = [rows_at(BLOCK, D, here)] + [whole(a) for a in ins[1:]]
     outs = [like((size, D), BF16), like(state.shape, F32)]
     out_specs = [rows_at(BLOCK, D, lambda i: i), fixed(state.shape)]
     widths = [
-        (D, BF16),
         (2 * DK + DV, BF16),
         (DV, F32),
         (LANES, BF16),
@@ -750,16 +743,17 @@
     return lax.ppermute(array, "dp", [(i, (i + 2 * by) % count) for i in range(count)])
 
 
-def gather_attn(own, earlier):
+def gather_attn(own, soon, later):
     dp_at = lax.axis_index("dp")
     found = {(0, 0): own, (1, 0): shift_layer(own, 1), (3, 0): shift_layer(own, 3), (0, 1): swap_row(own)}
     first = list(found.values())[1:]
-    found[2, 0] = shift_layer(after(own, *first), 2)
+    found[2, 0] = shift_layer(after(own, *first, *soon), 2)
     for k in (1, 3):
         found[k, 1] = swap_row(after(found[k, 0], *first))
     second = [found[2, 0], found[1, 1], found[3, 1]]
-    found[2, 1] = swap_row(after(*second, earlier))
-    places = [((dp_at - 2 * k) % (2 * SLABS)) ^ h for k, h in found]
+    places = jnp.stack([((dp_at - 2 * k) % (2 * SLABS)) ^ h for k, h in [*found, (2, 1)]]).astype(jnp.int32)
+    sent, places, *_ = lax.optimization_barrier((found[2, 0], places, *second[1:], *later))
+    found[2, 1] = swap_row(sent)
     pieces = list(found.values())
     rows = D
     return first, pl.pallas_call(
@@ -769,10 +763,10 @@
         out_shape=(like((rows, ATTN), BF16), like((rows, DV), BF16), like((LANES, DK), BF16)),
         compiler_params=params(),
         name="assemble",
-    )(jnp.stack(places).astype(jnp.int32), *pieces)
-
-
-def gather_plain(own, earlier):
+    )(places, *pieces)
+
+
+def gather_plain(own, soon, later):
     count, rows = lax.axis_size("dp"), own.shape[0]
     full = lax.all_gather(own, "dp", axis=0, tiled=True)
     keys = DK // count
@@ -872,8 +866,6 @@
         weight_qk, weight_vg, weight_lowin.T, weight_lowout[:, 0, :], weight_mixout,
         turn(5, weight_gateup), weight_down,
     )
-    arrived, (w, wo, wb) = (gather_attn if layered else gather_plain)(attn_pack, far_cots[0])
-    wf = lax.all_gather(after(feed_pack, *arrived), "dp", axis=0, tiled=True)
     doc_ends = jnp.cumsum(doc_lengths[0])
     slots = jnp.stack([tensor_at ^ o for o in ORDER])
     meta = jnp.concatenate([slots.astype(jnp.int32), doc_ends[-1:].astype(jnp.int32), doc_ends.astype(jnp.int32)])
@@ -884,7 +876,13 @@
     x = inputs
     x_wide = x.astype(F32)
     in_scale = lax.rsqrt(jnp.mean(x_wide * x_wide, axis=-1, keepdims=True) + NORM_EPS)
-    meta, _, in_scale = lax.optimization_barrier((meta, far_cots[-1], in_scale))
+    in_scale = lax.optimization_barrier(in_scale)
+    xn = lax.optimization_barrier((x_wide * in_scale * g1).astype(BF16))
+    arrived, (w, wo, wb) = (gather_attn if layered else gather_plain)(
+        attn_pack, [in_scale], [far_cots[0], xn, meta, gate_bias]
+    )
+    wf = lax.all_gather(after(feed_pack, *arrived), "dp", axis=0, tiled=True)
+    meta = after(meta, far_cots[-1])
     core_cot = swap_core(after(cotangent, w))
     dys = [(cotangent, far, core_cot, swap_core(after(far, w))) for far in far_cots]
 
@@ -893,13 +891,13 @@
     terms = []
     earlier = before = []
     for piece in range(PIECES):
-        (part, state), saved = attend(piece, meta, x, w, wo, wb, g1, go, gate_bias, state, saved)
+        (part, state), saved = attend(piece, meta, xn, w, wo, wb, go, gate_bias, state, saved)
         own, part, core, far = sum_terms(part, earlier, before=before, halves=piece < PIECES - 1)
         terms.append((part, core, far))
         earlier = far[:1]
         before = far[-1:]
         state = after(state, *own)
-    xn, *kept = saved
+    kept = list(saved)
     z = kept.pop(5)
     terms = [(part, core, *far, *(swap_core(after(f, *own)) for f in far)) for part, core, far in terms]
 

time: 366 us -> 362 us (0.989)
  waiting for transfers between devices: 90.8 us -> 84.2 us
  other arithmetic: 32.7 us -> 36.7 us
    ppermute x3, waiting for transfers between devices: 27.3 us -> 22.4 us  [shift_layer(): lax.ppermute(array, 'dp', [(i, (i + 2 * by) % count) for i in range(count)])]
    convert_element_type x0 -> x1, other arithmetic: none -> 4.15 us  [body(): xn = lax.optimization_barrier((x_wide * in_scale * g1).astype(BF16))]
  transfers between devices with their start and end apart: 52 -> 52, of which waited for: 24 -> 23; matrix products, arithmetic and copies ran while one was open for 10% -> 11% of each run, Pallas kernels for 42% -> 42%
where the time goes in v2:
time: 362 us; the launch traced here: 361 us
  Pallas kernels  160 us (44%)
  waiting for transfers between devices  84.2 us (23%)
  starting transfers between devices  43.3 us (12%)
  other arithmetic  36.7 us (10%)
  local copies, waits for them, and re-layouts  19.2 us (5%)
  between operations  17.3 us (5%)
    pallas_call x8, Pallas kernels, run_kernel(): pl.pallas_call(functools.partial(body, len(given)), grid_spec=pltpu.Prefe...  113 us
    ppermute x47, waiting for transfers between devices, swap(): lax.ppermute(array, axis, [(i, i ^ bit) for i in range(lax.axis_size(axis...  61.7 us
    ppermute x47, starting transfers between devices, swap(): lax.ppermute(array, axis, [(i, i ^ bit) for i in range(lax.axis_size(axis...  36.8 us
    ppermute x3, waiting for transfers between devices, shift_layer(): lax.ppermute(array, 'dp', [(i, (i + 2 * by) % count) for i in range(count)])  22.4 us
    pallas_call x2, Pallas kernels, feed_grad(): pl.pallas_call(feed_grad_kernel, grid=(D // SLAB,), in_specs=[pl.BlockSpe...  19.1 us
    pallas_call x2, Pallas kernels, attn_grad(): pl.pallas_call(attn_grad_kernel, grid_spec=pltpu.PrefetchScalarGridSpec(n...  13.8 us
    unnamed x78, local copies, waits for them, and re-layouts  9.57 us
    convert_element_type x4, other arithmetic, sum_terms(): own.append((part[:, start:stop].astype(F32) + beside).astype(BF16))  9.08 us
  transfers between devices with their start and end apart: 52, of which 23 were waited for; matrix products, arithmetic and copies ran while one was open for 11% of the time, Pallas kernels for 42%

profile of v2, /device:TPU:0, one launch (start us, length us, event | category | flops | bytes accessed | tf_op | source)
XLA Modules:
  0.0 361.0 jit_solution(6926064770256395866)
XLA Ops:
  9.9 3.0 collective-permute-start.1
  18.8 3.1 fusion
  23.0 4.9 %collective-permute-done.2.refs_2_ = bf16[128,1152]{1,0:T(8,128)(2,1)S(1)} collective-permute-done((bf16[128,1152]{1,0:T(8,128)(2,1)}, bf16[128,1152]{1,0:T(8,128)(2,1)S(1)}, u32[]{:S(2)}, u32[]{:S(2)}) %collective-permute-start.2) | collective-permute-done | bytes 294944 | tf_op jit(solution)/shard_map/ppermute | solution.py:743
  32.1 4.2 %fusion.2.refs_0_.refs_3_ = bf16[2048,1024]{1,0:T(8,128)(2,1)} fusion(bf16[2048,1024]{1,0:T(8,128)(2,1)} %refs_2_.4, f32[1024]{0:T(1024)S(1)} %get-tuple-element.351, f32[2048]{0:T(1024)S(1)} %add_rsqrt_fusion), kind=kLoop, calls=%fused_computation.4 | loop fusion | flops 8388608 | bytes 8400896 | tf_op jit(solution)/shard_map/convert_element_type | solution.py:880
  39.5 16.5 %collective-permute-done.4.refs_4_ = bf16[128,1152]{1,0:T(8,128)(2,1)} collective-permute-done((bf16[128,1152]{1,0:T(8,128)(2,1)S(1)}, bf16[128,1152]{1,0:T(8,128)(2,1)}, u32[]{:S(2)}, u32[]{:S(2)}) %collective-permute-start.4) | collective-permute-done | bytes 294944 | tf_op jit(solution)/shard_map/ppermute | solution.py:743
  58.4 4.5 %collective-permute-done.8.refs_7_ = bf16[128,1152]{1,0:T(8,128)(2,1)S(1)} collective-permute-done((bf16[128,1152]{1,0:T(8,128)(2,1)}, bf16[128,1152]{1,0:T(8,128)(2,1)S(1)}, u32[]{:S(2)}, u32[]{:S(2)}) %collective-permute-start.8) | collective-permute-done | bytes 294944 | tf_op jit(solution)/shard_map/ppermute | solution.py:726
  63.6 3.1 assemble.1
  67.4 11.4 %attend.2 = (bf16[1024,1024]{1,0:T(8,128)(2,1)}, f32[256,128]{1,0:T(8,128)}, bf16[2048,512]{1,0:T(8,128)(2,1)}, f32[2048,256]{1,0:T(8,128)}, bf16[2048,128]{1,0:...) custom-call(s32[8]{0:T(128)} %concatenate.12.meta, ...), custom_call_target="tpu_custom_call" | custom-call | flops 8589934592 | bytes 1024 | tf_op jit(solution)/shard_map/attend/pallas_call | solution.py:513
  78.9 4.4 %collective-permute-done.9.refs_2_ = bf16[1024,1024]{1,0:T(8,128)(2,1)S(1)} collective-permute-done((bf16[1024,1024]{1,0:T(8,128)(2,1)}, bf16[1024,1024]{1,0:T(8,128)(2,1)S(1)}, u32[]{:S(2)}, u32[]{:S(2)}) %collective-permute-start.9) | collective-permute-done | bytes 2097184 | tf_op jit(solution)/shard_map/ppermute | solution.py:726
  87.9 11.2 %attend.3 = (bf16[1024,1024]{1,0:T(8,128)(2,1)}, f32[256,128]{1,0:T(8,128)}, bf16[2048,512]{1,0:T(8,128)(2,1)}, f32[2048,256]{1,0:T(8,128)}, bf16[2048,128]{1,0:...) custom-call(s32[8]{0:T(128)} %concatenate.12.meta, ...), custom_call_target="tpu_custom_call", output_to_operand_aliasing={{2}: (8, {}), {3}: (9, {}), {4}: (10, {}), {5}: (11, {}), {... | custom-call | flops 8589934592 | bytes 1024 | tf_op jit(solution)/shard_map/attend/pallas_call | solution.py:513
  105.4 3.3 add_convert_fusion.4
  108.7 6.6 %collective-permute-done.12.refs_4_ = bf16[1024,256]{1,0:T(8,128)(2,1)S(1)} collective-permute-done((bf16[1024,256]{1,0:T(8,128)(2,1)S(1)}, bf16[1024,256]{1,0:T(8,128)(2,1)S(1)}, u32[]{:S(2)}, u32[]{:S(2)}) %collective-permute-start.12) | collective-permute-done | bytes 524320 | tf_op jit(solution)/shard_map/ppermute | solution.py:726
  119.5 20.2 %feed.2 = (bf16[1024,1024]{1,0:T(8,128)(2,1)}, bf16[2048,512]{1,0:T(8,128)(2,1)}, bf16[2048,512]{1,0:T(8,128)(2,1)}, bf16[2048,1024]{1,0:T(8,128)(2,1)}, bf16[20...) custom-call(s32[8]{0:T(128)} %concatenate.12.meta, ...), custom_call_target="tpu_custom_call" | custom-call | flops 9663676416 | bytes 1024 | tf_op jit(solution)/shard_map/feed/pallas_call | solution.py:513
  141.8 3.9 %collective-permute-done.18.refs_1_ = bf16[1024,1024]{1,0:T(8,128)(2,1)S(1)} collective-permute-done((bf16[1024,1024]{1,0:T(8,128)(2,1)}, bf16[1024,1024]{1,0:T(8,128)(2,1)S(1)}, u32[]{:S(2)}, u32[]{:S(2)}) %collective-permute-start.18) | collective-permute-done | bytes 2097184 | tf_op jit(solution)/shard_map/ppermute | solution.py:726
  151.5 20.4 %feed.3 = (bf16[1024,1024]{1,0:T(8,128)(2,1)}, bf16[2048,512]{1,0:T(8,128)(2,1)}, bf16[2048,512]{1,0:T(8,128)(2,1)}, bf16[2048,1024]{1,0:T(8,128)(2,1)}, bf16[20...) custom-call(s32[8]{0:T(128)} %concatenate.12.meta, ...), custom_call_target="tpu_custom_call", output_to_operand_aliasing={{1}: (12, {}), {2}: (13, {}), {3}: (14, {}), {4}: (15, {}),... | custom-call | flops 9663676416 | bytes 1024 | tf_op jit(solution)/shard_map/feed/pallas_call | solution.py:513
  174.0 7.7 %feed_grad.2.refs_0_ = bf16[1024,2304]{1,0:T(8,128)(2,1)} custom-call(bf16[2048,1024]{1,0:T(8,128)(2,1)} %get-tuple-element.202.first_ref.refs_4_, bf16[2048,768]{1,0:T(8,128)(2,1)} %get-tuple-element.203.second_ref), custom_call_target="tpu_custom_call" | custom-call | flops 6442450944 | bytes 1024 | tf_op jit(solution)/shard_map/feed_grad/pallas_call | solution.py:642
  186.5 11.4 %feed_grad.3 = bf16[1024,2304]{1,0:T(8,128)(2,1)} custom-call(bf16[2048,1024]{1,0:T(8,128)(2,1)} %get-tuple-element.208.first_ref, bf16[2048,1536]{1,0:T(8,128)(2,1)} %get-tuple-element.209.second_ref, bf16[1024,2304]{1,0:T(8,128)(2,1)} %feed_grad.2.refs_0_), custom_call_target="tpu_custom_call", output_to_operand_aliasing={{}: (2, {})} | custom-call | flops 12884901888 | bytes 1024 | tf_op jit(solution)/shard_map/feed_grad/pallas_call | solution.py:642
  199.2 2.8 add_convert_fusion
  202.7 9.9 %turn.2 = (f32[32,1024]{1,0:T(8,128)}, bf16[2048,1024]{1,0:T(8,128)(2,1)}, f32[2048,256]{1,0:T(8,128)}, bf16[2048,256]{1,0:T(8,128)(2,1)}, bf16[2048,256]{1,0:T(8,128)(2,1)}) custom-call(s32[8]{0:T(128)} %concatenate.12.meta, bf16[1024,1024]{1,0:T(8,128)(2,1)} %get-tuple-element.184.refs_0_, bf16[1024,1024]{1,0:T(8,128)(2,1)} %copy-done.3, ...), custom_call_target="tpu_custom_call" | custom-call | flops 42949672 | bytes 1024 | tf_op jit(solution)/shard_map/turn/pallas_call | solution.py:513
  215.5 10.1 %turn.3 = (f32[32,1024]{1,0:T(8,128)}, bf16[2048,1024]{1,0:T(8,128)(2,1)}, f32[2048,256]{1,0:T(8,128)}, bf16[2048,256]{1,0:T(8,128)(2,1)}, bf16[2048,256]{1,0:T(8,128)(2,1)}) custom-call(s32[8]{0:T(128)} %concatenate.12.meta, ...), custom_call_target="tpu_custom_call", output_to_operand_aliasing={{1}: (14, {}), {2}: (15, {}), {3}: (16, {}), {4}: (17, {})} | custom-call | flops 42949672 | bytes 1024 | tf_op jit(solution)/shard_map/turn/pallas_call | solution.py:513
  225.6 7.2 %attn_grad.2 = (bf16[4,128,512]{2,1,0:T(8,128)(2,1)}, bf16[4,128,512]{2,1,0:T(8,128)(2,1)}) custom-call(s32[1]{0:T(128)} %bitcast.23.row_ref, bf16[2048,1024]{1,0:T(8,128)(2,1)} %fusion.2.refs_0_.refs_3_, bf16[2048,256]{1,0:T(8,128)(2,1)} %get-tuple-element.221.refs_1_, bf16[2048,1024]{1,0:T(8,128)(2,1)} %get-tuple-element.222.refs_2_, ...), custom_call_target="tpu_custom_call" | custom-call | flops 2147483648 | bytes 1024 | tf_op jit(solution)/shard_map/attn_grad/pallas_call | solution.py:668
  235.3 14.7 %back.2 = (bf16[1024,512]{1,0:T(8,128)(2,1)}, bf16[1024,512]{1,0:T(8,128)(2,1)}, f32[256,128]{1,0:T(8,128)}, bf16[256,128]{1,0:T(8,128)(2,1)}, f32[32,1024]{1,0:T(8,128)}, /*index=5*/bf16[2048,640]{1,0:T(8,128)(2,1)}) custom-call(s32[8]{0:T(128)} %concatenate.12.meta, bf16[2048,256]{1,0:T(8,128)(2,1)} %get-tuple-element.228.refs_0_, ...), custom_call_target="tpu_custom_call" | custom-call | flops 9019430912 | bytes 1024 | tf_op jit(solution)/shard_map/back/pallas_call | solution.py:513
  254.5 14.9 %back.3 = (bf16[1024,512]{1,0:T(8,128)(2,1)}, bf16[1024,512]{1,0:T(8,128)(2,1)}, f32[256,128]{1,0:T(8,128)}, bf16[256,128]{1,0:T(8,128)(2,1)}, f32[32,1024]{1,0:T(8,128)}, /*index=5*/bf16[2048,640]{1,0:T(8,128)(2,1)}) custom-call(s32[8]{0:T(128)} %concatenate.12.meta, ...), custom_call_target="tpu_custom_call", output_to_operand_aliasing={{5}: (14, {})} | custom-call | flops 9019430912 | bytes 1024 | tf_op jit(solution)/shard_map/back/pallas_call | solution.py:513
  270.3 6.6 %attn_grad.3 = (bf16[4,128,512]{2,1,0:T(8,128)(2,1)}, bf16[4,128,512]{2,1,0:T(8,128)(2,1)}) custom-call(s32[1]{0:T(128)} %bitcast.23.row_ref, bf16[2048,1024]{1,0:T(8,128)(2,1)} %fusion.2.refs_0_.refs_3_, bf16[2048,640]{1,0:T(8,128)(2,1)} %get-tuple-element.239.refs_1_), custom_call_target="tpu_custom_call" | custom-call | flops 2147483648 | bytes 1024 | tf_op jit(solution)/shard_map/attn_grad/pallas_call | solution.py:668
  280.0 2.8 collective-permute-start.31
  287.9 10.0 %collective-permute-done.31.refs_3_ = bf16[128,512]{1,0:T(8,128)(2,1)S(1)} collective-permute-done((bf16[128,512]{1,0:T(8,128)(2,1)S(1)}, bf16[128,512]{1,0:T(8,128)(2,1)S(1)}, u32[]{:S(2)}, u32[]{:S(2)}) %collective-permute-start.31) | collective-permute-done | bytes 131104 | tf_op jit(solution)/shard_map/ppermute | solution.py:726
  305.0 3.4 collective-permute-done.38
  310.1 3.4 collective-permute-done.48
  314.2 5.6 %collective-permute-done.49 = bf16[32,1024]{1,0:T(8,128)(2,1)S(1)} collective-permute-done((bf16[32,1024]{1,0:T(8,128)(2,1)S(1)}, bf16[32,1024]{1,0:T(8,128)(2,1)S(1)}, u32[]{:S(2)}, u32[]{:S(2)}) %collective-permute-start.49) | collective-permute-done | bytes 65568 | tf_op jit(solution)/shard_map/ppermute | solution.py:726
  334.5 3.6 collective-permute-done.43
  338.2 3.3 multiply_add_fusion
  346.5 6.5 %update.1 = (f32[2,128,128]{2,1,0:T(8,128)}, f32[2,128,256]{2,1,0:T(8,128)}, f32[256,128]{1,0:T(8,128)}, f32[2,704,128]{2,1,0:T(8,128)}, f32[704,128]{1,0:T(8,12...) custom-call(f32[1]{0:T(128)} %bitcast.38.clip_ref, ...), custom_call_target="tpu_custom_call" | custom-call | tf_op jit(solution)/shard_map/update/pallas_call | solution.py:707
  (228 shorter events, 99.3 us)
Async XLA Ops:
  7.2 112.3 %all-gather.2.cloned.1.call-start = ((), (), s32[]{:S(2)}) async-start(), calls=%async_computation.1 | async-start | bytes 5308416 | tf_op jit(solution)/shard_map/all_gather | solution.py:884
  9.9 13.1 %collective-permute-start.1 = (bf16[128,1152]{1,0:T(8,128)(2,1)}, bf16[128,1152]{1,0:T(8,128)(2,1)S(1)}, u32[]{:S(2)}, u32[]{:S(2)}) collective-permute-start(bf16[128,1152]{1,0:T(8,128)(2,1)} %get-tuple-element.154.refs_0_), channel_id=1, source_target_pairs={{0,8},{4,12},{8,16},{12,20},{16,24},{20,28},{24,0},{28,4},{1,9},{5... | collective-permute-start | bytes 884744 | tf_op jit(solution)/shard_map/ppermute | solution.py:743
  12.9 15.0 %collective-permute-start.2 = (bf16[128,1152]{1,0:T(8,128)(2,1)}, bf16[128,1152]{1,0:T(8,128)(2,1)S(1)}, u32[]{:S(2)}, u32[]{:S(2)}) collective-permute-start(bf16[128,1152]{1,0:T(8,128)(2,1)} %get-tuple-element.154.refs_0_), channel_id=1, source_target_pairs={{0,24},{4,28},{8,0},{12,4},{16,8},{20,12},{24,16},{28,20},{1,25},{... | collective-permute-start | bytes 884744 | tf_op jit(solution)/shard_map/ppermute | solution.py:743
  14.9 13.0 %collective-permute-start.3 = (bf16[128,1152]{1,0:T(8,128)(2,1)}, bf16[128,1152]{1,0:T(8,128)(2,1)S(1)}, u32[]{:S(2)}, u32[]{:S(2)}) collective-permute-start(bf16[128,1152]{1,0:T(8,128)(2,1)} %get-tuple-element.154.refs_0_), channel_id=1, source_target_pairs={{0,4},{4,0},{8,12},{12,8},{16,20},{20,16},{24,28},{28,24},{1,5},{5... | collective-permute-start | bytes 884744 | tf_op jit(solution)/shard_map/ppermute | solution.py:726
  16.7 22.7 %collective-permute-start.7 = (bf16[1024,256]{1,0:T(8,128)(2,1)S(1)}, bf16[1024,256]{1,0:T(8,128)(2,1)}, u32[]{:S(2)}, u32[]{:S(2)}) collective-permute-start(bf16[1024,256]{1,0:T(8,128)(2,1)S(1)} %get-tuple-element.342), channel_id=1, source_target_pairs={{0,2},{1,3},{2,0},{3,1},{4,6},{5,7},{6,4},{7,5},{8,10},{9,11},{10,... | collective-permute-start | bytes 1572872 | tf_op jit(solution)/shard_map/ppermute | solution.py:726
  18.3 40.1 %collective-permute-start = (bf16[1024,256]{1,0:T(8,128)(2,1)S(1)}, bf16[1024,256]{1,0:T(8,128)(2,1)}, u32[]{:S(2)}, u32[]{:S(2)}) collective-permute-start(bf16[1024,256]{1,0:T(8,128)(2,1)S(1)} %get-tuple-element.343), channel_id=1, source_target_pairs={{0,2},{1,3},{2,0},{3,1},{4,6},{5,7},{6,4},{7,5},{8,10},{9,11},{10,... | collective-permute-start | bytes 1572872 | tf_op jit(solution)/shard_map/ppermute | solution.py:726
  27.9 294.8 %reduce-scatter.2.cloned.1.call-start = ((), (), s32[]{:S(2)}) async-start(), calls=%async_computation.2 | async-start | bytes 5308416 | tf_op jit(solution)/shard_map/reduce_scatter | solution.py:922
  28.7 27.3 %collective-permute-start.4 = (bf16[128,1152]{1,0:T(8,128)(2,1)S(1)}, bf16[128,1152]{1,0:T(8,128)(2,1)}, u32[]{:S(2)}, u32[]{:S(2)}) collective-permute-start(bf16[128,1152]{1,0:T(8,128)(2,1)S(1)} %copy-done.16), channel_id=1, source_target_pairs={{0,16},{4,20},{8,24},{12,28},{16,0},{20,4},{24,8},{28,12},{1,17},{... | collective-permute-start | bytes 884744 | tf_op jit(solution)/shard_map/ppermute | solution.py:743
  30.0 25.9 %collective-permute-start.5 = (bf16[128,1152]{1,0:T(8,128)(2,1)S(1)}, bf16[128,1152]{1,0:T(8,128)(2,1)}, u32[]{:S(2)}, u32[]{:S(2)}) collective-permute-start(bf16[128,1152]{1,0:T(8,128)(2,1)S(1)} %collective-permute-done.1.refs_1_), channel_id=1, source_target_pairs={{0,4},{4,0},{8,12},{12,8},{16,20},{20,16},{24,28},{28,24},{1,5},{5... | collective-permute-start | bytes 884744 | tf_op jit(solution)/shard_map/ppermute | solution.py:726
  31.5 24.4 %collective-permute-start.6 = (bf16[128,1152]{1,0:T(8,128)(2,1)S(1)}, bf16[128,1152]{1,0:T(8,128)(2,1)}, u32[]{:S(2)}, u32[]{:S(2)}) collective-permute-start(bf16[128,1152]{1,0:T(8,128)(2,1)S(1)} %collective-permute-done.2.refs_2_), channel_id=1, source_target_pairs={{0,4},{4,0},{8,12},{12,8},{16,20},{20,16},{24,28},{28,24},{1,5},{5... | collective-permute-start | bytes 884744 | tf_op jit(solution)/shard_map/ppermute | solution.py:726
  86.1 14.0 %collective-permute-start.10 = (bf16[1024,256]{1,0:T(8,128)(2,1)S(1)}, bf16[1024,256]{1,0:T(8,128)(2,1)S(1)}, u32[]{:S(2)}, u32[]{:S(2)}) collective-permute-start(bf16[1024,256]{1,0:T(8,128)(2,1)S(1)} %get-tuple-element.341), channel_id=1, source_target_pairs={{0,2},{1,3},{2,0},{3,1},{4,6},{5,7},{6,4},{7,5},{8,10},{9,11},{10,... | collective-permute-start | bytes 1572872 | tf_op jit(solution)/shard_map/ppermute | solution.py:726
  101.0 14.3 %collective-permute-start.12 = (bf16[1024,256]{1,0:T(8,128)(2,1)S(1)}, bf16[1024,256]{1,0:T(8,128)(2,1)S(1)}, u32[]{:S(2)}, u32[]{:S(2)}) collective-permute-start(bf16[1024,256]{1,0:T(8,128)(2,1)S(1)} %get-tuple-element.175), channel_id=1, source_target_pairs={{0,2},{1,3},{2,0},{3,1},{4,6},{5,7},{6,4},{7,5},{8,10},{9,11},{10,... | collective-permute-start | bytes 1572872 | tf_op jit(solution)/shard_map/ppermute | solution.py:726
  102.7 14.9 %collective-permute-start.15 = (bf16[2048,256]{1,0:T(8,128)(2,1)S(1)}, bf16[2048,256]{1,0:T(8,128)(2,1)S(1)}, u32[]{:S(2)}, u32[]{:S(2)}) collective-permute-start(bf16[2048,256]{1,0:T(8,128)(2,1)S(1)} %copy-done.4), channel_id=1, source_target_pairs={{0,1},{1,0},{2,3},{3,2},{4,5},{5,4},{6,7},{7,6},{8,9},{9,8},{10,11... | collective-permute-start | bytes 3145736 | tf_op jit(solution)/shard_map/ppermute | solution.py:726
  102.9 14.6 %collective-permute-start.16 = (bf16[1024,256]{1,0:T(8,128)(2,1)}, bf16[1024,256]{1,0:T(8,128)(2,1)S(1)}, u32[]{:S(2)}, u32[]{:S(2)}) collective-permute-start(bf16[1024,256]{1,0:T(8,128)(2,1)} %collective-permute-done.7.refs_8_), channel_id=1, source_target_pairs={{0,1},{1,0},{2,3},{3,2},{4,5},{5,4},{6,7},{7,6},{8,9},{9,8},{10,11... | collective-permute-start | bytes 1572872 | tf_op jit(solution)/shard_map/ppermute | solution.py:726
  115.8 25.5 %collective-permute-start.17 = (bf16[1024,512]{1,0:T(8,128)(2,1)}, bf16[1024,512]{1,0:T(8,128)(2,1)}, u32[]{:S(2)}, u32[]{:S(2)}) collective-permute-start(bf16[1024,512]{1,0:T(8,128)(2,1)} %add_convert_fusion.4), channel_id=1, source_target_pairs={{0,2},{1,3},{2,0},{3,1},{4,6},{5,7},{6,4},{7,5},{8,10},{9,11},{10,... | collective-permute-start | bytes 3145736 | tf_op jit(solution)/shard_map/ppermute | solution.py:726
  141.3 9.1 %collective-permute-start.19 = (bf16[1024,512]{1,0:T(8,128)(2,1)}, bf16[1024,512]{1,0:T(8,128)(2,1)S(1)}, u32[]{:S(2)}, u32[]{:S(2)}) collective-permute-start(bf16[1024,512]{1,0:T(8,128)(2,1)} %collective-permute-done.17.refs_3_), channel_id=1, source_target_pairs={{0,1},{1,0},{2,3},{3,2},{4,5},{5,4},{6,7},{7,6},{8,9},{9,8},{10,11... | collective-permute-start | bytes 3145736 | tf_op jit(solution)/shard_map/ppermute | solution.py:726
  141.8 8.6 %collective-permute-start.20 = (bf16[1024,256]{1,0:T(8,128)(2,1)}, bf16[1024,256]{1,0:T(8,128)(2,1)S(1)}, u32[]{:S(2)}, u32[]{:S(2)}) collective-permute-start(bf16[1024,256]{1,0:T(8,128)(2,1)} %collective-permute-done.refs_6_), channel_id=1, source_target_pairs={{0,1},{1,0},{2,3},{3,2},{4,5},{5,4},{6,7},{7,6},{8,9},{9,8},{10,11... | collective-permute-start | bytes 1572872 | tf_op jit(solution)/shard_map/ppermute | solution.py:726
  148.6 25.4 %collective-permute-start.21 = (bf16[1024,512]{1,0:T(8,128)(2,1)S(1)}, bf16[1024,512]{1,0:T(8,128)(2,1)}, u32[]{:S(2)}, u32[]{:S(2)}) collective-permute-start(bf16[1024,512]{1,0:T(8,128)(2,1)S(1)} %add_convert_fusion.3), channel_id=1, source_target_pairs={{0,2},{1,3},{2,0},{3,1},{4,6},{5,7},{6,4},{7,5},{8,10},{9,11},{10,... | collective-permute-start | bytes 3145736 | tf_op jit(solution)/shard_map/ppermute | solution.py:726
  174.0 7.7 %collective-permute-start.22 = (bf16[1024,1024]{1,0:T(8,128)(2,1)}, bf16[1024,1024]{1,0:T(8,128)(2,1)}, u32[]{:S(2)}, u32[]{:S(2)}) collective-permute-start(bf16[1024,1024]{1,0:T(8,128)(2,1)} %get-tuple-element.201.refs_0_), channel_id=1, source_target_pairs={{0,1},{1,0},{2,3},{3,2},{4,5},{5,4},{6,7},{7,6},{8,9},{9,8},{10,11... | collective-permute-start | bytes 6291464 | tf_op jit(solution)/shard_map/ppermute | solution.py:726
  184.3 13.6 %collective-permute-start.23 = (bf16[2048,512]{1,0:T(8,128)(2,1)}, bf16[2048,512]{1,0:T(8,128)(2,1)S(1)}, u32[]{:S(2)}, u32[]{:S(2)}) collective-permute-start(bf16[2048,512]{1,0:T(8,128)(2,1)} %get-tuple-element.205), channel_id=1, source_target_pairs={{0,1},{1,0},{2,3},{3,2},{4,5},{5,4},{6,7},{7,6},{8,9},{9,8},{10,11... | collective-permute-start | bytes 6291464 | tf_op jit(solution)/shard_map/ppermute | solution.py:726
  184.8 17.2 %collective-permute-start.26 = (bf16[1024,512]{1,0:T(8,128)(2,1)}, bf16[1024,512]{1,0:T(8,128)(2,1)}, u32[]{:S(2)}, u32[]{:S(2)}) collective-permute-start(bf16[1024,512]{1,0:T(8,128)(2,1)} %collective-permute-done.21.refs_2_), channel_id=1, source_target_pairs={{0,1},{1,0},{2,3},{3,2},{4,5},{5,4},{6,7},{7,6},{8,9},{9,8},{10,11... | collective-permute-start | bytes 3145736 | tf_op jit(solution)/shard_map/ppermute | solution.py:726
  184.8 27.8 %collective-permute-start.24 = (bf16[1024,512]{1,0:T(8,128)(2,1)}, bf16[1024,512]{1,0:T(8,128)(2,1)S(1)}, u32[]{:S(2)}, u32[]{:S(2)}) collective-permute-start(bf16[1024,512]{1,0:T(8,128)(2,1)} %add_convert_fusion.2), channel_id=1, source_target_pairs={{0,2},{1,3},{2,0},{3,1},{4,6},{5,7},{6,4},{7,5},{8,10},{9,11},{10,... | collective-permute-start | bytes 3145736 | tf_op jit(solution)/shard_map/ppermute | solution.py:726
  214.0 56.3 %collective-permute-start.25 = (bf16[2048,256]{1,0:T(8,128)(2,1)}, bf16[2048,256]{1,0:T(8,128)(2,1)}, u32[]{:S(2)}, u32[]{:S(2)}) collective-permute-start(bf16[2048,256]{1,0:T(8,128)(2,1)} %slice.123), channel_id=1, source_target_pairs={{0,2},{1,3},{2,0},{3,1},{4,6},{5,7},{6,4},{7,5},{8,10},{9,11},{10,... | collective-permute-start | bytes 3145736 | tf_op jit(solution)/shard_map/ppermute | solution.py:726
  232.8 19.6 %collective-permute-start.28 = (bf16[4,128,512]{2,1,0:T(8,128)(2,1)}, bf16[4,128,512]{2,1,0:T(8,128)(2,1)S(1)}, u32[]{:S(2)}, u32[]{:S(2)}) collective-permute-start(bf16[4,128,512]{2,1,0:T(8,128)(2,1)} %get-tuple-element.225), channel_id=1, source_target_pairs={{0,4},{4,0},{8,12},{12,8},{16,20},{20,16},{24,28},{28,24},{1,5},{5... | collective-permute-start | bytes 1572872 | tf_op jit(solution)/shard_map/ppermute | solution.py:726
  254.5 15.0 %collective-permute-start.29 = (bf16[2,128,512]{2,1,0:T(8,128)(2,1)S(1)}, bf16[2,128,512]{2,1,0:T(8,128)(2,1)S(1)}, u32[]{:S(2)}, u32[]{:S(2)}) collective-permute-start(bf16[2,128,512]{2,1,0:T(8,128)(2,1)S(1)} %fusion.3), channel_id=1, source_target_pairs={{0,8},{4,12},{8,0},{12,4},{16,24},{20,28},{24,16},{28,20},{1,9},{5... | collective-permute-start | bytes 786440 | tf_op jit(solution)/shard_map/ppermute | solution.py:726
  276.9 21.0 %collective-permute-start.34 = (bf16[1024,512]{1,0:T(8,128)(2,1)}, bf16[1024,512]{1,0:T(8,128)(2,1)}, u32[]{:S(2)}, u32[]{:S(2)}) collective-permute-start(bf16[1024,512]{1,0:T(8,128)(2,1)} %get-tuple-element.251), channel_id=1, source_target_pairs={{0,1},{1,0},{2,3},{3,2},{4,5},{5,4},{6,7},{7,6},{8,9},{9,8},{10,11... | collective-permute-start | bytes 3145736 | tf_op jit(solution)/shard_map/ppermute | solution.py:726
  277.6 22.1 %collective-permute-start.30 = (bf16[4,128,512]{2,1,0:T(8,128)(2,1)}, bf16[4,128,512]{2,1,0:T(8,128)(2,1)S(1)}, u32[]{:S(2)}, u32[]{:S(2)}) collective-permute-start(bf16[4,128,512]{2,1,0:T(8,128)(2,1)} %get-tuple-element.241), channel_id=1, source_target_pairs={{0,4},{4,0},{8,12},{12,8},{16,20},{20,16},{24,28},{28,24},{1,5},{5... | collective-permute-start | bytes 1572872 | tf_op jit(solution)/shard_map/ppermute | solution.py:726
  280.0 17.9 %collective-permute-start.31 = (bf16[128,512]{1,0:T(8,128)(2,1)S(1)}, bf16[128,512]{1,0:T(8,128)(2,1)S(1)}, u32[]{:S(2)}, u32[]{:S(2)}) collective-permute-start(bf16[128,512]{1,0:T(8,128)(2,1)S(1)} %fusion.5), channel_id=1, source_target_pairs={{0,16},{4,20},{8,24},{12,28},{16,0},{20,4},{24,8},{28,12},{1,17},{... | collective-permute-start | bytes 393224 | tf_op jit(solution)/shard_map/ppermute | solution.py:726
  285.7 14.0 %collective-permute-start.33 = (bf16[1024,256]{1,0:T(8,128)(2,1)S(1)}, bf16[1024,256]{1,0:T(8,128)(2,1)S(1)}, u32[]{:S(2)}, u32[]{:S(2)}) collective-permute-start(bf16[1024,256]{1,0:T(8,128)(2,1)S(1)} %slice.150), channel_id=1, source_target_pairs={{0,2},{1,3},{2,0},{3,1},{4,6},{5,7},{6,4},{7,5},{8,10},{9,11},{10,... | collective-permute-start | bytes 1572872 | tf_op jit(solution)/shard_map/ppermute | solution.py:726
  300.0 8.4 %collective-permute-start.38 = (bf16[2,128,512]{2,1,0:T(8,128)(2,1)S(1)}, bf16[2,128,512]{2,1,0:T(8,128)(2,1)S(1)}, u32[]{:S(2)}, u32[]{:S(2)}) collective-permute-start(bf16[2,128,512]{2,1,0:T(8,128)(2,1)S(1)} %fusion.4), channel_id=1, source_target_pairs={{0,8},{4,12},{8,0},{12,4},{16,24},{20,28},{24,16},{28,20},{1,9},{5... | collective-permute-start | bytes 786440 | tf_op jit(solution)/shard_map/ppermute | solution.py:726
  300.5 20.0 %collective-permute-start.35 = (bf16[1024,256]{1,0:T(8,128)(2,1)S(1)}, bf16[1024,256]{1,0:T(8,128)(2,1)S(1)}, u32[]{:S(2)}, u32[]{:S(2)}) collective-permute-start(bf16[1024,256]{1,0:T(8,128)(2,1)S(1)} %slice.149), channel_id=1, source_target_pairs={{0,2},{1,3},{2,0},{3,1},{4,6},{5,7},{6,4},{7,5},{8,10},{9,11},{10,... | collective-permute-start | bytes 1572872 | tf_op jit(solution)/shard_map/ppermute | solution.py:726
  308.9 11.7 %collective-permute-start.39 = (bf16[128,512]{1,0:T(8,128)(2,1)S(1)}, bf16[128,512]{1,0:T(8,128)(2,1)S(1)}, u32[]{:S(2)}, u32[]{:S(2)}) collective-permute-start(bf16[128,512]{1,0:T(8,128)(2,1)S(1)} %fusion.6), channel_id=1, source_target_pairs={{0,16},{4,20},{8,24},{12,28},{16,0},{20,4},{24,8},{28,12},{1,17},{... | collective-permute-start | bytes 393224 | tf_op jit(solution)/shard_map/ppermute | solution.py:726
  (59 other events, 343.4 us)
Sparse Core Ops, SparseCore 0:
  28.1 84.2 all-gather.1
  198.0 104.3 reduce-scatter.1
